TPU v7x, 32 devices: a whole 2x2x4 slice. The times are simulated.
32 devices in a mesh: reg: 4 (over x, core), dam: 8 (over z, y).
Axes of the slice: x: 2, y: 2, z: 4, core: 2. Of those that a mesh axis runs over, the one named last changes fastest.
Arguments:
- history: bfloat16 [4096, 384], P(('reg', 'dam')), may hold values from -6 to 6
- routes: int32 [4096, 2], P(('reg', 'dam')), may hold values from 0 to 31, all different within a row; in each aligned block of 128 rows (0 to 127, 128 to 255, ...) at most 16 rows name the same one
- dam_field: bfloat16 [16384, 384], P(('reg', 'dam')), may hold values from -6 to 6
- conn_free: int32 [2048, 64], P(('reg', 'dam')), may hold values from 0 to 511
- conn_dam: int32 [2048, 64], P(('reg', 'dam')), may hold values from 0 to 511
- stiff_ref: bfloat16 [192, 192], replicated, may hold values from -0.4375 to 0.4375
- stiff_coef: float32 [2048], P(('reg', 'dam')), may hold values from 0.25 to 1
- mass_coef: float32 [2048], P(('reg', 'dam')), may hold values from 0.02 to 0.1
- reg_step: float32 [4096], P(('reg', 'dam')), may hold values from 0.05 to 0.2
- dam_step: float32 [16384], P(('reg', 'dam')), may hold values from 0.05 to 0.2
Outputs:
- history_out: bfloat16 [4096, 384], P(('reg', 'dam'))
- returned_force: float32 [4096, 384], P(('reg', 'dam'))
- dam_out: bfloat16 [16384, 384], P(('reg', 'dam'))
Inputs may be any that keep to these rules, and one draw needn't show every extreme that they name: `routes`: in the rows of one device no device number appears more than 16 times; some number appears exactly 16 times in some devices' rows.
All inputs are finite; a program needn't handle non-finite values.
Results may differ from a plain program's by a relative error of at most 0.0047.
Values may be sent and summed in bfloat16 or wider, within the bound.
No kernel may reach another device: no remote copies, remote signals or barrier semaphores. Data moves between devices by JAX's collectives and lax.ppermute only.
A program may use at most 64 MiB of HBM per device.

v0:
```python
import functools

import jax
import jax.numpy as jnp
from jax import lax
from jax.experimental import pallas as pl
from jax.experimental.pallas import tpu as pltpu
from jax.sharding import PartitionSpec as P

ROUNDS = 2
GROUP = 8
VMEM_BYTES = 20 * 1024 * 1024
BF16 = jnp.bfloat16
F32 = jnp.float32


def mask_to_bf16(mask):
    return jnp.where(mask, 1.0, 0.0).astype(BF16)


def dot(left, right):
    return jnp.dot(left, right, preferred_element_type=F32)


def dot_first(left, right):
    return lax.dot_general(left, right, (((0,), (0,)), ((), ())), preferred_element_type=F32)


def as_column(row):
    size = row.shape[1]
    down = lax.broadcasted_iota(jnp.int32, (size, size), 0)
    across = lax.broadcasted_iota(jnp.int32, (size, size), 1)
    return jnp.sum(jnp.where(down == across, row, jnp.zeros_like(row)), axis=1, keepdims=True)


def pack_kernel(capacity, routes_ref, history_ref, out_ref, place_ref):
    slots, rows = place_ref.shape
    row0, row1 = routes_ref[0:1, :], routes_ref[1:2, :]
    col0, col1 = as_column(row0), as_column(row1)
    down = lax.broadcasted_iota(jnp.int32, (rows, rows), 0)
    across = lax.broadcasted_iota(jnp.int32, (rows, rows), 1)
    numbers = lax.broadcasted_iota(jnp.int32, (slots, rows), 0)
    hits = []
    for own in (row0, row1):
        same = jnp.where(col0 == own, 1, 0) + jnp.where(col1 == own, 1, 0)
        slot = jnp.sum(jnp.where(down < across, same, 0), axis=0, keepdims=True)
        hits.append(own * capacity + slot == numbers)
    place = mask_to_bf16(hits[0] | hits[1])
    place_ref[...] = place
    out_ref[...] = dot(place, history_ref[...]).astype(BF16)


def turn_kernel(place_ref, returned_ref, history_ref, step_ref, next_ref, out_ref):
    place = place_ref[...]
    pulled = dot_first(place, returned_ref[...])
    following = (history_ref[...].astype(F32) - step_ref[:, 0:1] * pulled).astype(BF16)
    next_ref[...] = following
    out_ref[...] = dot(place, following).astype(BF16)


def last_kernel(place_ref, returned_ref, history_ref, step_ref, next_ref, pulled_ref):
    pulled = dot_first(place_ref[...], returned_ref[...])
    next_ref[...] = (history_ref[...].astype(F32) - step_ref[:, 0:1] * pulled).astype(BF16)
    pulled_ref[...] = pulled


def select_rows(conn_ref, select_ref):
    elements, nodes = conn_ref.shape
    columns = conn_ref[...].T
    lanes = lax.broadcasted_iota(jnp.int32, (nodes, select_ref.shape[1]), 1)
    for e in range(elements):
        select_ref[e * nodes : (e + 1) * nodes, :] = mask_to_bf16(columns[:, e : e + 1] == lanes)


def prepare_kernel(
    free_ref,
    dam_ref,
    stiff_ref,
    reg_ref,
    step_ref,
    free_select_ref,
    dam_select_ref,
    order_ref,
    reg_out_ref,
    step_out_ref,
):
    select_rows(free_ref, free_select_ref)
    select_rows(dam_ref, dam_select_ref)
    size = stiff_ref.shape[0]
    nodes = size // 3
    down = lax.broadcasted_iota(jnp.int32, (size, size), 0)
    across = lax.broadcasted_iota(jnp.int32, (size, size), 1)
    part = (down >= nodes).astype(jnp.int32) + (down >= 2 * nodes).astype(jnp.int32)
    order = mask_to_bf16(across == 3 * (down - part * nodes) + part)
    half = dot(order, stiff_ref[...]).astype(BF16)
    order_ref[...] = lax.dot_general(
        half, order, (((1,), (1,)), ((), ())), preferred_element_type=F32
    ).astype(BF16)
    reg_out_ref[...] = jnp.broadcast_to(as_column(reg_ref[...]), reg_out_ref.shape)
    step_out_ref[...] = jnp.broadcast_to(as_column(step_ref[...]), step_out_ref.shape)


def element_forces(u, stiff, stiff_coef_ref, mass_coef_ref, first, count):
    nodes = u.shape[0] // count
    samples = u.shape[1] // 3
    lane = lax.broadcasted_iota(jnp.int32, (nodes, samples), 1)

    def part(e, c):
        return u[e * nodes : (e + 1) * nodes, c * samples : (c + 1) * samples]

    blocks = []
    for pair in range(0, count, 2):
        sides = [jnp.concatenate([part(e, c) for c in range(3)], axis=0) for e in (pair, pair + 1)]
        product = dot(stiff, jnp.concatenate(sides, axis=1))
        for side, e in enumerate((pair, pair + 1)):
            k = stiff_coef_ref[first + e]
            m = mass_coef_ref[first + e]
            row = []
            for c in range(3):
                own = product[c * nodes : (c + 1) * nodes, side * samples : (side + 1) * samples]
                w = part(e, c).astype(F32)
                before = jnp.where(lane == 0, 0.0, pltpu.roll(w, 1, 1))
                after = jnp.where(lane == samples - 1, 0.0, pltpu.roll(w, samples - 1, 1))
                row.append((k * own + m * (after - 2.0 * w + before)).astype(BF16))
            blocks.append(jnp.concatenate(row, axis=1))
    return jnp.concatenate(blocks, axis=0)


def sweep(select_ref, table, stiff, coefs, force_ref, held, add):
    pairs = held[0].shape[0]
    groups = select_ref.shape[0] // pairs
    for turn in range(groups + 2):
        if turn >= 2:
            rows = slice((turn - 2) * pairs, (turn - 1) * pairs)
            add(rows, force_ref[rows, :])
        if 1 <= turn <= groups:
            rows = slice((turn - 1) * pairs, turn * pairs)
            u = held[(turn - 1) % 2][...]
            force_ref[rows, :] = element_forces(u, stiff, *coefs, (turn - 1) * GROUP, GROUP)
        if turn < groups:
            rows = slice(turn * pairs, (turn + 1) * pairs)
            held[turn % 2][...] = dot(select_ref[rows, :], table).astype(BF16)


def dam_part_kernel(
    free_select_ref,
    dam_select_ref,
    dam_ref,
    stiff_ref,
    stiff_coef_ref,
    mass_coef_ref,
    back_ref,
    sum_ref,
    force_ref,
    *held,
):
    back_ref[...] = jnp.zeros_like(back_ref)
    sum_ref[...] = jnp.zeros_like(sum_ref)

    def add(rows, force):
        back_ref[...] += dot_first(force, free_select_ref[rows, :])
        sum_ref[...] += dot_first(force, dam_select_ref[rows, :])

    coefs = (stiff_coef_ref, mass_coef_ref)
    sweep(dam_select_ref, dam_ref[...], stiff_ref[...], coefs, force_ref, held, add)


def free_part_kernel(
    select_ref,
    received_ref,
    stiff_ref,
    stiff_coef_ref,
    mass_coef_ref,
    start_ref,
    force_ref,
    back_ref,
    total_ref,
    *held,
):
    total_ref[...] = start_ref[...]

    def add(rows, force):
        total_ref[...] += dot_first(force, select_ref[rows, :])

    coefs = (stiff_coef_ref, mass_coef_ref)
    sweep(select_ref, received_ref[...], stiff_ref[...], coefs, force_ref, held, add)
    back_ref[...] = total_ref[...].T.astype(BF16)


def dam_update_kernel(select_ref, force_ref, start_ref, dam_ref, step_ref, next_ref):
    total = start_ref[...] + dot_first(force_ref[...], select_ref[...])
    next_ref[...] = (dam_ref[...].astype(F32) - step_ref[:, 0:1] * total.T).astype(BF16)


def exchange(rows, devices, capacity):
    width = rows.shape[1]
    shaped = rows.reshape(devices, capacity, width)
    arrived = lax.all_to_all(shaped, ("reg", "dam"), split_axis=0, concat_axis=0, tiled=True)
    return arrived.reshape(devices * capacity, width)


def kernel(body, name, n_in, out_shape, scalars=(), scratch=(), flops=0, moved=0):
    vmem = pl.BlockSpec(memory_space=pltpu.VMEM)
    smem = pl.BlockSpec(memory_space=pltpu.SMEM)
    return pl.pallas_call(
        body,
        name=name,
        in_specs=[smem if i in scalars else vmem for i in range(n_in)],
        out_specs=[vmem] * len(out_shape),
        out_shape=out_shape,
        scratch_shapes=list(scratch),
        compiler_params=pltpu.CompilerParams(vmem_limit_bytes=VMEM_BYTES),
        cost_estimate=pl.CostEstimate(flops=flops, bytes_accessed=moved, transcendentals=0),
    )


def shards(
    history,
    routes,
    dam_field,
    conn_free,
    conn_dam,
    stiff_ref,
    stiff_coef,
    mass_coef,
    reg_step,
    dam_step,
):
    devices = lax.axis_size(("reg", "dam"))
    row_count, width = history.shape
    capacity = 4 * row_count // devices
    slots = devices * capacity
    dam_count = dam_field.shape[0]
    elements, nodes = conn_free.shape
    all_pairs = elements * nodes
    pairs = GROUP * nodes
    lanes = 128

    shape = jax.ShapeDtypeStruct
    product = 2 * all_pairs * slots * width
    held = [pltpu.VMEM((pairs, width), BF16)] * 2

    pack = kernel(
        functools.partial(pack_kernel, capacity),
        "pack",
        2,
        [shape((slots, width), BF16), shape((slots, row_count), BF16)],
    )
    prepare = kernel(
        prepare_kernel,
        "prepare",
        5,
        [
            shape((all_pairs, slots), BF16),
            shape((all_pairs, dam_count), BF16),
            shape(stiff_ref.shape, BF16),
            shape((row_count, lanes), F32),
            shape((dam_count, lanes), F32),
        ],
        flops=product,
        moved=4 * all_pairs * slots,
    )
    dam_part = kernel(
        dam_part_kernel,
        "dam_part",
        6,
        [shape((width, slots), F32), shape((width, dam_count), F32)],
        scalars=(4, 5),
        scratch=[pltpu.VMEM((all_pairs, width), BF16)] + held,
        flops=4 * product,
        moved=4 * all_pairs * slots,
    )
    free_part = kernel(
        free_part_kernel,
        "free_part",
        6,
        [shape((all_pairs, width), BF16), shape((slots, width), BF16)],
        scalars=(3, 4),
        scratch=[pltpu.VMEM((width, slots), F32)] + held,
        flops=3 * product,
        moved=4 * all_pairs * slots,
    )
    dam_update = kernel(
        dam_update_kernel,
        "dam_update",
        5,
        [shape((dam_count, width), BF16)],
        flops=product,
        moved=4 * all_pairs * slots,
    )
    turn = kernel(
        turn_kernel, "turn", 4, [shape((row_count, width), BF16), shape((slots, width), BF16)]
    )
    last = kernel(
        last_kernel, "last", 4, [shape((row_count, width), BF16), shape((row_count, width), F32)]
    )

    outgoing, place = pack(routes.T, history)
    free_select, dam_select, stiff, reg_column, dam_column = prepare(
        conn_free,
        conn_dam,
        stiff_ref,
        reg_step.reshape(1, row_count),
        dam_step.reshape(1, dam_count),
    )
    for round_index in range(ROUNDS):
        received = exchange(outgoing, devices, capacity)
        back_start, sum_start = dam_part(
            free_select, dam_select, dam_field, stiff, stiff_coef, mass_coef
        )
        received, back_start = lax.optimization_barrier((received, back_start))
        force, back = free_part(free_select, received, stiff, stiff_coef, mass_coef, back_start)
        returned = exchange(back, devices, capacity)
        (dam_field,) = dam_update(dam_select, force, sum_start, dam_field, dam_column)
        returned, dam_field = lax.optimization_barrier((returned, dam_field))
        if round_index < ROUNDS - 1:
            history, outgoing = turn(place, returned, history, reg_column)
        else:
            history, pulled = last(place, returned, history, reg_column)
    return (history, pulled, dam_field)


def solution(mesh):
    rows = P(("reg", "dam"), None)
    flat = P(("reg", "dam"))
    in_specs = (rows, rows, rows, rows, rows, P(), flat, flat, flat, flat)
    return jax.shard_map(
        shards, mesh=mesh, in_specs=in_specs, out_specs=(rows, rows, rows), check_vma=False
    )
```

profile of v0, /device:TPU:0, one launch (start us, length us, event | category | flops | bytes accessed | tf_op | source)
XLA Modules:
  0.0 123.2 jit_solution(10348400211820455118)
XLA Ops:
  0.7 0.9 copy-done.20
  2.3 1.1 pack.1
  4.1 7.3 %all-to-all-start = ((bf16[32,16,384]{2,1,0:T(8,128)(2,1)}), bf16[32,16,384]{2,1,0:T(8,128)(2,1)S(1)}, u32[]{:S(2)}, u32[]{:S(2)}) async-start(bf16[32,16,384]{2,1,0:T(8,128)(2,1)} %bitcast.3), calls=%async_computation | async-start | bytes 786432 | tf_op jit(solution)/shard_map/all_to_all | solution.py:198
  11.4 0.9 copy-done.28
  15.1 1.9 %prepare.1 = (bf16[4096,512]{1,0:T(8,128)(2,1)S(1)}, bf16[4096,512]{1,0:T(8,128)(2,1)S(1)}, bf16[192,192]{1,0:T(8,128)(2,1)S(1)}, f32[128,128]{1,0:T(8,128)S(1)}, f32[512,128]{1,0:T(8,128)S(1)}) custom-call(s32[64,64]{1,0:T(8,128)S(1)} %copy-done.29, s32[64,64]{1,0:T(8,128)S(1)} %copy-done.30, bf16[192,192]{1,0:T(8,128)(2,1)S(1)} %copy-done.28, ...), custom_call_target="tpu_custom_call" | custom-call | flops 1610612736 | bytes 8388608 | tf_op jit(solution)/shard_map/prepare/pallas_call | solution.py:299
  18.4 7.8 %dam_part.2 = (f32[384,512]{1,0:T(8,128)S(1)}, f32[384,512]{1,0:T(8,128)S(1)}) custom-call(bf16[4096,512]{1,0:T(8,128)(2,1)S(1)} %get-tuple-element.31.free_select_ref.select_ref, bf16[4096,512]{1,0:T(8,128)(2,1)S(1)} %get-tuple-element.33.dam_select_ref.select_ref, bf16[512,384]{1,0:T(8,128)(2,1)S(1)} %copy-done.14, ...), custom_call_target="tpu_custom_call" | custom-call | flops 6442450944 | bytes 8388608 | tf_op jit(solution)/shard_map/dam_part/pallas_call | solution.py:308
  26.2 2.0 %copy-done = bf16[4096,512]{1,0:T(8,128)(2,1)} copy-done((bf16[4096,512]{1,0:T(8,128)(2,1)}, bf16[4096,512]{1,0:T(8,128)(2,1)S(1)}, u32[]{:S(2)}) %copy-start) | copy-done | bytes 4194328
  28.2 0.9 copy-done.9
  29.1 2.0 %copy-done.35 = bf16[4096,512]{1,0:T(8,128)(2,1)} copy-done((bf16[4096,512]{1,0:T(8,128)(2,1)}, bf16[4096,512]{1,0:T(8,128)(2,1)S(1)}, u32[]{:S(2)}) %copy-start.35) | copy-done | bytes 4194328
  31.1 0.9 copy-done.41
  32.6 2.2 %copy-done.36 = bf16[4096,512]{1,0:T(8,128)(2,1)S(1)} copy-done((bf16[4096,512]{1,0:T(8,128)(2,1)S(1)}, bf16[4096,512]{1,0:T(8,128)(2,1)}, u32[]{:S(2)}) %copy-start.36) | copy-done | bytes 4194328
  34.8 1.1 copy-done.42
  35.9 0.9 copy-done.44
  36.8 6.2 %free_part.2 = (bf16[4096,384]{1,0:T(8,128)(2,1)S(1)}, bf16[512,384]{1,0:T(8,128)(2,1)S(1)}) custom-call(bf16[4096,512]{1,0:T(8,128)(2,1)S(1)} %copy-done.36, bf16[512,384]{1,0:T(8,128)(2,1)S(1)} %bitcast.11, bf16[192,192]{1,0:T(8,128)(2,1)S(1)} %copy-done.44, f32[64]{0:T(128)S(1)} %copy-done.33, f32[64]{0:T(128)S(1)} %copy-done.34, f32[384,512]{1,0:T(8,128)S(1)} %copy-done.42), custom_call_target="tpu_custom_call" | custom-call | flops 4831838208 | bytes 8388608 | tf_op jit(solution)/shard_map/free_part/pallas_call | solution.py:312
  43.8 5.9 %all-to-all-start.1 = ((bf16[32,16,384]{2,1,0:T(8,128)(2,1)}), bf16[32,16,384]{2,1,0:T(8,128)(2,1)}, u32[]{:S(2)}, u32[]{:S(2)}) async-start(bf16[32,16,384]{2,1,0:T(8,128)(2,1)} %bitcast.14), calls=%async_computation.1 | async-start | bytes 786432 | tf_op jit(solution)/shard_map/all_to_all | solution.py:198
  49.8 2.2 %copy-done.1 = bf16[4096,512]{1,0:T(8,128)(2,1)S(1)} copy-done((bf16[4096,512]{1,0:T(8,128)(2,1)S(1)}, bf16[4096,512]{1,0:T(8,128)(2,1)}, u32[]{:S(2)}) %copy-start.1) | copy-done | bytes 4194328
  51.9 0.9 copy-done.5
  52.9 1.1 copy-done.10
  54.0 1.0 copy-done.15
  55.0 2.0 %dam_update.2.dam_ref = bf16[512,384]{1,0:T(8,128)(2,1)S(1)} custom-call(bf16[4096,512]{1,0:T(8,128)(2,1)S(1)} %copy-done.1, bf16[4096,384]{1,0:T(8,128)(2,1)S(1)} %get-tuple-element.39.force_ref, f32[384,512]{1,0:T(8,128)S(1)} %copy-done.10, bf16[512,384]{1,0:T(8,128)(2,1)S(1)} %copy-done.15, f32[512,128]{1,0:T(8,128)S(1)} %copy-done.5), custom_call_target="tpu_custom_call" | custom-call | flops 1610612736 | bytes 8388608 | tf_op jit(solution)/shard_map/dam_update/pallas_call | solution.py:314
  57.0 6.3 %all-to-all-done.1 = bf16[32,16,384]{2,1,0:T(8,128)(2,1)} async-done(((bf16[32,16,384]{2,1,0:T(8,128)(2,1)}), bf16[32,16,384]{2,1,0:T(8,128)(2,1)}, u32[]{:S(2)}, u32[]{:S(2)}) %all-to-all-start.1) | async-done | bytes 393248 | tf_op jit(solution)/shard_map/all_to_all | solution.py:198
  63.3 0.9 copy-done.12
  64.2 0.9 copy-done.21
  65.1 0.8 copy-done.23
  65.9 2.2 %turn.1 = (bf16[128,384]{1,0:T(8,128)(2,1)S(1)}, bf16[512,384]{1,0:T(8,128)(2,1)}) custom-call(bf16[512,128]{1,0:T(8,128)(2,1)S(1)} %copy-done.12, bf16[512,384]{1,0:T(8,128)(2,1)} %bitcast.6.returned_ref, bf16[128,384]{1,0:T(8,128)(2,1)S(1)} %copy-done.21, f32[128,128]{1,0:T(8,128)S(1)} %copy-done.23), custom_call_target="tpu_custom_call" | custom-call | tf_op jit(solution)/shard_map/turn/pallas_call | solution.py:317
  68.8 2.6 %all-to-all-start.2 = ((bf16[32,16,384]{2,1,0:T(8,128)(2,1)}), bf16[32,16,384]{2,1,0:T(8,128)(2,1)S(1)}, u32[]{:S(2)}, u32[]{:S(2)}) async-start(bf16[32,16,384]{2,1,0:T(8,128)(2,1)} %bitcast.7), calls=%async_computation.2 | async-start | bytes 786432 | tf_op jit(solution)/shard_map/all_to_all | solution.py:198
  71.4 2.2 %copy-done.2 = bf16[4096,512]{1,0:T(8,128)(2,1)S(1)} copy-done((bf16[4096,512]{1,0:T(8,128)(2,1)S(1)}, bf16[4096,512]{1,0:T(8,128)(2,1)}, u32[]{:S(2)}) %copy-start.2) | copy-done | bytes 4194328
  73.6 2.2 %copy-done.37 = bf16[4096,512]{1,0:T(8,128)(2,1)S(1)} copy-done((bf16[4096,512]{1,0:T(8,128)(2,1)S(1)}, bf16[4096,512]{1,0:T(8,128)(2,1)}, u32[]{:S(2)}) %copy-start.37) | copy-done | bytes 4194328
  75.8 0.9 copy-done.45
  76.7 7.8 %dam_part.3 = (f32[384,512]{1,0:T(8,128)S(1)}, f32[384,512]{1,0:T(8,128)S(1)}) custom-call(bf16[4096,512]{1,0:T(8,128)(2,1)S(1)} %copy-done.37, bf16[4096,512]{1,0:T(8,128)(2,1)S(1)} %copy-done.2, bf16[512,384]{1,0:T(8,128)(2,1)S(1)} %dam_update.2.dam_ref, bf16[192,192]{1,0:T(8,128)(2,1)S(1)} %copy-done.45, f32[64]{0:T(128)S(1)} %copy-done.33, f32[64]{0:T(128)S(1)} %copy-done.34), custom_call_target="tpu_custom_call" | custom-call | flops 6442450944 | bytes 8388608 | tf_op jit(solution)/shard_map/dam_part/pallas_call | solution.py:308
  84.5 0.9 copy-done.7
  85.3 0.9 copy-done.39
  87.0 1.0 copy-done.17
  88.0 2.2 %copy-done.38 = bf16[4096,512]{1,0:T(8,128)(2,1)S(1)} copy-done((bf16[4096,512]{1,0:T(8,128)(2,1)S(1)}, bf16[4096,512]{1,0:T(8,128)(2,1)}, u32[]{:S(2)}) %copy-start.38) | copy-done | bytes 4194328
  90.2 1.1 copy-done.40
  91.3 0.9 copy-done.46
  92.2 6.1 %free_part.3 = (bf16[4096,384]{1,0:T(8,128)(2,1)S(1)}, bf16[512,384]{1,0:T(8,128)(2,1)S(1)}) custom-call(bf16[4096,512]{1,0:T(8,128)(2,1)S(1)} %copy-done.38, bf16[512,384]{1,0:T(8,128)(2,1)S(1)} %bitcast.12, bf16[192,192]{1,0:T(8,128)(2,1)S(1)} %copy-done.46, f32[64]{0:T(128)S(1)} %copy-done.33, f32[64]{0:T(128)S(1)} %copy-done.34, f32[384,512]{1,0:T(8,128)S(1)} %copy-done.40), custom_call_target="tpu_custom_call" | custom-call | flops 4831838208 | bytes 8388608 | tf_op jit(solution)/shard_map/free_part/pallas_call | solution.py:312
  98.3 0.8 copy-done.18
  99.1 5.9 %all-to-all-start.3 = ((bf16[32,16,384]{2,1,0:T(8,128)(2,1)}), bf16[32,16,384]{2,1,0:T(8,128)(2,1)}, u32[]{:S(2)}, u32[]{:S(2)}) async-start(bf16[32,16,384]{2,1,0:T(8,128)(2,1)} %bitcast.13), calls=%async_computation.3 | async-start | bytes 786432 | tf_op jit(solution)/shard_map/all_to_all | solution.py:198
  105.1 2.2 %copy-done.3 = bf16[4096,512]{1,0:T(8,128)(2,1)S(1)} copy-done((bf16[4096,512]{1,0:T(8,128)(2,1)S(1)}, bf16[4096,512]{1,0:T(8,128)(2,1)}, u32[]{:S(2)}) %copy-start.3) | copy-done | bytes 4194328
  107.2 0.9 copy-done.6
  108.2 1.1 copy-done.8
  109.3 2.8 %dam_update.3 = bf16[512,384]{1,0:T(8,128)(2,1)} custom-call(bf16[4096,512]{1,0:T(8,128)(2,1)S(1)} %copy-done.3, bf16[4096,384]{1,0:T(8,128)(2,1)S(1)} %get-tuple-element.50.force_ref, f32[384,512]{1,0:T(8,128)S(1)} %copy-done.8, bf16[512,384]{1,0:T(8,128)(2,1)S(1)} %dam_update.2.dam_ref, f32[512,128]{1,0:T(8,128)S(1)} %copy-done.6), custom_call_target="tpu_custom_call" | custom-call | flops 1610612736 | bytes 8388608 | tf_op jit(solution)/shard_map/dam_update/pallas_call | solution.py:314
  112.1 6.5 %all-to-all-done.3 = bf16[32,16,384]{2,1,0:T(8,128)(2,1)} async-done(((bf16[32,16,384]{2,1,0:T(8,128)(2,1)}), bf16[32,16,384]{2,1,0:T(8,128)(2,1)}, u32[]{:S(2)}, u32[]{:S(2)}) %all-to-all-start.3) | async-done | bytes 393248 | tf_op jit(solution)/shard_map/all_to_all | solution.py:198
  118.6 0.9 copy-done.13
  119.5 0.8 copy-done.24
  120.3 0.9 copy-done.26
  121.2 2.0 %last.1 = (bf16[128,384]{1,0:T(8,128)(2,1)}, f32[128,384]{1,0:T(8,128)}) custom-call(bf16[512,128]{1,0:T(8,128)(2,1)S(1)} %copy-done.13, bf16[512,384]{1,0:T(8,128)(2,1)} %bitcast.10.returned_ref, bf16[128,384]{1,0:T(8,128)(2,1)S(1)} %copy-done.26, f32[128,128]{1,0:T(8,128)S(1)} %copy-done.24), custom_call_target="tpu_custom_call" | custom-call | tf_op jit(solution)/shard_map/last/pallas_call | solution.py:319
  (64 shorter events, 8.3 us)
Async XLA Ops:
  0.6 17.7 %copy-start.14 = (bf16[512,384]{1,0:T(8,128)(2,1)S(1)}, bf16[512,384]{1,0:T(8,128)(2,1)}, u32[]{:S(2)}) copy-start(bf16[512,384]{1,0:T(8,128)(2,1)} %dam_ref.5) | copy-start | bytes 1179652
  0.6 0.9 copy-start.20
  1.6 0.7 copy-start.27
  2.3 16.1 %copy-start.33 = (f32[64]{0:T(128)S(1)}, f32[64]{0:T(128)}, u32[]{:S(2)}) copy-start(f32[64]{0:T(128)} %stiff_coef_ref.7) | copy-start | bytes 772
  2.3 16.1 %copy-start.34 = (f32[64]{0:T(128)S(1)}, f32[64]{0:T(128)}, u32[]{:S(2)}) copy-start(f32[64]{0:T(128)} %mass_coef_ref.7) | copy-start | bytes 772
  3.4 0.7 copy-start.11
  4.1 28.5 %all-to-all-start = ((bf16[32,16,384]{2,1,0:T(8,128)(2,1)}), bf16[32,16,384]{2,1,0:T(8,128)(2,1)S(1)}, u32[]{:S(2)}, u32[]{:S(2)}) async-start(bf16[32,16,384]{2,1,0:T(8,128)(2,1)} %bitcast.3), calls=%async_computation | async-start | bytes 786432 | tf_op jit(solution)/shard_map/all_to_all | solution.py:198
  11.4 0.9 copy-start.28
  12.3 0.8 copy-start.29
  13.0 0.8 copy-start.30
  13.8 0.7 copy-start.31
  14.5 0.7 copy-start.32
  17.0 0.7 copy-start.4
  26.2 2.0 %copy-start = (bf16[4096,512]{1,0:T(8,128)(2,1)}, bf16[4096,512]{1,0:T(8,128)(2,1)S(1)}, u32[]{:S(2)}) copy-start(bf16[4096,512]{1,0:T(8,128)(2,1)S(1)} %get-tuple-element.33.dam_select_ref.select_ref) | copy-start | bytes 12582916
  28.2 0.9 copy-start.9
  29.1 2.0 %copy-start.35 = (bf16[4096,512]{1,0:T(8,128)(2,1)}, bf16[4096,512]{1,0:T(8,128)(2,1)S(1)}, u32[]{:S(2)}) copy-start(bf16[4096,512]{1,0:T(8,128)(2,1)S(1)} %get-tuple-element.31.free_select_ref.select_ref) | copy-start | bytes 12582916
  31.1 0.9 copy-start.41
  32.6 2.2 %copy-start.36 = (bf16[4096,512]{1,0:T(8,128)(2,1)S(1)}, bf16[4096,512]{1,0:T(8,128)(2,1)}, u32[]{:S(2)}) copy-start(bf16[4096,512]{1,0:T(8,128)(2,1)} %copy-done.35) | copy-start | bytes 12582916
  34.8 1.1 copy-start.42
  35.9 0.9 copy-start.44
  43.1 0.7 copy-start.19
  43.8 19.5 %all-to-all-start.1 = ((bf16[32,16,384]{2,1,0:T(8,128)(2,1)}), bf16[32,16,384]{2,1,0:T(8,128)(2,1)}, u32[]{:S(2)}, u32[]{:S(2)}) async-start(bf16[32,16,384]{2,1,0:T(8,128)(2,1)} %bitcast.14), calls=%async_computation.1 | async-start | bytes 786432 | tf_op jit(solution)/shard_map/all_to_all | solution.py:198
  49.8 2.2 %copy-start.1 = (bf16[4096,512]{1,0:T(8,128)(2,1)S(1)}, bf16[4096,512]{1,0:T(8,128)(2,1)}, u32[]{:S(2)}) copy-start(bf16[4096,512]{1,0:T(8,128)(2,1)} %copy-done) | copy-start | bytes 12582916
  51.9 0.9 copy-start.5
  52.9 1.1 copy-start.10
  54.0 1.0 copy-start.15
  63.3 0.9 copy-start.12
  64.2 0.9 copy-start.21
  65.1 0.8 copy-start.23
  68.8 17.4 %all-to-all-start.2 = ((bf16[32,16,384]{2,1,0:T(8,128)(2,1)}), bf16[32,16,384]{2,1,0:T(8,128)(2,1)S(1)}, u32[]{:S(2)}, u32[]{:S(2)}) async-start(bf16[32,16,384]{2,1,0:T(8,128)(2,1)} %bitcast.7), calls=%async_computation.2 | async-start | bytes 786432 | tf_op jit(solution)/shard_map/all_to_all | solution.py:198
  71.4 2.2 %copy-start.2 = (bf16[4096,512]{1,0:T(8,128)(2,1)S(1)}, bf16[4096,512]{1,0:T(8,128)(2,1)}, u32[]{:S(2)}) copy-start(bf16[4096,512]{1,0:T(8,128)(2,1)} %copy-done) | copy-start | bytes 12582916
  73.6 2.2 %copy-start.37 = (bf16[4096,512]{1,0:T(8,128)(2,1)S(1)}, bf16[4096,512]{1,0:T(8,128)(2,1)}, u32[]{:S(2)}) copy-start(bf16[4096,512]{1,0:T(8,128)(2,1)} %copy-done.35) | copy-start | bytes 12582916
  75.8 0.9 copy-start.45
  84.4 0.9 copy-start.7
  85.3 0.9 copy-start.39
  86.2 0.7 copy-start.16
  87.0 1.0 copy-start.17
  88.0 2.2 %copy-start.38 = (bf16[4096,512]{1,0:T(8,128)(2,1)S(1)}, bf16[4096,512]{1,0:T(8,128)(2,1)}, u32[]{:S(2)}) copy-start(bf16[4096,512]{1,0:T(8,128)(2,1)} %copy-done.35) | copy-start | bytes 12582916
  90.2 1.1 copy-start.40
  91.3 0.9 copy-start.46
  98.3 0.8 copy-start.18
  99.1 19.5 %all-to-all-start.3 = ((bf16[32,16,384]{2,1,0:T(8,128)(2,1)}), bf16[32,16,384]{2,1,0:T(8,128)(2,1)}, u32[]{:S(2)}, u32[]{:S(2)}) async-start(bf16[32,16,384]{2,1,0:T(8,128)(2,1)} %bitcast.13), calls=%async_computation.3 | async-start | bytes 786432 | tf_op jit(solution)/shard_map/all_to_all | solution.py:198
  105.1 2.2 %copy-start.3 = (bf16[4096,512]{1,0:T(8,128)(2,1)S(1)}, bf16[4096,512]{1,0:T(8,128)(2,1)}, u32[]{:S(2)}) copy-start(bf16[4096,512]{1,0:T(8,128)(2,1)} %copy-done) | copy-start | bytes 12582916
  107.2 0.9 copy-start.6
  108.2 1.1 copy-start.8
  118.6 0.9 copy-start.13
  119.5 0.8 copy-start.24
  120.3 0.9 copy-start.26
  (3 other events, 1.9 us)
where the time goes:
time: 125 us; the launch traced here: 123 us
  local copies, waits for them, and re-layouts  47.9 us (38%)
  Pallas kernels  39.9 us (32%)
  starting transfers between devices  21.8 us (17%)
  waiting for transfers between devices  12.8 us (10%)
    unnamed x94, local copies, waits for them, and re-layouts  47.9 us
    all_to_all x4, starting transfers between devices, exchange(): lax.all_to_all(shaped, ('reg', 'dam'), split_axis=0, concat_axis=0, tiled...  21.8 us
    pallas_call x2, Pallas kernels, shards(): dam_part(free_select, dam_select, dam_field, stiff, stiff_coef, mass_coef)  15.5 us
    all_to_all x4, waiting for transfers between devices, exchange(): lax.all_to_all(shaped, ('reg', 'dam'), split_axis=0, concat_axis=0, tiled...  12.8 us
    pallas_call x2, Pallas kernels, shards(): free_part(free_select, received, stiff, stiff_coef, mass_coef, back_start)  12.3 us
    pallas_call x2, Pallas kernels, shards(): dam_field, = dam_update(dam_select, force, sum_start, dam_field, dam_column)  4.76 us
  transfers between devices with their start and end apart: 4, of which 2 were waited for; matrix products, arithmetic and copies ran while one was open for 0% of the time, Pallas kernels for 18%

commit v1 on v0

v1 whole, which is shorter than its diff:
```python
import functools

import jax
import jax.numpy as jnp
from jax import lax
from jax.experimental import pallas as pl
from jax.experimental.pallas import tpu as pltpu
from jax.sharding import PartitionSpec as P

ROUNDS = 2
GROUP = 8
VMEM_BYTES = 28 * 1024 * 1024
BF16 = jnp.bfloat16
F32 = jnp.float32


def mask_to_bf16(mask):
    return jnp.where(mask, 1.0, 0.0).astype(BF16)


def dot(left, right):
    return jnp.dot(left, right, preferred_element_type=F32)


def dot_first(left, right):
    return lax.dot_general(left, right, (((0,), (0,)), ((), ())), preferred_element_type=F32)


def transfer(pairs, sems):
    copies = [pltpu.make_async_copy(a, b, sems.at[i]) for i, (a, b) in enumerate(pairs)]
    for copy in copies:
        copy.start()
    return copies


def finish(copies):
    for copy in copies:
        copy.wait()


def as_column(row):
    size = row.shape[1]
    down = lax.broadcasted_iota(jnp.int32, (size, size), 0)
    across = lax.broadcasted_iota(jnp.int32, (size, size), 1)
    return jnp.sum(jnp.where(down == across, row, jnp.zeros_like(row)), axis=1, keepdims=True)


def pack_kernel(
    capacity, routes_hbm, history_hbm, out_hbm, place_hbm, routes_ref, history_ref, out_ref, place_ref, sems
):
    inward = transfer([(routes_hbm, routes_ref), (history_hbm, history_ref)], sems)
    slots, rows = place_ref.shape
    finish(inward[:1])
    row0, row1 = routes_ref[0:1, :], routes_ref[1:2, :]
    col0, col1 = as_column(row0), as_column(row1)
    down = lax.broadcasted_iota(jnp.int32, (rows, rows), 0)
    across = lax.broadcasted_iota(jnp.int32, (rows, rows), 1)
    numbers = lax.broadcasted_iota(jnp.int32, (slots, rows), 0)
    hits = []
    for own in (row0, row1):
        same = jnp.where(col0 == own, 1, 0) + jnp.where(col1 == own, 1, 0)
        slot = jnp.sum(jnp.where(down < across, same, 0), axis=0, keepdims=True)
        hits.append(own * capacity + slot == numbers)
    place = mask_to_bf16(hits[0] | hits[1])
    place_ref[...] = place
    finish(inward[1:])
    out_ref[...] = dot(place, history_ref[...]).astype(BF16)
    finish(transfer([(out_ref, out_hbm), (place_ref, place_hbm)], sems))


def turn_kernel(
    place_hbm,
    returned_ref,
    history_hbm,
    step_hbm,
    after_hbm,
    next_hbm,
    out_hbm,
    place_ref,
    history_ref,
    step_ref,
    next_ref,
    out_ref,
    sems,
):
    inward = transfer(
        [(place_hbm, place_ref), (history_hbm, history_ref), (step_hbm, step_ref)], sems
    )
    finish(inward)
    place = place_ref[...]
    pulled = dot_first(place, returned_ref[...])
    step = as_column(step_ref[...])
    following = (history_ref[...].astype(F32) - step * pulled).astype(BF16)
    next_ref[...] = following
    out_ref[...] = dot(place, following).astype(BF16)
    finish(transfer([(next_ref, next_hbm), (out_ref, out_hbm)], sems))


def last_kernel(
    place_hbm,
    returned_ref,
    history_hbm,
    step_hbm,
    after_hbm,
    next_hbm,
    pulled_hbm,
    place_ref,
    history_ref,
    step_ref,
    next_ref,
    pulled_ref,
    sems,
):
    inward = transfer(
        [(place_hbm, place_ref), (history_hbm, history_ref), (step_hbm, step_ref)], sems
    )
    finish(inward)
    pulled = dot_first(place_ref[...], returned_ref[...])
    step = as_column(step_ref[...])
    next_ref[...] = (history_ref[...].astype(F32) - step * pulled).astype(BF16)
    pulled_ref[...] = pulled
    finish(transfer([(next_ref, next_hbm), (pulled_ref, pulled_hbm)], sems))


def by_component(stiff):
    size = stiff.shape[0]
    nodes = size // 3
    down = lax.broadcasted_iota(jnp.int32, (size, size), 0)
    across = lax.broadcasted_iota(jnp.int32, (size, size), 1)
    part = (down >= nodes).astype(jnp.int32) + (down >= 2 * nodes).astype(jnp.int32)
    order = mask_to_bf16(across == 3 * (down - part * nodes) + part)
    half = dot(order, stiff).astype(BF16)
    return lax.dot_general(
        half, order, (((1,), (1,)), ((), ())), preferred_element_type=F32
    ).astype(BF16)


def select_rows(columns, first, width):
    nodes = columns.shape[0]
    lanes = lax.broadcasted_iota(jnp.int32, (nodes, width), 1).astype(jnp.int16)
    parts = []
    for e in range(first, first + GROUP):
        own = jnp.broadcast_to(columns[:, e : e + 1], (nodes, width)).astype(jnp.int16)
        parts.append(jnp.where(own == lanes, jnp.ones((), BF16), jnp.zeros((), BF16)))
    return jnp.concatenate(parts, axis=0)


def element_forces(u, stiff, stiff_coef_ref, mass_coef_ref, first):
    nodes = u.shape[0] // GROUP
    samples = u.shape[1] // 3
    lane = lax.broadcasted_iota(jnp.int32, (nodes, samples), 1).astype(jnp.int16)
    nothing = jnp.zeros((), BF16)

    def part(e, c):
        return u[e * nodes : (e + 1) * nodes, c * samples : (c + 1) * samples]

    blocks = []
    for pair in range(0, GROUP, 2):
        sides = [jnp.concatenate([part(e, c) for c in range(3)], axis=0) for e in (pair, pair + 1)]
        product = dot(stiff, jnp.concatenate(sides, axis=1))
        for side, e in enumerate((pair, pair + 1)):
            k = stiff_coef_ref[first + e]
            m = mass_coef_ref[first + e]
            row = []
            for c in range(3):
                own = product[c * nodes : (c + 1) * nodes, side * samples : (side + 1) * samples]
                w = part(e, c)
                before = jnp.where(lane == 0, nothing, pltpu.roll(w, 1, 1))
                after = jnp.where(lane == samples - 1, nothing, pltpu.roll(w, samples - 1, 1))
                accel = ((before + after) - (w + w)).astype(F32)
                row.append((k * own + m * accel).astype(BF16))
            blocks.append(jnp.concatenate(row, axis=1))
    return jnp.concatenate(blocks, axis=0)


def sweep(select, table, stiff, coefs, force_ref, held, add):
    pairs = held[0].shape[0]
    groups = force_ref.shape[0] // pairs
    for turn in range(groups + 3):
        if turn >= 3:
            add(turn - 3, slice((turn - 3) * pairs, (turn - 2) * pairs))
        if 2 <= turn < groups + 2:
            rows = slice((turn - 2) * pairs, (turn - 1) * pairs)
            force_ref[rows, :] = element_forces(
                held[turn % 2][...], stiff, *coefs, (turn - 2) * GROUP
            )
        if 1 <= turn < groups + 1:
            rows = slice((turn - 1) * pairs, turn * pairs)
            held[(turn - 1) % 2][...] = dot(select.made[rows, :], table).astype(BF16)
        if turn < groups:
            select.make(turn)


class Selection:
    def __init__(self, made, columns):
        self.made = made
        self.columns = columns

    def make(self, group):
        pairs = GROUP * self.columns.shape[0]
        self.made[group * pairs : (group + 1) * pairs, :] = select_rows(
            self.columns, group * GROUP, self.made.shape[1]
        )


def dam_part_kernel(
    free_hbm,
    dam_conn_hbm,
    dam_hbm,
    stiff_hbm,
    stiff_coef_hbm,
    mass_coef_hbm,
    back_hbm,
    sum_hbm,
    order_hbm,
    free_ref,
    dam_conn_ref,
    dam_ref,
    stiff_ref,
    stiff_coef_ref,
    mass_coef_ref,
    back_ref,
    sum_ref,
    free_made,
    dam_made,
    force_ref,
    held0,
    held1,
    sems,
):
    inward = transfer(
        [
            (free_hbm, free_ref),
            (dam_conn_hbm, dam_conn_ref),
            (dam_hbm, dam_ref),
            (stiff_hbm, stiff_ref),
            (stiff_coef_hbm, stiff_coef_ref),
            (mass_coef_hbm, mass_coef_ref),
        ],
        sems,
    )
    back_ref[...] = jnp.zeros_like(back_ref)
    sum_ref[...] = jnp.zeros_like(sum_ref)
    finish(inward)
    stiff_ref[...] = by_component(stiff_ref[...])
    outward = transfer([(stiff_ref, order_hbm)], sems)
    free = Selection(free_made, free_ref[...].T)
    dam = Selection(dam_made, dam_conn_ref[...].T)

    def add(group, rows):
        force = force_ref[rows, :]
        free.make(group)
        sum_ref[...] += dot_first(force, dam_made[rows, :])
        back_ref[...] += dot_first(force, free_made[rows, :])

    coefs = (stiff_coef_ref, mass_coef_ref)
    sweep(dam, dam_ref[...], stiff_ref[...], coefs, force_ref, (held0, held1), add)
    finish(outward)
    finish(transfer([(back_ref, back_hbm), (sum_ref, sum_hbm)], sems))


def free_part_kernel(
    free_hbm,
    received_ref,
    stiff_hbm,
    stiff_coef_hbm,
    mass_coef_hbm,
    start_hbm,
    force_hbm,
    back_hbm,
    free_ref,
    stiff_ref,
    stiff_coef_ref,
    mass_coef_ref,
    start_ref,
    total_ref,
    made,
    force_ref,
    back_ref,
    held0,
    held1,
    sems,
    out_sems,
):
    inward = transfer(
        [
            (free_hbm, free_ref),
            (stiff_hbm, stiff_ref),
            (stiff_coef_hbm, stiff_coef_ref),
            (mass_coef_hbm, mass_coef_ref),
            (start_hbm, start_ref),
        ],
        sems,
    )
    finish(inward[:4])
    outward = []

    def add(group, rows):
        own = force_ref.at[rows, :]
        copy = pltpu.make_async_copy(own, force_hbm.at[rows, :], out_sems.at[group])
        copy.start()
        outward.append(copy)
        part = dot_first(own[...], made[rows, :])
        total_ref[...] = part if group == 0 else total_ref[...] + part

    coefs = (stiff_coef_ref, mass_coef_ref)
    select = Selection(made, free_ref[...].T)
    sweep(select, received_ref[...], stiff_ref[...], coefs, force_ref, (held0, held1), add)
    finish(inward[4:])
    back_ref[...] = (start_ref[...] + total_ref[...]).T.astype(BF16)
    finish(transfer([(back_ref, back_hbm)], sems))
    finish(outward)


def dam_update_kernel(
    dam_conn_hbm,
    force_hbm,
    start_hbm,
    dam_hbm,
    step_hbm,
    next_hbm,
    dam_conn_ref,
    force_ref,
    total_ref,
    dam_ref,
    step_ref,
    next_ref,
    made,
    sems,
    in_sems,
):
    inward = transfer(
        [
            (dam_conn_hbm, dam_conn_ref),
            (start_hbm, total_ref),
            (dam_hbm, dam_ref),
            (step_hbm, step_ref),
        ],
        sems,
    )
    nodes = dam_conn_ref.shape[1]
    pairs = GROUP * nodes
    groups = made.shape[0] // pairs
    chunks = [slice(g * pairs, (g + 1) * pairs) for g in range(groups)]
    forces = transfer([(force_hbm.at[rows, :], force_ref.at[rows, :]) for rows in chunks], in_sems)
    finish(inward)
    select = Selection(made, dam_conn_ref[...].T)
    for turn in range(groups + 1):
        if turn >= 1:
            rows = chunks[turn - 1]
            finish(forces[turn - 1 : turn])
            total_ref[...] += dot_first(force_ref[rows, :], made[rows, :])
        if turn < groups:
            select.make(turn)
    step = as_column(step_ref[...])
    next_ref[...] = (dam_ref[...].astype(F32) - step * total_ref[...].T).astype(BF16)
    finish(transfer([(next_ref, next_hbm)], sems))


def exchange(rows, devices, capacity):
    width = rows.shape[1]
    shaped = rows.reshape(devices, capacity, width)
    arrived = lax.all_to_all(shaped, ("reg", "dam"), split_axis=0, concat_axis=0, tiled=True)
    return arrived.reshape(devices * capacity, width)


def kernel(body, name, n_in, outs, scratch, inside=(), flops=0, moved=0):
    hbm = pl.BlockSpec(memory_space=pltpu.HBM)
    vmem = pl.BlockSpec(memory_space=pltpu.VMEM)
    call = pl.pallas_call(
        body,
        name=name,
        in_specs=[vmem if i in inside else hbm for i in range(n_in)],
        out_specs=[hbm] * len(outs),
        out_shape=[pltpu.HBM(*out) for out in outs],
        scratch_shapes=scratch,
        compiler_params=pltpu.CompilerParams(vmem_limit_bytes=VMEM_BYTES),
        cost_estimate=pl.CostEstimate(flops=flops, bytes_accessed=moved, transcendentals=0),
    )

    def run(*operands):
        return call(
            *[
                x if i in inside else pltpu.with_memory_space_constraint(x, pltpu.HBM)
                for i, x in enumerate(operands)
            ]
        )

    return run


def shards(
    history,
    routes,
    dam_field,
    conn_free,
    conn_dam,
    stiff_ref,
    stiff_coef,
    mass_coef,
    reg_step,
    dam_step,
):
    devices = lax.axis_size(("reg", "dam"))
    row_count, width = history.shape
    capacity = 4 * row_count // devices
    slots = devices * capacity
    dam_count = dam_field.shape[0]
    elements, nodes = conn_free.shape
    all_pairs = elements * nodes
    pairs = GROUP * nodes
    groups = elements // GROUP

    I32 = jnp.int32
    vmem = pltpu.VMEM
    dma = pltpu.SemaphoreType.DMA
    conn = vmem((elements, nodes), I32)
    stiff = vmem(stiff_ref.shape, BF16)
    coefs = [pltpu.SMEM((elements,), F32)] * 2
    held = [vmem((pairs, width), BF16)] * 2
    forces = vmem((all_pairs, width), BF16)
    free_made = vmem((all_pairs, slots), BF16)
    dam_made = vmem((all_pairs, dam_count), BF16)
    place_type = ((slots, row_count), BF16)
    slots_type = ((slots, width), BF16)
    rows_type = ((row_count, width), BF16)
    dam_type = ((dam_count, width), BF16)
    product = 2 * all_pairs * slots * width

    pack = kernel(
        functools.partial(pack_kernel, capacity),
        "pack",
        2,
        [slots_type, place_type],
        [vmem((2, row_count), I32), vmem(*rows_type), vmem(*slots_type), vmem(*place_type), dma((2,))],
    )
    turn_scratch = [vmem(*place_type), vmem(*rows_type), vmem((1, row_count), F32), vmem(*rows_type)]
    turn = kernel(
        turn_kernel,
        "turn",
        5,
        [rows_type, slots_type],
        turn_scratch + [vmem(*slots_type), dma((3,))],
        inside=(1,),
    )
    last = kernel(
        last_kernel,
        "last",
        5,
        [rows_type, ((row_count, width), F32)],
        turn_scratch + [vmem((row_count, width), F32), dma((3,))],
        inside=(1,),
    )
    dam_part = kernel(
        dam_part_kernel,
        "dam_part",
        6,
        [((width, slots), F32), ((width, dam_count), F32), (stiff_ref.shape, BF16)],
        [conn, conn, vmem(*dam_type), stiff, *coefs]
        + [vmem((width, slots), F32), vmem((width, dam_count), F32)]
        + [free_made, dam_made, forces, *held, dma((6,))],
        flops=4 * product,
        moved=4 * all_pairs * width,
    )
    free_part = kernel(
        free_part_kernel,
        "free_part",
        6,
        [((all_pairs, width), BF16), slots_type],
        [conn, stiff, *coefs, vmem((width, slots), F32), vmem((width, slots), F32)]
        + [free_made, forces, vmem(*slots_type), *held, dma((5,)), dma((groups,))],
        inside=(1,),
        flops=3 * product,
        moved=4 * all_pairs * width,
    )
    dam_update = kernel(
        dam_update_kernel,
        "dam_update",
        5,
        [dam_type],
        [conn, forces, vmem((width, dam_count), F32), vmem(*dam_type), vmem((1, dam_count), F32)]
        + [vmem(*dam_type), dam_made, dma((4,)), dma((groups,))],
        flops=product,
        moved=4 * all_pairs * width,
    )

    reg_row = reg_step.reshape(1, row_count)
    dam_row = dam_step.reshape(1, dam_count)
    outgoing, place = pack(routes.T, history)
    for round_index in range(ROUNDS):
        received = exchange(outgoing, devices, capacity)
        back_start, sum_start, ordered = dam_part(
            conn_free, conn_dam, dam_field, stiff_ref, stiff_coef, mass_coef
        )
        force, back = free_part(conn_free, received, ordered, stiff_coef, mass_coef, back_start)
        returned = exchange(back, devices, capacity)
        (dam_field,) = dam_update(conn_dam, force, sum_start, dam_field, dam_row)
        if round_index < ROUNDS - 1:
            history, outgoing = turn(place, returned, history, reg_row, dam_field)
        else:
            history, pulled = last(place, returned, history, reg_row, dam_field)
    return (history, pulled, dam_field)


def solution(mesh):
    rows = P(("reg", "dam"), None)
    flat = P(("reg", "dam"))
    in_specs = (rows, rows, rows, rows, rows, P(), flat, flat, flat, flat)
    return jax.shard_map(
        shards, mesh=mesh, in_specs=in_specs, out_specs=(rows, rows, rows), check_vma=False
    )
```

time: 125 us -> 92.6 us (0.74); the launches traced: 123 us -> 92.1 us
  local copies, waits for them, and re-layouts: 47.9 us -> 0 us
  Pallas kernels: 39.9 us -> 53.1 us
  waiting for transfers between devices: 12.8 us -> 22.9 us
  starting transfers between devices: 21.8 us -> 15.2 us
    unnamed x94 -> x0, local copies, waits for them, and re-layouts: 47.9 us -> none
    pallas_call x10 -> x9, Pallas kernels: 39.9 us -> 53.1 us  [run(): call(*[x if i in inside else pltpu.with_memory_space_constraint(x, pltpu....]
    all_to_all x4, waiting for transfers between devices: 12.8 us -> 22.9 us  [exchange(): lax.all_to_all(shaped, ('reg', 'dam'), split_axis=0, concat_axis=0, tiled...]
    all_to_all x4, starting transfers between devices: 21.8 us -> 15.2 us  [exchange(): lax.all_to_all(shaped, ('reg', 'dam'), split_axis=0, concat_axis=0, tiled...]
  transfers between devices with their start and end apart: 4 -> 4, of which waited for: 2 -> 4; matrix products, arithmetic and copies ran while one was open for 0% -> 0% of each run, Pallas kernels for 18% -> 34%
where the time goes in v1:
time: 92.6 us; the launch traced here: 92.1 us
  Pallas kernels  53.1 us (57%)
  waiting for transfers between devices  22.9 us (25%)
  starting transfers between devices  15.2 us (16%)
    pallas_call x9, Pallas kernels, run(): call(*[x if i in inside else pltpu.with_memory_space_constraint(x, pltpu....  53.1 us
    all_to_all x4, waiting for transfers between devices, exchange(): lax.all_to_all(shaped, ('reg', 'dam'), split_axis=0, concat_axis=0, tiled...  22.9 us
    all_to_all x4, starting transfers between devices, exchange(): lax.all_to_all(shaped, ('reg', 'dam'), split_axis=0, concat_axis=0, tiled...  15.2 us
  transfers between devices with their start and end apart: 4, of which 4 were waited for; matrix products, arithmetic and copies ran while one was open for 0% of the time, Pallas kernels for 34%

profile of v1, /device:TPU:0, one launch (start us, length us, event | category | flops | bytes accessed | tf_op | source)
XLA Modules:
  0.0 92.1 jit_solution(7012842439467477160)
XLA Ops:
  0.6 2.0 %pack.1 = (bf16[512,384]{1,0:T(8,128)(2,1)}, bf16[512,128]{1,0:T(8,128)(2,1)}) custom-call(s32[2,128]{1,0:T(2,128)} %bitcast.21, bf16[128,384]{1,0:T(8,128)(2,1)} %history_hbm.3), custom_call_target="tpu_custom_call" | custom-call | tf_op jit(solution)/shard_map/pack/pallas_call | solution.py:382
  2.6 7.3 %all-to-all-start = ((bf16[32,16,384]{2,1,0:T(8,128)(2,1)}), bf16[32,16,384]{2,1,0:T(8,128)(2,1)S(1)}, u32[]{:S(2)}, u32[]{:S(2)}) async-start(bf16[32,16,384]{2,1,0:T(8,128)(2,1)} %bitcast.18), calls=%async_computation | async-start | bytes 786432 | tf_op jit(solution)/shard_map/all_to_all | solution.py:363
  9.9 9.8 %dam_part.2 = (f32[384,512]{1,0:T(8,128)}, f32[384,512]{1,0:T(8,128)}, bf16[192,192]{1,0:T(8,128)(2,1)}) custom-call(s32[64,64]{1,0:T(8,128)} %free_hbm.7, s32[64,64]{1,0:T(8,128)} %dam_conn_hbm.7, bf16[512,384]{1,0:T(8,128)(2,1)} %dam_hbm.3, bf16[192,192]{1,0:T(8,128)(2,1)} %stiff_hbm.3, f32[64]{0:T(128)} %stiff_coef_hbm.7, f32[64]{0:T(128)} %mass_coef_hbm.7), custom_call_target="tpu_custom_call" | custom-call | flops 6442450944 | bytes 6291456 | tf_op jit(solution)/shard_map/dam_part/pallas_call | solution.py:382
  19.7 3.8 %all-to-all-done = bf16[32,16,384]{2,1,0:T(8,128)(2,1)S(1)} async-done(((bf16[32,16,384]{2,1,0:T(8,128)(2,1)}), bf16[32,16,384]{2,1,0:T(8,128)(2,1)S(1)}, u32[]{:S(2)}, u32[]{:S(2)}) %all-to-all-start) | async-done | bytes 393248 | tf_op jit(solution)/shard_map/all_to_all | solution.py:363
  23.5 7.8 %free_part.2 = (bf16[4096,384]{1,0:T(8,128)(2,1)}, bf16[512,384]{1,0:T(8,128)(2,1)}) custom-call(s32[64,64]{1,0:T(8,128)} %free_hbm.7, bf16[512,384]{1,0:T(8,128)(2,1)S(1)} %bitcast.13, bf16[192,192]{1,0:T(8,128)(2,1)} %get-tuple-element.21.stiff_hbm, f32[64]{0:T(128)} %stiff_coef_hbm.7, f32[64]{0:T(128)} %mass_coef_hbm.7, ...), custom_call_target="tpu_custom_call" | custom-call | flops 4831838208 | bytes 6291456 | tf_op jit(solution)/shard_map/free_part/pallas_call | solution.py:382
  31.3 2.6 %all-to-all-start.1 = ((bf16[32,16,384]{2,1,0:T(8,128)(2,1)}), bf16[32,16,384]{2,1,0:T(8,128)(2,1)S(1)}, u32[]{:S(2)}, u32[]{:S(2)}) async-start(bf16[32,16,384]{2,1,0:T(8,128)(2,1)} %bitcast.16), calls=%async_computation.1 | async-start | bytes 786432 | tf_op jit(solution)/shard_map/all_to_all | solution.py:363
  33.9 5.8 %dam_update.2.after_hbm.dam_hbm = bf16[512,384]{1,0:T(8,128)(2,1)} custom-call(s32[64,64]{1,0:T(8,128)} %dam_conn_hbm.7, bf16[4096,384]{1,0:T(8,128)(2,1)} %get-tuple-element.24.force_hbm, f32[384,512]{1,0:T(8,128)} %get-tuple-element.25.start_hbm, bf16[512,384]{1,0:T(8,128)(2,1)} %dam_hbm.3, f32[1,512]{1,0:T(1,128)} %bitcast.22), custom_call_target="tpu_custom_call" | custom-call | flops 1610612736 | bytes 6291456 | tf_op jit(solution)/shard_map/dam_update/pallas_call | solution.py:382
  39.8 7.7 %all-to-all-done.1 = bf16[32,16,384]{2,1,0:T(8,128)(2,1)S(1)} async-done(((bf16[32,16,384]{2,1,0:T(8,128)(2,1)}), bf16[32,16,384]{2,1,0:T(8,128)(2,1)S(1)}, u32[]{:S(2)}, u32[]{:S(2)}) %all-to-all-start.1) | async-done | bytes 393248 | tf_op jit(solution)/shard_map/all_to_all | solution.py:363
  47.5 2.2 %turn.1 = (bf16[128,384]{1,0:T(8,128)(2,1)}, bf16[512,384]{1,0:T(8,128)(2,1)}) custom-call(bf16[512,128]{1,0:T(8,128)(2,1)} %get-tuple-element.19.place_hbm, bf16[512,384]{1,0:T(8,128)(2,1)S(1)} %bitcast.12, bf16[128,384]{1,0:T(8,128)(2,1)} %history_hbm.3, f32[1,128]{1,0:T(1,128)} %bitcast.19, bf16[512,384]{1,0:T(8,128)(2,1)} %dam_update.2.after_hbm.dam_hbm), custom_call_target="tpu_custom_call" | custom-call | tf_op jit(solution)/shard_map/turn/pallas_call | solution.py:382
  49.7 2.6 %all-to-all-start.2 = ((bf16[32,16,384]{2,1,0:T(8,128)(2,1)}), bf16[32,16,384]{2,1,0:T(8,128)(2,1)S(1)}, u32[]{:S(2)}, u32[]{:S(2)}) async-start(bf16[32,16,384]{2,1,0:T(8,128)(2,1)} %bitcast.17), calls=%async_computation.2 | async-start | bytes 786432 | tf_op jit(solution)/shard_map/all_to_all | solution.py:363
  52.3 9.8 %dam_part.3 = (f32[384,512]{1,0:T(8,128)}, f32[384,512]{1,0:T(8,128)}, bf16[192,192]{1,0:T(8,128)(2,1)}) custom-call(s32[64,64]{1,0:T(8,128)} %free_hbm.7, s32[64,64]{1,0:T(8,128)} %dam_conn_hbm.7, bf16[512,384]{1,0:T(8,128)(2,1)} %dam_update.2.after_hbm.dam_hbm, bf16[192,192]{1,0:T(8,128)(2,1)} %stiff_hbm.3, f32[64]{0:T(128)} %stiff_coef_hbm.7, f32[64]{0:T(128)} %mass_coef_hbm.7), custom_call_target="tpu_custom_call" | custom-call | flops 6442450944 | bytes 6291456 | tf_op jit(solution)/shard_map/dam_part/pallas_call | solution.py:382
  62.1 3.8 %all-to-all-done.2 = bf16[32,16,384]{2,1,0:T(8,128)(2,1)S(1)} async-done(((bf16[32,16,384]{2,1,0:T(8,128)(2,1)}), bf16[32,16,384]{2,1,0:T(8,128)(2,1)S(1)}, u32[]{:S(2)}, u32[]{:S(2)}) %all-to-all-start.2) | async-done | bytes 393248 | tf_op jit(solution)/shard_map/all_to_all | solution.py:363
  65.9 7.9 %free_part.3 = (bf16[4096,384]{1,0:T(8,128)(2,1)}, bf16[512,384]{1,0:T(8,128)(2,1)}) custom-call(s32[64,64]{1,0:T(8,128)} %free_hbm.7, bf16[512,384]{1,0:T(8,128)(2,1)S(1)} %bitcast.14, bf16[192,192]{1,0:T(8,128)(2,1)} %get-tuple-element.27.stiff_hbm, f32[64]{0:T(128)} %stiff_coef_hbm.7, f32[64]{0:T(128)} %mass_coef_hbm.7, ...), custom_call_target="tpu_custom_call" | custom-call | flops 4831838208 | bytes 6291456 | tf_op jit(solution)/shard_map/free_part/pallas_call | solution.py:382
  73.8 2.6 %all-to-all-start.3 = ((bf16[32,16,384]{2,1,0:T(8,128)(2,1)}), bf16[32,16,384]{2,1,0:T(8,128)(2,1)S(1)}, u32[]{:S(2)}, u32[]{:S(2)}) async-start(bf16[32,16,384]{2,1,0:T(8,128)(2,1)} %bitcast.15), calls=%async_computation.3 | async-start | bytes 786432 | tf_op jit(solution)/shard_map/all_to_all | solution.py:363
  76.4 5.9 %dam_update.3.after_hbm = bf16[512,384]{1,0:T(8,128)(2,1)} custom-call(s32[64,64]{1,0:T(8,128)} %dam_conn_hbm.7, bf16[4096,384]{1,0:T(8,128)(2,1)} %get-tuple-element.31.force_hbm, f32[384,512]{1,0:T(8,128)} %get-tuple-element.32.start_hbm, bf16[512,384]{1,0:T(8,128)(2,1)} %dam_update.2.after_hbm.dam_hbm, f32[1,512]{1,0:T(1,128)} %bitcast.23), custom_call_target="tpu_custom_call" | custom-call | flops 1610612736 | bytes 6291456 | tf_op jit(solution)/shard_map/dam_update/pallas_call | solution.py:382
  82.3 7.7 %all-to-all-done.3 = bf16[32,16,384]{2,1,0:T(8,128)(2,1)S(1)} async-done(((bf16[32,16,384]{2,1,0:T(8,128)(2,1)}), bf16[32,16,384]{2,1,0:T(8,128)(2,1)S(1)}, u32[]{:S(2)}, u32[]{:S(2)}) %all-to-all-start.3) | async-done | bytes 393248 | tf_op jit(solution)/shard_map/all_to_all | solution.py:363
  90.0 1.9 %last.1 = (bf16[128,384]{1,0:T(8,128)(2,1)}, f32[128,384]{1,0:T(8,128)}) custom-call(bf16[512,128]{1,0:T(8,128)(2,1)} %get-tuple-element.19.place_hbm, bf16[512,384]{1,0:T(8,128)(2,1)S(1)} %bitcast.11, bf16[128,384]{1,0:T(8,128)(2,1)} %get-tuple-element.30.history_hbm, f32[1,128]{1,0:T(1,128)} %bitcast.20, bf16[512,384]{1,0:T(8,128)(2,1)} %dam_update.3.after_hbm), custom_call_target="tpu_custom_call" | custom-call | tf_op jit(solution)/shard_map/last/pallas_call | solution.py:382
Async XLA Ops:
  2.6 20.9 %all-to-all-start = ((bf16[32,16,384]{2,1,0:T(8,128)(2,1)}), bf16[32,16,384]{2,1,0:T(8,128)(2,1)S(1)}, u32[]{:S(2)}, u32[]{:S(2)}) async-start(bf16[32,16,384]{2,1,0:T(8,128)(2,1)} %bitcast.18), calls=%async_computation | async-start | bytes 786432 | tf_op jit(solution)/shard_map/all_to_all | solution.py:363
  31.3 16.2 %all-to-all-start.1 = ((bf16[32,16,384]{2,1,0:T(8,128)(2,1)}), bf16[32,16,384]{2,1,0:T(8,128)(2,1)S(1)}, u32[]{:S(2)}, u32[]{:S(2)}) async-start(bf16[32,16,384]{2,1,0:T(8,128)(2,1)} %bitcast.16), calls=%async_computation.1 | async-start | bytes 786432 | tf_op jit(solution)/shard_map/all_to_all | solution.py:363
  49.7 16.2 %all-to-all-start.2 = ((bf16[32,16,384]{2,1,0:T(8,128)(2,1)}), bf16[32,16,384]{2,1,0:T(8,128)(2,1)S(1)}, u32[]{:S(2)}, u32[]{:S(2)}) async-start(bf16[32,16,384]{2,1,0:T(8,128)(2,1)} %bitcast.17), calls=%async_computation.2 | async-start | bytes 786432 | tf_op jit(solution)/shard_map/all_to_all | solution.py:363
  73.8 16.2 %all-to-all-start.3 = ((bf16[32,16,384]{2,1,0:T(8,128)(2,1)}), bf16[32,16,384]{2,1,0:T(8,128)(2,1)S(1)}, u32[]{:S(2)}, u32[]{:S(2)}) async-start(bf16[32,16,384]{2,1,0:T(8,128)(2,1)} %bitcast.15), calls=%async_computation.3 | async-start | bytes 786432 | tf_op jit(solution)/shard_map/all_to_all | solution.py:363

commit v2 on v1

--- a/solution.py
+++ b/solution.py
@@ -173,37 +173,31 @@
     return jnp.concatenate(blocks, axis=0)
 
 
-def sweep(select, table, stiff, coefs, force_ref, held, add):
-    pairs = held[0].shape[0]
-    groups = force_ref.shape[0] // pairs
-    for turn in range(groups + 3):
-        if turn >= 3:
-            add(turn - 3, slice((turn - 3) * pairs, (turn - 2) * pairs))
-        if 2 <= turn < groups + 2:
-            rows = slice((turn - 2) * pairs, (turn - 1) * pairs)
-            force_ref[rows, :] = element_forces(
-                held[turn % 2][...], stiff, *coefs, (turn - 2) * GROUP
-            )
-        if 1 <= turn < groups + 1:
-            rows = slice((turn - 1) * pairs, turn * pairs)
-            held[(turn - 1) % 2][...] = dot(select.made[rows, :], table).astype(BF16)
+def chunks_of(ref, groups):
+    rows = ref.shape[0] // groups
+    return [ref.at[g * rows : (g + 1) * rows, :] for g in range(groups)]
+
+
+def sweep(groups, gather, forces, add):
+    for turn in range(groups + 2):
+        if turn >= 2:
+            add(turn - 2)
+        if 1 <= turn <= groups:
+            forces(turn - 1)
         if turn < groups:
-            select.make(turn)
-
-
-class Selection:
-    def __init__(self, made, columns):
-        self.made = made
-        self.columns = columns
-
-    def make(self, group):
-        pairs = GROUP * self.columns.shape[0]
-        self.made[group * pairs : (group + 1) * pairs, :] = select_rows(
-            self.columns, group * GROUP, self.made.shape[1]
+            gather(turn)
+
+
+def forces_stage(held, stiff_ref, coefs, force_chunks):
+    def stage(group):
+        force_chunks[group][...] = element_forces(
+            held[group % 2][...], stiff_ref[...], *coefs, group * GROUP
         )
 
-
-def dam_part_kernel(
+    return stage
+
+
+def dam_first_kernel(
     free_hbm,
     dam_conn_hbm,
     dam_hbm,
@@ -211,8 +205,10 @@
     stiff_coef_hbm,
     mass_coef_hbm,
     back_hbm,
-    sum_hbm,
     order_hbm,
+    force_hbm,
+    free_made_hbm,
+    dam_made_hbm,
     free_ref,
     dam_conn_ref,
     dam_ref,
@@ -220,13 +216,15 @@
     stiff_coef_ref,
     mass_coef_ref,
     back_ref,
-    sum_ref,
+    force_ref,
     free_made,
     dam_made,
-    force_ref,
     held0,
     held1,
     sems,
+    force_sems,
+    free_sems,
+    dam_sems,
 ):
     inward = transfer(
         [
@@ -239,119 +237,157 @@
         ],
         sems,
     )
-    back_ref[...] = jnp.zeros_like(back_ref)
-    sum_ref[...] = jnp.zeros_like(sum_ref)
     finish(inward)
     stiff_ref[...] = by_component(stiff_ref[...])
     outward = transfer([(stiff_ref, order_hbm)], sems)
-    free = Selection(free_made, free_ref[...].T)
-    dam = Selection(dam_made, dam_conn_ref[...].T)
-
-    def add(group, rows):
-        force = force_ref[rows, :]
-        free.make(group)
-        sum_ref[...] += dot_first(force, dam_made[rows, :])
-        back_ref[...] += dot_first(force, free_made[rows, :])
+    free_columns, dam_columns = free_ref[...].T, dam_conn_ref[...].T
+    groups = dam_conn_ref.shape[0] // GROUP
+    held = (held0, held1)
+    force_chunks = chunks_of(force_ref, groups)
+    free_chunks = chunks_of(free_made, groups)
+    dam_chunks = chunks_of(dam_made, groups)
+
+    def send(chunks, target, sems, group):
+        copy = pltpu.make_async_copy(
+            chunks[group], chunks_of(target, groups)[group], sems.at[group]
+        )
+        copy.start()
+        outward.append(copy)
+
+    def gather(group):
+        select = select_rows(dam_columns, group * GROUP, dam_made.shape[1])
+        dam_chunks[group][...] = select
+        held[group % 2][...] = dot(select, dam_ref[...]).astype(BF16)
+
+    def add(group):
+        select = select_rows(free_columns, group * GROUP, free_made.shape[1])
+        free_chunks[group][...] = select
+        part = dot_first(force_chunks[group][...], select)
+        back_ref[...] = part if group == 0 else back_ref[...] + part
+        send(force_chunks, force_hbm, force_sems, group)
+        send(dam_chunks, dam_made_hbm, dam_sems, group)
+        send(free_chunks, free_made_hbm, free_sems, group)
 
     coefs = (stiff_coef_ref, mass_coef_ref)
-    sweep(dam, dam_ref[...], stiff_ref[...], coefs, force_ref, (held0, held1), add)
+    sweep(groups, gather, forces_stage(held, stiff_ref, coefs, force_chunks), add)
     finish(outward)
-    finish(transfer([(back_ref, back_hbm), (sum_ref, sum_hbm)], sems))
-
-
-def free_part_kernel(
-    free_hbm,
-    received_ref,
-    stiff_hbm,
+    finish(transfer([(back_ref, back_hbm)], sems))
+
+
+def part_kernel(
+    last,
+    gather_hbm,
+    add_hbm,
+    table_ref,
+    order_hbm,
     stiff_coef_hbm,
     mass_coef_hbm,
-    start_hbm,
-    force_hbm,
-    back_hbm,
-    free_ref,
-    stiff_ref,
-    stiff_coef_ref,
-    mass_coef_ref,
-    start_ref,
-    total_ref,
-    made,
-    force_ref,
-    back_ref,
-    held0,
-    held1,
-    sems,
-    out_sems,
-):
+    *refs,
+):
+    if last:
+        (start_hbm, force_hbm, out_hbm, start_ref, out_ref, *refs) = refs
+        add_made, made_sems = None, refs[-2]
+    else:
+        (force_hbm, out_hbm, add_made, add_sems, *refs) = refs
+        made_sems = refs[-2]
+    order_ref, stiff_coef_ref, mass_coef_ref, total_ref, force_ref, made, held0, held1 = refs[:8]
+    sems, made_sems, force_sems = refs[8:]
+    groups = made_sems.shape[0]
+    arriving = transfer(list(zip(chunks_of(gather_hbm, groups), chunks_of(made, groups))), made_sems)
     inward = transfer(
         [
-            (free_hbm, free_ref),
-            (stiff_hbm, stiff_ref),
+            (order_hbm, order_ref),
             (stiff_coef_hbm, stiff_coef_ref),
             (mass_coef_hbm, mass_coef_ref),
-            (start_hbm, start_ref),
         ],
         sems,
     )
-    finish(inward[:4])
+    if last:
+        starting = pltpu.make_async_copy(start_hbm, start_ref, sems.at[3])
+        starting.start()
+    else:
+        adding = transfer(
+            list(zip(chunks_of(add_hbm, groups), chunks_of(add_made, groups))), add_sems
+        )
     outward = []
-
-    def add(group, rows):
-        own = force_ref.at[rows, :]
-        copy = pltpu.make_async_copy(own, force_hbm.at[rows, :], out_sems.at[group])
+    held = (held0, held1)
+    force_chunks = chunks_of(force_ref, groups)
+    made_chunks = chunks_of(made, groups)
+    add_chunks = made_chunks if last else chunks_of(add_made, groups)
+
+    def gather(group):
+        finish(arriving[group : group + 1])
+        held[group % 2][...] = dot(made_chunks[group][...], table_ref[...]).astype(BF16)
+        if group == 0:
+            finish(inward)
+
+    def add(group):
+        if not last:
+            finish(adding[group : group + 1])
+        copy = pltpu.make_async_copy(
+            force_chunks[group], chunks_of(force_hbm, groups)[group], force_sems.at[group]
+        )
         copy.start()
         outward.append(copy)
-        part = dot_first(own[...], made[rows, :])
+        part = dot_first(force_chunks[group][...], add_chunks[group][...])
         total_ref[...] = part if group == 0 else total_ref[...] + part
 
     coefs = (stiff_coef_ref, mass_coef_ref)
-    select = Selection(made, free_ref[...].T)
-    sweep(select, received_ref[...], stiff_ref[...], coefs, force_ref, (held0, held1), add)
-    finish(inward[4:])
-    back_ref[...] = (start_ref[...] + total_ref[...]).T.astype(BF16)
-    finish(transfer([(back_ref, back_hbm)], sems))
+    sweep(groups, gather, forces_stage(held, order_ref, coefs, force_chunks), add)
+    if last:
+        starting.wait()
+        lanes = 128
+        slots = total_ref.shape[1]
+        for i, at in enumerate(range(0, slots, lanes)):
+            part = start_ref[:, at : at + lanes] + total_ref[:, at : at + lanes]
+            out_ref[at : at + lanes, :] = part.T.astype(BF16)
+            copy = pltpu.make_async_copy(
+                out_ref.at[at : at + lanes, :], out_hbm.at[at : at + lanes, :], sems.at[i % 4]
+            )
+            copy.start()
+            outward.append(copy)
+    else:
+        outward += transfer([(total_ref, out_hbm)], sems)
     finish(outward)
 
 
 def dam_update_kernel(
-    dam_conn_hbm,
-    force_hbm,
-    start_hbm,
+    made_hbm,
+    free_force_hbm,
+    dam_force_hbm,
     dam_hbm,
     step_hbm,
     next_hbm,
-    dam_conn_ref,
-    force_ref,
+    made,
+    free_force,
+    dam_force,
     total_ref,
     dam_ref,
     step_ref,
     next_ref,
-    made,
     sems,
-    in_sems,
-):
-    inward = transfer(
-        [
-            (dam_conn_hbm, dam_conn_ref),
-            (start_hbm, total_ref),
-            (dam_hbm, dam_ref),
-            (step_hbm, step_ref),
-        ],
-        sems,
-    )
-    nodes = dam_conn_ref.shape[1]
-    pairs = GROUP * nodes
-    groups = made.shape[0] // pairs
-    chunks = [slice(g * pairs, (g + 1) * pairs) for g in range(groups)]
-    forces = transfer([(force_hbm.at[rows, :], force_ref.at[rows, :]) for rows in chunks], in_sems)
+    made_sems,
+    free_sems,
+    dam_sems,
+):
+    groups = made_sems.shape[0]
+
+    def bring(source, target, sems):
+        return transfer(list(zip(chunks_of(source, groups), chunks_of(target, groups))), sems)
+
+    arriving = [
+        bring(made_hbm, made, made_sems),
+        bring(free_force_hbm, free_force, free_sems),
+        bring(dam_force_hbm, dam_force, dam_sems),
+    ]
+    inward = transfer([(dam_hbm, dam_ref), (step_hbm, step_ref)], sems)
+    for group in range(groups):
+        finish([copies[group] for copies in arriving])
+        force = chunks_of(free_force, groups)[group][...].astype(F32)
+        force = (force + chunks_of(dam_force, groups)[group][...].astype(F32)).astype(BF16)
+        part = dot_first(force, chunks_of(made, groups)[group][...])
+        total_ref[...] = part if group == 0 else total_ref[...] + part
     finish(inward)
-    select = Selection(made, dam_conn_ref[...].T)
-    for turn in range(groups + 1):
-        if turn >= 1:
-            rows = chunks[turn - 1]
-            finish(forces[turn - 1 : turn])
-            total_ref[...] += dot_first(force_ref[rows, :], made[rows, :])
-        if turn < groups:
-            select.make(turn)
     step = as_column(step_ref[...])
     next_ref[...] = (dam_ref[...].astype(F32) - step * total_ref[...].T).astype(BF16)
     finish(transfer([(next_ref, next_hbm)], sems))
@@ -418,9 +454,11 @@
     stiff = vmem(stiff_ref.shape, BF16)
     coefs = [pltpu.SMEM((elements,), F32)] * 2
     held = [vmem((pairs, width), BF16)] * 2
-    forces = vmem((all_pairs, width), BF16)
-    free_made = vmem((all_pairs, slots), BF16)
-    dam_made = vmem((all_pairs, dam_count), BF16)
+    forces_type = ((all_pairs, width), BF16)
+    free_type = ((all_pairs, slots), BF16)
+    dam_rows_type = ((all_pairs, dam_count), BF16)
+    back_type = ((width, slots), F32)
+    stiff_type = (stiff_ref.shape, BF16)
     place_type = ((slots, row_count), BF16)
     slots_type = ((slots, width), BF16)
     rows_type = ((row_count, width), BF16)
@@ -451,25 +489,42 @@
         turn_scratch + [vmem((row_count, width), F32), dma((3,))],
         inside=(1,),
     )
-    dam_part = kernel(
-        dam_part_kernel,
-        "dam_part",
+    dam_first = kernel(
+        dam_first_kernel,
+        "dam_first",
         6,
-        [((width, slots), F32), ((width, dam_count), F32), (stiff_ref.shape, BF16)],
+        [back_type, stiff_type, forces_type, free_type, dam_rows_type],
         [conn, conn, vmem(*dam_type), stiff, *coefs]
-        + [vmem((width, slots), F32), vmem((width, dam_count), F32)]
-        + [free_made, dam_made, forces, *held, dma((6,))],
-        flops=4 * product,
+        + [vmem(*back_type), vmem(*forces_type), vmem(*free_type), vmem(*dam_rows_type)]
+        + [*held, dma((6,)), dma((groups,)), dma((groups,)), dma((groups,))],
+        flops=3 * product,
         moved=4 * all_pairs * width,
     )
+    part_scratch = [stiff, *coefs, vmem(*back_type), vmem(*forces_type)]
+    part_sems = [dma((4,)), dma((groups,)), dma((groups,))]
+    dam_again = kernel(
+        functools.partial(part_kernel, False),
+        "dam_again",
+        6,
+        [forces_type, back_type],
+        [vmem(*free_type), dma((groups,))]
+        + part_scratch
+        + [vmem(*dam_rows_type), *held]
+        + part_sems,
+        inside=(2,),
+        flops=3 * product,
+        moved=4 * all_pairs * width,
+    )
     free_part = kernel(
-        free_part_kernel,
+        functools.partial(part_kernel, True),
         "free_part",
-        6,
-        [((all_pairs, width), BF16), slots_type],
-        [conn, stiff, *coefs, vmem((width, slots), F32), vmem((width, slots), F32)]
-        + [free_made, forces, vmem(*slots_type), *held, dma((5,)), dma((groups,))],
-        inside=(1,),
+        7,
+        [forces_type, slots_type],
+        [vmem(*back_type), vmem(*slots_type)]
+        + part_scratch
+        + [vmem(*free_type), *held]
+        + part_sems,
+        inside=(2,),
         flops=3 * product,
         moved=4 * all_pairs * width,
     )
@@ -478,8 +533,9 @@
         "dam_update",
         5,
         [dam_type],
-        [conn, forces, vmem((width, dam_count), F32), vmem(*dam_type), vmem((1, dam_count), F32)]
-        + [vmem(*dam_type), dam_made, dma((4,)), dma((groups,))],
+        [vmem(*dam_rows_type), vmem(*forces_type), vmem(*forces_type)]
+        + [vmem((width, dam_count), F32), vmem(*dam_type), vmem((1, dam_count), F32)]
+        + [vmem(*dam_type), dma((2,)), dma((groups,)), dma((groups,)), dma((groups,))],
         flops=product,
         moved=4 * all_pairs * width,
     )
@@ -489,12 +545,19 @@
     outgoing, place = pack(routes.T, history)
     for round_index in range(ROUNDS):
         received = exchange(outgoing, devices, capacity)
-        back_start, sum_start, ordered = dam_part(
-            conn_free, conn_dam, dam_field, stiff_ref, stiff_coef, mass_coef
+        if round_index == 0:
+            back_start, ordered, dam_force, free_made, dam_made = dam_first(
+                conn_free, conn_dam, dam_field, stiff_ref, stiff_coef, mass_coef
+            )
+        else:
+            dam_force, back_start = dam_again(
+                dam_made, free_made, dam_field, ordered, stiff_coef, mass_coef
+            )
+        free_force, back = free_part(
+            free_made, free_made, received, ordered, stiff_coef, mass_coef, back_start
         )
-        force, back = free_part(conn_free, received, ordered, stiff_coef, mass_coef, back_start)
         returned = exchange(back, devices, capacity)
-        (dam_field,) = dam_update(conn_dam, force, sum_start, dam_field, dam_row)
+        (dam_field,) = dam_update(dam_made, free_force, dam_force, dam_field, dam_row)
         if round_index < ROUNDS - 1:
             history, outgoing = turn(place, returned, history, reg_row, dam_field)
         else:

time: 92.6 us -> 96.9 us (1.046)
  Pallas kernels: 53.1 us -> 55.7 us
  starting transfers between devices: 15.2 us -> 17.2 us
  waiting for transfers between devices: 22.9 us -> 21.5 us
  local copies, waits for them, and re-layouts: 0 us -> 0.99 us
    pallas_call x9, Pallas kernels: 53.1 us -> 55.7 us  [run(): call(*[x if i in inside else pltpu.with_memory_space_constraint(x, pltpu....]
    all_to_all x4, starting transfers between devices: 15.2 us -> 17.2 us  [exchange(): lax.all_to_all(shaped, ('reg', 'dam'), split_axis=0, concat_axis=0, tiled...]
    all_to_all x4, waiting for transfers between devices: 22.9 us -> 21.5 us  [exchange(): lax.all_to_all(shaped, ('reg', 'dam'), split_axis=0, concat_axis=0, tiled...]
    unnamed x0 -> x2, local copies, waits for them, and re-layouts: none -> 0.99 us
  transfers between devices with their start and end apart: 4 -> 4, of which waited for: 4 -> 4; matrix products, arithmetic and copies ran while one was open for 0% -> 0% of each run, Pallas kernels for 34% -> 33%
where the time goes in v2:
time: 96.9 us; the launch traced here: 96.4 us
  Pallas kernels  55.7 us (57%)
  waiting for transfers between devices  21.5 us (22%)
  starting transfers between devices  17.2 us (18%)
  local copies, waits for them, and re-layouts  0.99 us (1%)
    pallas_call x9, Pallas kernels, run(): call(*[x if i in inside else pltpu.with_memory_space_constraint(x, pltpu....  55.7 us
    all_to_all x4, waiting for transfers between devices, exchange(): lax.all_to_all(shaped, ('reg', 'dam'), split_axis=0, concat_axis=0, tiled...  21.5 us
    all_to_all x4, starting transfers between devices, exchange(): lax.all_to_all(shaped, ('reg', 'dam'), split_axis=0, concat_axis=0, tiled...  17.2 us
  transfers between devices with their start and end apart: 4, of which 4 were waited for; matrix products, arithmetic and copies ran while one was open for 0% of the time, Pallas kernels for 33%

profile of v2, /device:TPU:0, one launch (start us, length us, event | category | flops | bytes accessed | tf_op | source)
XLA Modules:
  0.0 96.4 jit_solution(11484320749183466786)
XLA Ops:
  0.6 2.0 %pack.1 = (bf16[512,384]{1,0:T(8,128)(2,1)}, bf16[512,128]{1,0:T(8,128)(2,1)}) custom-call(s32[2,128]{1,0:T(2,128)} %bitcast.23, bf16[128,384]{1,0:T(8,128)(2,1)} %history_hbm.3), custom_call_target="tpu_custom_call" | custom-call | tf_op jit(solution)/shard_map/pack/pallas_call | solution.py:418
  2.6 7.3 %all-to-all-start = ((bf16[32,16,384]{2,1,0:T(8,128)(2,1)}), bf16[32,16,384]{2,1,0:T(8,128)(2,1)S(1)}, u32[]{:S(2)}, u32[]{:S(2)}) async-start(bf16[32,16,384]{2,1,0:T(8,128)(2,1)} %bitcast.16), calls=%async_computation | async-start | bytes 786432 | tf_op jit(solution)/shard_map/all_to_all | solution.py:399
  9.9 8.6 %dam_first.1 = (f32[384,512]{1,0:T(8,128)}, bf16[192,192]{1,0:T(8,128)(2,1)}, bf16[4096,384]{1,0:T(8,128)(2,1)}, bf16[4096,512]{1,0:T(8,128)(2,1)}, bf16[4096,512]{1,0:T(8,128)(2,1)}) custom-call(s32[64,64]{1,0:T(8,128)} %free_hbm.1, s32[64,64]{1,0:T(8,128)} %dam_conn_hbm.1, bf16[512,384]{1,0:T(8,128)(2,1)} %dam_hbm.3, bf16[192,192]{1,0:T(8,128)(2,1)} %stiff_hbm.1, ...), custom_call_target="tpu_custom_call" | custom-call | flops 4831838208 | bytes 6291456 | tf_op jit(solution)/shard_map/dam_first/pallas_call | solution.py:418
  18.5 4.9 %all-to-all-done = bf16[32,16,384]{2,1,0:T(8,128)(2,1)S(1)} async-done(((bf16[32,16,384]{2,1,0:T(8,128)(2,1)}), bf16[32,16,384]{2,1,0:T(8,128)(2,1)S(1)}, u32[]{:S(2)}, u32[]{:S(2)}) %all-to-all-start) | async-done | bytes 393248 | tf_op jit(solution)/shard_map/all_to_all | solution.py:399
  23.5 9.1 %free_part.2 = (bf16[4096,384]{1,0:T(8,128)(2,1)}, bf16[512,384]{1,0:T(8,128)(2,1)}) custom-call(bf16[4096,512]{1,0:T(8,128)(2,1)} %get-tuple-element.21.gather_hbm.add_hbm, bf16[4096,512]{1,0:T(8,128)(2,1)} %get-tuple-element.21.gather_hbm.add_hbm, bf16[512,384]{1,0:T(8,128)(2,1)S(1)} %bitcast.13, bf16[192,192]{1,0:T(8,128)(2,1)} %get-tuple-element.23.order_hbm, ...), custom_call_target="tpu_custom_call" | custom-call | flops 4831838208 | bytes 6291456 | tf_op jit(solution)/shard_map/free_part/pallas_call | solution.py:418
  32.5 2.6 %all-to-all-start.1 = ((bf16[32,16,384]{2,1,0:T(8,128)(2,1)}), bf16[32,16,384]{2,1,0:T(8,128)(2,1)S(1)}, u32[]{:S(2)}, u32[]{:S(2)}) async-start(bf16[32,16,384]{2,1,0:T(8,128)(2,1)} %bitcast.17), calls=%async_computation.1 | async-start | bytes 786432 | tf_op jit(solution)/shard_map/all_to_all | solution.py:399
  35.2 5.8 %dam_update.2.after_hbm.table_ref.dam_hbm = bf16[512,384]{1,0:T(8,128)(2,1)} custom-call(bf16[4096,512]{1,0:T(8,128)(2,1)} %get-tuple-element.26.made_hbm.gather_hbm, bf16[4096,384]{1,0:T(8,128)(2,1)} %get-tuple-element.27.free_force_hbm, bf16[4096,384]{1,0:T(8,128)(2,1)} %get-tuple-element.28.dam_force_hbm, bf16[512,384]{1,0:T(8,128)(2,1)} %dam_hbm.3, ...), custom_call_target="tpu_custom_call" | custom-call | flops 1610612736 | bytes 6291456 | tf_op jit(solution)/shard_map/dam_update/pallas_call | solution.py:418
  41.0 7.7 %all-to-all-done.1 = bf16[32,16,384]{2,1,0:T(8,128)(2,1)S(1)} async-done(((bf16[32,16,384]{2,1,0:T(8,128)(2,1)}), bf16[32,16,384]{2,1,0:T(8,128)(2,1)S(1)}, u32[]{:S(2)}, u32[]{:S(2)}) %all-to-all-start.1) | async-done | bytes 393248 | tf_op jit(solution)/shard_map/all_to_all | solution.py:399
  48.7 2.2 %turn.1 = (bf16[128,384]{1,0:T(8,128)(2,1)}, bf16[512,384]{1,0:T(8,128)(2,1)}) custom-call(bf16[512,128]{1,0:T(8,128)(2,1)} %get-tuple-element.20.place_hbm, bf16[512,384]{1,0:T(8,128)(2,1)S(1)} %bitcast.12, bf16[128,384]{1,0:T(8,128)(2,1)} %history_hbm.3, f32[1,128]{1,0:T(1,128)} %bitcast.21, bf16[512,384]{1,0:T(8,128)(2,1)} %dam_update.2.after_hbm.table_ref.dam_hbm), custom_call_target="tpu_custom_call" | custom-call | tf_op jit(solution)/shard_map/turn/pallas_call | solution.py:418
  50.9 2.8 %all-to-all-start.2 = ((bf16[32,16,384]{2,1,0:T(8,128)(2,1)}), bf16[32,16,384]{2,1,0:T(8,128)(2,1)S(1)}, u32[]{:S(2)}, u32[]{:S(2)}) async-start(bf16[32,16,384]{2,1,0:T(8,128)(2,1)} %bitcast.18), calls=%async_computation.2 | async-start | bytes 786432 | tf_op jit(solution)/shard_map/all_to_all | solution.py:399
  53.7 0.0 copy-start
  53.7 1.0 %copy-done = bf16[512,384]{1,0:T(8,128)(2,1)S(1)} copy-done((bf16[512,384]{1,0:T(8,128)(2,1)S(1)}, bf16[512,384]{1,0:T(8,128)(2,1)}, u32[]{:S(2)}) %copy-start) | copy-done | bytes 393240
  54.7 11.2 %dam_again.1 = (bf16[4096,384]{1,0:T(8,128)(2,1)}, f32[384,512]{1,0:T(8,128)}) custom-call(bf16[4096,512]{1,0:T(8,128)(2,1)} %get-tuple-element.26.made_hbm.gather_hbm, bf16[4096,512]{1,0:T(8,128)(2,1)} %get-tuple-element.21.gather_hbm.add_hbm, bf16[512,384]{1,0:T(8,128)(2,1)S(1)} %copy-done, bf16[192,192]{1,0:T(8,128)(2,1)} %get-tuple-element.23.order_hbm, ...), custom_call_target="tpu_custom_call" | custom-call | flops 4831838208 | bytes 6291456 | tf_op jit(solution)/shard_map/dam_again/pallas_call | solution.py:418
  65.9 1.2 %all-to-all-done.2 = bf16[32,16,384]{2,1,0:T(8,128)(2,1)S(1)} async-done(((bf16[32,16,384]{2,1,0:T(8,128)(2,1)}), bf16[32,16,384]{2,1,0:T(8,128)(2,1)S(1)}, u32[]{:S(2)}, u32[]{:S(2)}) %all-to-all-start.2) | async-done | bytes 393248 | tf_op jit(solution)/shard_map/all_to_all | solution.py:399
  67.1 9.1 %free_part.3 = (bf16[4096,384]{1,0:T(8,128)(2,1)}, bf16[512,384]{1,0:T(8,128)(2,1)}) custom-call(bf16[4096,512]{1,0:T(8,128)(2,1)} %get-tuple-element.21.gather_hbm.add_hbm, bf16[4096,512]{1,0:T(8,128)(2,1)} %get-tuple-element.21.gather_hbm.add_hbm, bf16[512,384]{1,0:T(8,128)(2,1)S(1)} %bitcast.14, bf16[192,192]{1,0:T(8,128)(2,1)} %get-tuple-element.23.order_hbm, ...), custom_call_target="tpu_custom_call" | custom-call | flops 4831838208 | bytes 6291456 | tf_op jit(solution)/shard_map/free_part/pallas_call | solution.py:418
  76.2 4.5 %all-to-all-start.3 = ((bf16[32,16,384]{2,1,0:T(8,128)(2,1)}), bf16[32,16,384]{2,1,0:T(8,128)(2,1)S(1)}, u32[]{:S(2)}, u32[]{:S(2)}) async-start(bf16[32,16,384]{2,1,0:T(8,128)(2,1)} %bitcast.15), calls=%async_computation.3 | async-start | bytes 786432 | tf_op jit(solution)/shard_map/all_to_all | solution.py:399
  80.7 5.8 %dam_update.3.after_hbm = bf16[512,384]{1,0:T(8,128)(2,1)} custom-call(bf16[4096,512]{1,0:T(8,128)(2,1)} %get-tuple-element.26.made_hbm.gather_hbm, bf16[4096,384]{1,0:T(8,128)(2,1)} %get-tuple-element.33.free_force_hbm, bf16[4096,384]{1,0:T(8,128)(2,1)} %get-tuple-element.34.dam_force_hbm, bf16[512,384]{1,0:T(8,128)(2,1)} %dam_update.2.after_hbm.table_ref.dam_hbm, ...), custom_call_target="tpu_custom_call" | custom-call | flops 1610612736 | bytes 6291456 | tf_op jit(solution)/shard_map/dam_update/pallas_call | solution.py:418
  86.6 7.7 %all-to-all-done.3 = bf16[32,16,384]{2,1,0:T(8,128)(2,1)S(1)} async-done(((bf16[32,16,384]{2,1,0:T(8,128)(2,1)}), bf16[32,16,384]{2,1,0:T(8,128)(2,1)S(1)}, u32[]{:S(2)}, u32[]{:S(2)}) %all-to-all-start.3) | async-done | bytes 393248 | tf_op jit(solution)/shard_map/all_to_all | solution.py:399
  94.3 1.9 %last.1 = (bf16[128,384]{1,0:T(8,128)(2,1)}, f32[128,384]{1,0:T(8,128)}) custom-call(bf16[512,128]{1,0:T(8,128)(2,1)} %get-tuple-element.20.place_hbm, bf16[512,384]{1,0:T(8,128)(2,1)S(1)} %bitcast.11, bf16[128,384]{1,0:T(8,128)(2,1)} %get-tuple-element.32.history_hbm, f32[1,128]{1,0:T(1,128)} %bitcast.22, bf16[512,384]{1,0:T(8,128)(2,1)} %dam_update.3.after_hbm), custom_call_target="tpu_custom_call" | custom-call | tf_op jit(solution)/shard_map/last/pallas_call | solution.py:418
Async XLA Ops:
  2.6 20.9 %all-to-all-start = ((bf16[32,16,384]{2,1,0:T(8,128)(2,1)}), bf16[32,16,384]{2,1,0:T(8,128)(2,1)S(1)}, u32[]{:S(2)}, u32[]{:S(2)}) async-start(bf16[32,16,384]{2,1,0:T(8,128)(2,1)} %bitcast.16), calls=%async_computation | async-start | bytes 786432 | tf_op jit(solution)/shard_map/all_to_all | solution.py:399
  32.5 16.2 %all-to-all-start.1 = ((bf16[32,16,384]{2,1,0:T(8,128)(2,1)}), bf16[32,16,384]{2,1,0:T(8,128)(2,1)S(1)}, u32[]{:S(2)}, u32[]{:S(2)}) async-start(bf16[32,16,384]{2,1,0:T(8,128)(2,1)} %bitcast.17), calls=%async_computation.1 | async-start | bytes 786432 | tf_op jit(solution)/shard_map/all_to_all | solution.py:399
  50.9 16.2 %all-to-all-start.2 = ((bf16[32,16,384]{2,1,0:T(8,128)(2,1)}), bf16[32,16,384]{2,1,0:T(8,128)(2,1)S(1)}, u32[]{:S(2)}, u32[]{:S(2)}) async-start(bf16[32,16,384]{2,1,0:T(8,128)(2,1)} %bitcast.18), calls=%async_computation.2 | async-start | bytes 786432 | tf_op jit(solution)/shard_map/all_to_all | solution.py:399
  53.7 1.0 %copy-start = (bf16[512,384]{1,0:T(8,128)(2,1)S(1)}, bf16[512,384]{1,0:T(8,128)(2,1)}, u32[]{:S(2)}) copy-start(bf16[512,384]{1,0:T(8,128)(2,1)} %dam_update.2.after_hbm.table_ref.dam_hbm) | copy-start | bytes 1179652
  76.2 18.1 %all-to-all-start.3 = ((bf16[32,16,384]{2,1,0:T(8,128)(2,1)}), bf16[32,16,384]{2,1,0:T(8,128)(2,1)S(1)}, u32[]{:S(2)}, u32[]{:S(2)}) async-start(bf16[32,16,384]{2,1,0:T(8,128)(2,1)} %bitcast.15), calls=%async_computation.3 | async-start | bytes 786432 | tf_op jit(solution)/shard_map/all_to_all | solution.py:399

commit v3 on v1

--- a/solution.py
+++ b/solution.py
@@ -173,34 +173,44 @@
     return jnp.concatenate(blocks, axis=0)
 
 
-def sweep(select, table, stiff, coefs, force_ref, held, add):
-    pairs = held[0].shape[0]
-    groups = force_ref.shape[0] // pairs
-    for turn in range(groups + 3):
-        if turn >= 3:
-            add(turn - 3, slice((turn - 3) * pairs, (turn - 2) * pairs))
-        if 2 <= turn < groups + 2:
-            rows = slice((turn - 2) * pairs, (turn - 1) * pairs)
-            force_ref[rows, :] = element_forces(
-                held[turn % 2][...], stiff, *coefs, (turn - 2) * GROUP
-            )
-        if 1 <= turn < groups + 1:
-            rows = slice((turn - 1) * pairs, turn * pairs)
-            held[(turn - 1) % 2][...] = dot(select.made[rows, :], table).astype(BF16)
+def chunks_of(ref, groups):
+    rows = ref.shape[0] // groups
+    return [ref.at[g * rows : (g + 1) * rows, :] for g in range(groups)]
+
+
+def sweep(groups, gather, forces, add):
+    for turn in range(groups + 2):
+        if turn >= 2:
+            add(turn - 2)
+        if 1 <= turn <= groups:
+            forces(turn - 1)
         if turn < groups:
-            select.make(turn)
-
-
-class Selection:
-    def __init__(self, made, columns):
-        self.made = made
-        self.columns = columns
-
-    def make(self, group):
-        pairs = GROUP * self.columns.shape[0]
-        self.made[group * pairs : (group + 1) * pairs, :] = select_rows(
-            self.columns, group * GROUP, self.made.shape[1]
+            gather(turn)
+
+
+def forces_stage(held, stiff_ref, coefs, force_chunks):
+    def stage(group):
+        force_chunks[group][...] = element_forces(
+            held[group % 2][...], stiff_ref[...], *coefs, group * GROUP
         )
+
+    return stage
+
+
+class Sender:
+    def __init__(self, source, target, sems):
+        self.chunks = chunks_of(source, sems.shape[0])
+        self.targets = chunks_of(target, sems.shape[0])
+        self.sems = sems
+        self.started = []
+
+    def start(self, group):
+        copy = pltpu.make_async_copy(self.chunks[group], self.targets[group], self.sems.at[group])
+        copy.start()
+        self.started.append(copy)
+
+    def finish(self):
+        finish(self.started)
 
 
 def dam_part_kernel(
@@ -211,8 +221,8 @@
     stiff_coef_hbm,
     mass_coef_hbm,
     back_hbm,
-    sum_hbm,
     order_hbm,
+    force_hbm,
     free_ref,
     dam_conn_ref,
     dam_ref,
@@ -220,56 +230,59 @@
     stiff_coef_ref,
     mass_coef_ref,
     back_ref,
-    sum_ref,
-    free_made,
-    dam_made,
     force_ref,
     held0,
     held1,
     sems,
+    force_sems,
 ):
     inward = transfer(
         [
-            (free_hbm, free_ref),
             (dam_conn_hbm, dam_conn_ref),
             (dam_hbm, dam_ref),
             (stiff_hbm, stiff_ref),
+            (free_hbm, free_ref),
             (stiff_coef_hbm, stiff_coef_ref),
             (mass_coef_hbm, mass_coef_ref),
         ],
         sems,
     )
-    back_ref[...] = jnp.zeros_like(back_ref)
-    sum_ref[...] = jnp.zeros_like(sum_ref)
     finish(inward)
     stiff_ref[...] = by_component(stiff_ref[...])
     outward = transfer([(stiff_ref, order_hbm)], sems)
-    free = Selection(free_made, free_ref[...].T)
-    dam = Selection(dam_made, dam_conn_ref[...].T)
-
-    def add(group, rows):
-        force = force_ref[rows, :]
-        free.make(group)
-        sum_ref[...] += dot_first(force, dam_made[rows, :])
-        back_ref[...] += dot_first(force, free_made[rows, :])
+    free_columns, dam_columns = free_ref[...].T, dam_conn_ref[...].T
+    groups = force_sems.shape[0]
+    held = (held0, held1)
+    sender = Sender(force_ref, force_hbm, force_sems)
+
+    def gather(group):
+        select = select_rows(dam_columns, group * GROUP, dam_ref.shape[0])
+        held[group % 2][...] = dot(select, dam_ref[...]).astype(BF16)
+
+    def add(group):
+        sender.start(group)
+        select = select_rows(free_columns, group * GROUP, back_ref.shape[1])
+        part = dot_first(sender.chunks[group][...], select)
+        back_ref[...] = part if group == 0 else back_ref[...] + part
 
     coefs = (stiff_coef_ref, mass_coef_ref)
-    sweep(dam, dam_ref[...], stiff_ref[...], coefs, force_ref, (held0, held1), add)
+    sweep(groups, gather, forces_stage(held, stiff_ref, coefs, sender.chunks), add)
     finish(outward)
-    finish(transfer([(back_ref, back_hbm), (sum_ref, sum_hbm)], sems))
+    finish(transfer([(back_ref, back_hbm)], sems))
+    sender.finish()
 
 
 def free_part_kernel(
     free_hbm,
     received_ref,
-    stiff_hbm,
+    order_hbm,
     stiff_coef_hbm,
     mass_coef_hbm,
     start_hbm,
     force_hbm,
     back_hbm,
     free_ref,
-    stiff_ref,
+    order_ref,
     stiff_coef_ref,
     mass_coef_ref,
     start_ref,
@@ -280,78 +293,84 @@
     held0,
     held1,
     sems,
-    out_sems,
+    force_sems,
 ):
     inward = transfer(
         [
             (free_hbm, free_ref),
-            (stiff_hbm, stiff_ref),
+            (order_hbm, order_ref),
             (stiff_coef_hbm, stiff_coef_ref),
             (mass_coef_hbm, mass_coef_ref),
             (start_hbm, start_ref),
         ],
         sems,
     )
-    finish(inward[:4])
+    finish(inward[:1])
+    columns = free_ref[...].T
+    groups = force_sems.shape[0]
+    made_chunks = chunks_of(made, groups)
+    held = (held0, held1)
+    sender = Sender(force_ref, force_hbm, force_sems)
+
+    def gather(group):
+        select = select_rows(columns, group * GROUP, received_ref.shape[0])
+        made_chunks[group][...] = select
+        held[group % 2][...] = dot(select, received_ref[...]).astype(BF16)
+        if group == 0:
+            finish(inward[1:4])
+
+    def add(group):
+        sender.start(group)
+        part = dot_first(sender.chunks[group][...], made_chunks[group][...])
+        total_ref[...] = part if group == 0 else total_ref[...] + part
+
+    coefs = (stiff_coef_ref, mass_coef_ref)
+    sweep(groups, gather, forces_stage(held, order_ref, coefs, sender.chunks), add)
+    finish(inward[4:])
+    slots = total_ref.shape[1]
+    quarter = slots // 4
     outward = []
-
-    def add(group, rows):
-        own = force_ref.at[rows, :]
-        copy = pltpu.make_async_copy(own, force_hbm.at[rows, :], out_sems.at[group])
+    for i in range(4):
+        rows = slice(i * quarter, (i + 1) * quarter)
+        back_ref[rows, :] = (start_ref[:, rows] + total_ref[:, rows]).T.astype(BF16)
+        copy = pltpu.make_async_copy(back_ref.at[rows, :], back_hbm.at[rows, :], sems.at[i])
         copy.start()
         outward.append(copy)
-        part = dot_first(own[...], made[rows, :])
-        total_ref[...] = part if group == 0 else total_ref[...] + part
-
-    coefs = (stiff_coef_ref, mass_coef_ref)
-    select = Selection(made, free_ref[...].T)
-    sweep(select, received_ref[...], stiff_ref[...], coefs, force_ref, (held0, held1), add)
-    finish(inward[4:])
-    back_ref[...] = (start_ref[...] + total_ref[...]).T.astype(BF16)
-    finish(transfer([(back_ref, back_hbm)], sems))
     finish(outward)
+    sender.finish()
 
 
 def dam_update_kernel(
     dam_conn_hbm,
-    force_hbm,
-    start_hbm,
+    free_force_hbm,
+    dam_force_hbm,
     dam_hbm,
     step_hbm,
     next_hbm,
     dam_conn_ref,
-    force_ref,
+    free_force,
+    dam_force,
     total_ref,
     dam_ref,
     step_ref,
     next_ref,
-    made,
     sems,
-    in_sems,
-):
-    inward = transfer(
-        [
-            (dam_conn_hbm, dam_conn_ref),
-            (start_hbm, total_ref),
-            (dam_hbm, dam_ref),
-            (step_hbm, step_ref),
-        ],
-        sems,
-    )
-    nodes = dam_conn_ref.shape[1]
-    pairs = GROUP * nodes
-    groups = made.shape[0] // pairs
-    chunks = [slice(g * pairs, (g + 1) * pairs) for g in range(groups)]
-    forces = transfer([(force_hbm.at[rows, :], force_ref.at[rows, :]) for rows in chunks], in_sems)
+    free_sems,
+    dam_sems,
+):
+    groups = free_sems.shape[0]
+    inward = transfer([(dam_conn_hbm, dam_conn_ref), (dam_hbm, dam_ref), (step_hbm, step_ref)], sems)
+    free_chunks, dam_chunks = chunks_of(free_force, groups), chunks_of(dam_force, groups)
+    free_copies = transfer(list(zip(chunks_of(free_force_hbm, groups), free_chunks)), free_sems)
+    dam_copies = transfer(list(zip(chunks_of(dam_force_hbm, groups), dam_chunks)), dam_sems)
     finish(inward)
-    select = Selection(made, dam_conn_ref[...].T)
-    for turn in range(groups + 1):
-        if turn >= 1:
-            rows = chunks[turn - 1]
-            finish(forces[turn - 1 : turn])
-            total_ref[...] += dot_first(force_ref[rows, :], made[rows, :])
-        if turn < groups:
-            select.make(turn)
+    columns = dam_conn_ref[...].T
+    for group in range(groups):
+        finish([free_copies[group], dam_copies[group]])
+        force = free_chunks[group][...].astype(F32) + dam_chunks[group][...].astype(F32)
+        select = select_rows(columns, group * GROUP, dam_ref.shape[0])
+        part = dot_first(force.astype(BF16), select)
+        total_ref[...] = part if group == 0 else total_ref[...] + part
     step = as_column(step_ref[...])
     next_ref[...] = (dam_ref[...].astype(F32) - step * total_ref[...].T).astype(BF16)
     finish(transfer([(next_ref, next_hbm)], sems))
@@ -418,9 +437,10 @@
     stiff = vmem(stiff_ref.shape, BF16)
     coefs = [pltpu.SMEM((elements,), F32)] * 2
     held = [vmem((pairs, width), BF16)] * 2
-    forces = vmem((all_pairs, width), BF16)
-    free_made = vmem((all_pairs, slots), BF16)
-    dam_made = vmem((all_pairs, dam_count), BF16)
+    forces_type = ((all_pairs, width), BF16)
+    free_type = ((all_pairs, slots), BF16)
+    back_type = ((width, slots), F32)
+    stiff_type = (stiff_ref.shape, BF16)
     place_type = ((slots, row_count), BF16)
     slots_type = ((slots, width), BF16)
     rows_type = ((row_count, width), BF16)
@@ -455,20 +475,20 @@
         dam_part_kernel,
         "dam_part",
         6,
-        [((width, slots), F32), ((width, dam_count), F32), (stiff_ref.shape, BF16)],
-        [conn, conn, vmem(*dam_type), stiff, *coefs]
-        + [vmem((width, slots), F32), vmem((width, dam_count), F32)]
-        + [free_made, dam_made, forces, *held, dma((6,))],
-        flops=4 * product,
+        [back_type, stiff_type, forces_type],
+        [conn, conn, vmem(*dam_type), stiff, *coefs, vmem(*back_type), vmem(*forces_type)]
+        + [*held, dma((6,)), dma((groups,))],
+        flops=3 * product,
         moved=4 * all_pairs * width,
     )
     free_part = kernel(
         free_part_kernel,
         "free_part",
         6,
-        [((all_pairs, width), BF16), slots_type],
-        [conn, stiff, *coefs, vmem((width, slots), F32), vmem((width, slots), F32)]
-        + [free_made, forces, vmem(*slots_type), *held, dma((5,)), dma((groups,))],
+        [forces_type, slots_type],
+        [conn, stiff, *coefs, vmem(*back_type), vmem(*back_type)]
+        + [vmem(*free_type), vmem(*forces_type), vmem(*slots_type), *held]
+        + [dma((5,)), dma((groups,))],
         inside=(1,),
         flops=3 * product,
         moved=4 * all_pairs * width,
@@ -478,8 +498,9 @@
         "dam_update",
         5,
         [dam_type],
-        [conn, forces, vmem((width, dam_count), F32), vmem(*dam_type), vmem((1, dam_count), F32)]
-        + [vmem(*dam_type), dam_made, dma((4,)), dma((groups,))],
+        [conn, vmem(*forces_type), vmem(*forces_type)]
+        + [vmem((width, dam_count), F32), vmem(*dam_type), vmem((1, dam_count), F32)]
+        + [vmem(*dam_type), dma((3,)), dma((groups,)), dma((groups,))],
         flops=product,
         moved=4 * all_pairs * width,
     )
@@ -489,12 +510,14 @@
     outgoing, place = pack(routes.T, history)
     for round_index in range(ROUNDS):
         received = exchange(outgoing, devices, capacity)
-        back_start, sum_start, ordered = dam_part(
+        back_start, ordered, dam_force = dam_part(
             conn_free, conn_dam, dam_field, stiff_ref, stiff_coef, mass_coef
         )
-        force, back = free_part(conn_free, received, ordered, stiff_coef, mass_coef, back_start)
+        free_force, back = free_part(
+            conn_free, received, ordered, stiff_coef, mass_coef, back_start
+        )
         returned = exchange(back, devices, capacity)
-        (dam_field,) = dam_update(conn_dam, force, sum_start, dam_field, dam_row)
+        (dam_field,) = dam_update(conn_dam, free_force, dam_force, dam_field, dam_row)
         if round_index < ROUNDS - 1:
             history, outgoing = turn(place, returned, history, reg_row, dam_field)
         else:

time: 92.6 us -> 91.8 us (level)
  Pallas kernels: 53.1 us -> 49.9 us
  waiting for transfers between devices: 22.9 us -> 24.9 us
    pallas_call x9, Pallas kernels: 53.1 us -> 49.9 us  [run(): call(*[x if i in inside else pltpu.with_memory_space_constraint(x, pltpu....]
    all_to_all x4, waiting for transfers between devices: 22.9 us -> 24.9 us  [exchange(): lax.all_to_all(shaped, ('reg', 'dam'), split_axis=0, concat_axis=0, tiled...]
  transfers between devices with their start and end apart: 4 -> 4, of which waited for: 4 -> 4; matrix products, arithmetic and copies ran while one was open for 0% -> 0% of each run, Pallas kernels for 34% -> 32%
where the time goes in v3:
time: 91.8 us; the launch traced here: 91.3 us
  Pallas kernels  49.9 us (54%)
  waiting for transfers between devices  24.9 us (27%)
  starting transfers between devices  15.6 us (17%)
    pallas_call x9, Pallas kernels, run(): call(*[x if i in inside else pltpu.with_memory_space_constraint(x, pltpu....  49.9 us
    all_to_all x4, waiting for transfers between devices, exchange(): lax.all_to_all(shaped, ('reg', 'dam'), split_axis=0, concat_axis=0, tiled...  24.9 us
    all_to_all x4, starting transfers between devices, exchange(): lax.all_to_all(shaped, ('reg', 'dam'), split_axis=0, concat_axis=0, tiled...  15.6 us
  transfers between devices with their start and end apart: 4, of which 4 were waited for; matrix products, arithmetic and copies ran while one was open for 0% of the time, Pallas kernels for 32%

profile of v3, /device:TPU:0, one launch (start us, length us, event | category | flops | bytes accessed | tf_op | source)
XLA Modules:
  0.0 91.3 jit_solution(9713756968044111003)
XLA Ops:
  0.6 2.0 %pack.1 = (bf16[512,384]{1,0:T(8,128)(2,1)}, bf16[512,128]{1,0:T(8,128)(2,1)}) custom-call(s32[2,128]{1,0:T(2,128)} %bitcast.23, bf16[128,384]{1,0:T(8,128)(2,1)} %history_hbm.3), custom_call_target="tpu_custom_call" | custom-call | tf_op jit(solution)/shard_map/pack/pallas_call | solution.py:401
  2.6 7.3 %all-to-all-start = ((bf16[32,16,384]{2,1,0:T(8,128)(2,1)}), bf16[32,16,384]{2,1,0:T(8,128)(2,1)S(1)}, u32[]{:S(2)}, u32[]{:S(2)}) async-start(bf16[32,16,384]{2,1,0:T(8,128)(2,1)} %bitcast.18), calls=%async_computation | async-start | bytes 786432 | tf_op jit(solution)/shard_map/all_to_all | solution.py:382
  9.9 7.8 %dam_part.2 = (f32[384,512]{1,0:T(8,128)}, bf16[192,192]{1,0:T(8,128)(2,1)}, bf16[4096,384]{1,0:T(8,128)(2,1)}) custom-call(s32[64,64]{1,0:T(8,128)} %free_hbm.7, s32[64,64]{1,0:T(8,128)} %dam_conn_hbm.7, bf16[512,384]{1,0:T(8,128)(2,1)} %dam_hbm.3, bf16[192,192]{1,0:T(8,128)(2,1)} %stiff_hbm.3, f32[64]{0:T(128)} %stiff_coef_hbm.7, f32[64]{0:T(128)} %mass_coef_hbm.7), custom_call_target="tpu_custom_call" | custom-call | flops 4831838208 | bytes 6291456 | tf_op jit(solution)/shard_map/dam_part/pallas_call | solution.py:401
  17.7 5.7 %all-to-all-done = bf16[32,16,384]{2,1,0:T(8,128)(2,1)S(1)} async-done(((bf16[32,16,384]{2,1,0:T(8,128)(2,1)}), bf16[32,16,384]{2,1,0:T(8,128)(2,1)S(1)}, u32[]{:S(2)}, u32[]{:S(2)}) %all-to-all-start) | async-done | bytes 393248 | tf_op jit(solution)/shard_map/all_to_all | solution.py:382
  23.5 7.4 %free_part.2 = (bf16[4096,384]{1,0:T(8,128)(2,1)}, bf16[512,384]{1,0:T(8,128)(2,1)}) custom-call(s32[64,64]{1,0:T(8,128)} %free_hbm.7, bf16[512,384]{1,0:T(8,128)(2,1)S(1)} %bitcast.13, bf16[192,192]{1,0:T(8,128)(2,1)} %get-tuple-element.21.order_hbm, f32[64]{0:T(128)} %stiff_coef_hbm.7, f32[64]{0:T(128)} %mass_coef_hbm.7, ...), custom_call_target="tpu_custom_call" | custom-call | flops 4831838208 | bytes 6291456 | tf_op jit(solution)/shard_map/free_part/pallas_call | solution.py:401
  30.8 2.8 %all-to-all-start.1 = ((bf16[32,16,384]{2,1,0:T(8,128)(2,1)}), bf16[32,16,384]{2,1,0:T(8,128)(2,1)S(1)}, u32[]{:S(2)}, u32[]{:S(2)}) async-start(bf16[32,16,384]{2,1,0:T(8,128)(2,1)} %bitcast.16), calls=%async_computation.1 | async-start | bytes 786432 | tf_op jit(solution)/shard_map/all_to_all | solution.py:382
  33.6 6.7 %dam_update.2.after_hbm.dam_hbm = bf16[512,384]{1,0:T(8,128)(2,1)} custom-call(s32[64,64]{1,0:T(8,128)} %dam_conn_hbm.7, bf16[4096,384]{1,0:T(8,128)(2,1)} %get-tuple-element.24.free_force_hbm, bf16[4096,384]{1,0:T(8,128)(2,1)} %get-tuple-element.25.dam_force_hbm, bf16[512,384]{1,0:T(8,128)(2,1)} %dam_hbm.3, f32[1,512]{1,0:T(1,128)} %bitcast.19), custom_call_target="tpu_custom_call" | custom-call | flops 1610612736 | bytes 6291456 | tf_op jit(solution)/shard_map/dam_update/pallas_call | solution.py:401
  40.4 6.8 %all-to-all-done.1 = bf16[32,16,384]{2,1,0:T(8,128)(2,1)S(1)} async-done(((bf16[32,16,384]{2,1,0:T(8,128)(2,1)}), bf16[32,16,384]{2,1,0:T(8,128)(2,1)S(1)}, u32[]{:S(2)}, u32[]{:S(2)}) %all-to-all-start.1) | async-done | bytes 393248 | tf_op jit(solution)/shard_map/all_to_all | solution.py:382
  47.2 2.2 %turn.1 = (bf16[128,384]{1,0:T(8,128)(2,1)}, bf16[512,384]{1,0:T(8,128)(2,1)}) custom-call(bf16[512,128]{1,0:T(8,128)(2,1)} %get-tuple-element.19.place_hbm, bf16[512,384]{1,0:T(8,128)(2,1)S(1)} %bitcast.12, bf16[128,384]{1,0:T(8,128)(2,1)} %history_hbm.3, f32[1,128]{1,0:T(1,128)} %bitcast.21, bf16[512,384]{1,0:T(8,128)(2,1)} %dam_update.2.after_hbm.dam_hbm), custom_call_target="tpu_custom_call" | custom-call | tf_op jit(solution)/shard_map/turn/pallas_call | solution.py:401
  49.4 2.6 %all-to-all-start.2 = ((bf16[32,16,384]{2,1,0:T(8,128)(2,1)}), bf16[32,16,384]{2,1,0:T(8,128)(2,1)S(1)}, u32[]{:S(2)}, u32[]{:S(2)}) async-start(bf16[32,16,384]{2,1,0:T(8,128)(2,1)} %bitcast.17), calls=%async_computation.2 | async-start | bytes 786432 | tf_op jit(solution)/shard_map/all_to_all | solution.py:382
  52.0 7.8 %dam_part.3 = (f32[384,512]{1,0:T(8,128)}, bf16[192,192]{1,0:T(8,128)(2,1)}, bf16[4096,384]{1,0:T(8,128)(2,1)}) custom-call(s32[64,64]{1,0:T(8,128)} %free_hbm.7, s32[64,64]{1,0:T(8,128)} %dam_conn_hbm.7, bf16[512,384]{1,0:T(8,128)(2,1)} %dam_update.2.after_hbm.dam_hbm, bf16[192,192]{1,0:T(8,128)(2,1)} %stiff_hbm.3, f32[64]{0:T(128)} %stiff_coef_hbm.7, ...), custom_call_target="tpu_custom_call" | custom-call | flops 4831838208 | bytes 6291456 | tf_op jit(solution)/shard_map/dam_part/pallas_call | solution.py:401
  59.8 5.7 %all-to-all-done.2 = bf16[32,16,384]{2,1,0:T(8,128)(2,1)S(1)} async-done(((bf16[32,16,384]{2,1,0:T(8,128)(2,1)}), bf16[32,16,384]{2,1,0:T(8,128)(2,1)S(1)}, u32[]{:S(2)}, u32[]{:S(2)}) %all-to-all-start.2) | async-done | bytes 393248 | tf_op jit(solution)/shard_map/all_to_all | solution.py:382
  65.6 7.4 %free_part.3 = (bf16[4096,384]{1,0:T(8,128)(2,1)}, bf16[512,384]{1,0:T(8,128)(2,1)}) custom-call(s32[64,64]{1,0:T(8,128)} %free_hbm.7, bf16[512,384]{1,0:T(8,128)(2,1)S(1)} %bitcast.14, bf16[192,192]{1,0:T(8,128)(2,1)} %get-tuple-element.27.order_hbm, f32[64]{0:T(128)} %stiff_coef_hbm.7, f32[64]{0:T(128)} %mass_coef_hbm.7, ...), custom_call_target="tpu_custom_call" | custom-call | flops 4831838208 | bytes 6291456 | tf_op jit(solution)/shard_map/free_part/pallas_call | solution.py:401
  73.0 2.8 %all-to-all-start.3 = ((bf16[32,16,384]{2,1,0:T(8,128)(2,1)}), bf16[32,16,384]{2,1,0:T(8,128)(2,1)S(1)}, u32[]{:S(2)}, u32[]{:S(2)}) async-start(bf16[32,16,384]{2,1,0:T(8,128)(2,1)} %bitcast.15), calls=%async_computation.3 | async-start | bytes 786432 | tf_op jit(solution)/shard_map/all_to_all | solution.py:382
  75.8 6.7 %dam_update.3.after_hbm = bf16[512,384]{1,0:T(8,128)(2,1)} custom-call(s32[64,64]{1,0:T(8,128)} %dam_conn_hbm.7, bf16[4096,384]{1,0:T(8,128)(2,1)} %get-tuple-element.31.free_force_hbm, bf16[4096,384]{1,0:T(8,128)(2,1)} %get-tuple-element.32.dam_force_hbm, bf16[512,384]{1,0:T(8,128)(2,1)} %dam_update.2.after_hbm.dam_hbm, f32[1,512]{1,0:T(1,128)} %bitcast.20), custom_call_target="tpu_custom_call" | custom-call | flops 1610612736 | bytes 6291456 | tf_op jit(solution)/shard_map/dam_update/pallas_call | solution.py:401
  82.5 6.6 %all-to-all-done.3 = bf16[32,16,384]{2,1,0:T(8,128)(2,1)S(1)} async-done(((bf16[32,16,384]{2,1,0:T(8,128)(2,1)}), bf16[32,16,384]{2,1,0:T(8,128)(2,1)S(1)}, u32[]{:S(2)}, u32[]{:S(2)}) %all-to-all-start.3) | async-done | bytes 393248 | tf_op jit(solution)/shard_map/all_to_all | solution.py:382
  89.1 2.0 %last.1 = (bf16[128,384]{1,0:T(8,128)(2,1)}, f32[128,384]{1,0:T(8,128)}) custom-call(bf16[512,128]{1,0:T(8,128)(2,1)} %get-tuple-element.19.place_hbm, bf16[512,384]{1,0:T(8,128)(2,1)S(1)} %bitcast.11, bf16[128,384]{1,0:T(8,128)(2,1)} %get-tuple-element.30.history_hbm, f32[1,128]{1,0:T(1,128)} %bitcast.22, bf16[512,384]{1,0:T(8,128)(2,1)} %dam_update.3.after_hbm), custom_call_target="tpu_custom_call" | custom-call | tf_op jit(solution)/shard_map/last/pallas_call | solution.py:401
Async XLA Ops:
  2.6 20.9 %all-to-all-start = ((bf16[32,16,384]{2,1,0:T(8,128)(2,1)}), bf16[32,16,384]{2,1,0:T(8,128)(2,1)S(1)}, u32[]{:S(2)}, u32[]{:S(2)}) async-start(bf16[32,16,384]{2,1,0:T(8,128)(2,1)} %bitcast.18), calls=%async_computation | async-start | bytes 786432 | tf_op jit(solution)/shard_map/all_to_all | solution.py:382
  30.8 16.3 %all-to-all-start.1 = ((bf16[32,16,384]{2,1,0:T(8,128)(2,1)}), bf16[32,16,384]{2,1,0:T(8,128)(2,1)S(1)}, u32[]{:S(2)}, u32[]{:S(2)}) async-start(bf16[32,16,384]{2,1,0:T(8,128)(2,1)} %bitcast.16), calls=%async_computation.1 | async-start | bytes 786432 | tf_op jit(solution)/shard_map/all_to_all | solution.py:382
  49.4 16.2 %all-to-all-start.2 = ((bf16[32,16,384]{2,1,0:T(8,128)(2,1)}), bf16[32,16,384]{2,1,0:T(8,128)(2,1)S(1)}, u32[]{:S(2)}, u32[]{:S(2)}) async-start(bf16[32,16,384]{2,1,0:T(8,128)(2,1)} %bitcast.17), calls=%async_computation.2 | async-start | bytes 786432 | tf_op jit(solution)/shard_map/all_to_all | solution.py:382
  73.0 16.2 %all-to-all-start.3 = ((bf16[32,16,384]{2,1,0:T(8,128)(2,1)}), bf16[32,16,384]{2,1,0:T(8,128)(2,1)S(1)}, u32[]{:S(2)}, u32[]{:S(2)}) async-start(bf16[32,16,384]{2,1,0:T(8,128)(2,1)} %bitcast.15), calls=%async_computation.3 | async-start | bytes 786432 | tf_op jit(solution)/shard_map/all_to_all | solution.py:382

commit v4 on v3

--- a/solution.py
+++ b/solution.py
@@ -46,9 +46,22 @@
 
 
 def pack_kernel(
-    capacity, routes_hbm, history_hbm, out_hbm, place_hbm, routes_ref, history_ref, out_ref, place_ref, sems
-):
-    inward = transfer([(routes_hbm, routes_ref), (history_hbm, history_ref)], sems)
+    capacity,
+    routes_hbm,
+    history_hbm,
+    step_hbm,
+    out_hbm,
+    place_ref,
+    history_ref,
+    column_ref,
+    routes_ref,
+    step_ref,
+    out_ref,
+    sems,
+):
+    inward = transfer(
+        [(routes_hbm, routes_ref), (history_hbm, history_ref), (step_hbm, step_ref)], sems
+    )
     slots, rows = place_ref.shape
     finish(inward[:1])
     row0, row1 = routes_ref[0:1, :], routes_ref[1:2, :]
@@ -65,61 +78,39 @@
     place_ref[...] = place
     finish(inward[1:])
     out_ref[...] = dot(place, history_ref[...]).astype(BF16)
-    finish(transfer([(out_ref, out_hbm), (place_ref, place_hbm)], sems))
+    outward = transfer([(out_ref, out_hbm)], sems)
+    column_ref[...] = jnp.broadcast_to(as_column(step_ref[...]), column_ref.shape)
+    finish(outward)
 
 
 def turn_kernel(
-    place_hbm,
-    returned_ref,
-    history_hbm,
-    step_hbm,
-    after_hbm,
-    next_hbm,
-    out_hbm,
-    place_ref,
-    history_ref,
-    step_ref,
-    next_ref,
-    out_ref,
-    sems,
-):
-    inward = transfer(
-        [(place_hbm, place_ref), (history_hbm, history_ref), (step_hbm, step_ref)], sems
-    )
-    finish(inward)
+    place_ref, returned_ref, history_ref, column_ref, after_hbm, next_ref, out_hbm, out_ref, sems
+):
     place = place_ref[...]
     pulled = dot_first(place, returned_ref[...])
-    step = as_column(step_ref[...])
-    following = (history_ref[...].astype(F32) - step * pulled).astype(BF16)
+    following = (history_ref[...].astype(F32) - column_ref[:, 0:1] * pulled).astype(BF16)
     next_ref[...] = following
     out_ref[...] = dot(place, following).astype(BF16)
-    finish(transfer([(next_ref, next_hbm), (out_ref, out_hbm)], sems))
+    finish(transfer([(out_ref, out_hbm)], sems))
 
 
 def last_kernel(
-    place_hbm,
+    place_ref,
     returned_ref,
-    history_hbm,
-    step_hbm,
+    history_ref,
+    column_ref,
     after_hbm,
     next_hbm,
     pulled_hbm,
-    place_ref,
-    history_ref,
-    step_ref,
     next_ref,
     pulled_ref,
     sems,
 ):
-    inward = transfer(
-        [(place_hbm, place_ref), (history_hbm, history_ref), (step_hbm, step_ref)], sems
-    )
-    finish(inward)
     pulled = dot_first(place_ref[...], returned_ref[...])
-    step = as_column(step_ref[...])
-    next_ref[...] = (history_ref[...].astype(F32) - step * pulled).astype(BF16)
     pulled_ref[...] = pulled
-    finish(transfer([(next_ref, next_hbm), (pulled_ref, pulled_hbm)], sems))
+    outward = transfer([(pulled_ref, pulled_hbm)], sems)
+    next_ref[...] = (history_ref[...].astype(F32) - column_ref[:, 0:1] * pulled).astype(BF16)
+    finish(outward + transfer([(next_ref, next_hbm)], sems.at[1:2]))
 
 
 def by_component(stiff):
@@ -221,7 +212,8 @@
     stiff_coef_hbm,
     mass_coef_hbm,
     back_hbm,
-    order_hbm,
+    order_ref,
+    columns_ref,
     force_hbm,
     free_ref,
     dam_conn_ref,
@@ -248,9 +240,9 @@
         sems,
     )
     finish(inward)
-    stiff_ref[...] = by_component(stiff_ref[...])
-    outward = transfer([(stiff_ref, order_hbm)], sems)
+    order_ref[...] = by_component(stiff_ref[...])
     free_columns, dam_columns = free_ref[...].T, dam_conn_ref[...].T
+    columns_ref[...] = free_columns
     groups = force_sems.shape[0]
     held = (held0, held1)
     sender = Sender(force_ref, force_hbm, force_sems)
@@ -266,23 +258,20 @@
         back_ref[...] = part if group == 0 else back_ref[...] + part
 
     coefs = (stiff_coef_ref, mass_coef_ref)
-    sweep(groups, gather, forces_stage(held, stiff_ref, coefs, sender.chunks), add)
-    finish(outward)
+    sweep(groups, gather, forces_stage(held, order_ref, coefs, sender.chunks), add)
     finish(transfer([(back_ref, back_hbm)], sems))
     sender.finish()
 
 
 def free_part_kernel(
-    free_hbm,
+    columns_ref,
     received_ref,
-    order_hbm,
+    order_ref,
     stiff_coef_hbm,
     mass_coef_hbm,
     start_hbm,
     force_hbm,
     back_hbm,
-    free_ref,
-    order_ref,
     stiff_coef_ref,
     mass_coef_ref,
     start_ref,
@@ -297,16 +286,13 @@
 ):
     inward = transfer(
         [
-            (free_hbm, free_ref),
-            (order_hbm, order_ref),
             (stiff_coef_hbm, stiff_coef_ref),
             (mass_coef_hbm, mass_coef_ref),
             (start_hbm, start_ref),
         ],
         sems,
     )
-    finish(inward[:1])
-    columns = free_ref[...].T
+    columns = columns_ref[...]
     groups = force_sems.shape[0]
     made_chunks = chunks_of(made, groups)
     held = (held0, held1)
@@ -317,7 +303,7 @@
         made_chunks[group][...] = select
         held[group % 2][...] = dot(select, received_ref[...]).astype(BF16)
         if group == 0:
-            finish(inward[1:4])
+            finish(inward[:2])
 
     def add(group):
         sender.start(group)
@@ -326,7 +312,7 @@
 
     coefs = (stiff_coef_ref, mass_coef_ref)
     sweep(groups, gather, forces_stage(held, order_ref, coefs, sender.chunks), add)
-    finish(inward[4:])
+    finish(inward[2:])
     slots = total_ref.shape[1]
     quarter = slots // 4
     outward = []
@@ -383,15 +369,16 @@
     return arrived.reshape(devices * capacity, width)
 
 
-def kernel(body, name, n_in, outs, scratch, inside=(), flops=0, moved=0):
+def kernel(body, name, ins, outs, scratch, flops=0, moved=0):
     hbm = pl.BlockSpec(memory_space=pltpu.HBM)
     vmem = pl.BlockSpec(memory_space=pltpu.VMEM)
+    spaces = {"h": pltpu.HBM, "v": pltpu.VMEM}
     call = pl.pallas_call(
         body,
         name=name,
-        in_specs=[vmem if i in inside else hbm for i in range(n_in)],
-        out_specs=[hbm] * len(outs),
-        out_shape=[pltpu.HBM(*out) for out in outs],
+        in_specs=[hbm if letter == "h" else vmem for letter in ins],
+        out_specs=[hbm if out[0] == "h" else vmem for out in outs],
+        out_shape=[spaces[out[0]](*out[1:]) for out in outs],
         scratch_shapes=scratch,
         compiler_params=pltpu.CompilerParams(vmem_limit_bytes=VMEM_BYTES),
         cost_estimate=pl.CostEstimate(flops=flops, bytes_accessed=moved, transcendentals=0),
@@ -400,8 +387,8 @@
     def run(*operands):
         return call(
             *[
-                x if i in inside else pltpu.with_memory_space_constraint(x, pltpu.HBM)
-                for i, x in enumerate(operands)
+                x if letter == "a" else pltpu.with_memory_space_constraint(x, spaces[letter])
+                for letter, x in zip(ins, operands)
             ]
         )
 
@@ -444,38 +431,37 @@
     place_type = ((slots, row_count), BF16)
     slots_type = ((slots, width), BF16)
     rows_type = ((row_count, width), BF16)
+    pulled_type = ((row_count, width), F32)
+    column_type = ((row_count, 128), F32)
     dam_type = ((dam_count, width), BF16)
     product = 2 * all_pairs * slots * width
 
     pack = kernel(
         functools.partial(pack_kernel, capacity),
         "pack",
-        2,
-        [slots_type, place_type],
-        [vmem((2, row_count), I32), vmem(*rows_type), vmem(*slots_type), vmem(*place_type), dma((2,))],
-    )
-    turn_scratch = [vmem(*place_type), vmem(*rows_type), vmem((1, row_count), F32), vmem(*rows_type)]
+        "hhh",
+        [("h", *slots_type), ("v", *place_type), ("v", *rows_type), ("v", *column_type)],
+        [vmem((2, row_count), I32), vmem((1, row_count), F32), vmem(*slots_type), dma((3,))],
+    )
     turn = kernel(
         turn_kernel,
         "turn",
-        5,
-        [rows_type, slots_type],
-        turn_scratch + [vmem(*slots_type), dma((3,))],
-        inside=(1,),
+        "vavvh",
+        [("v", *rows_type), ("h", *slots_type)],
+        [vmem(*slots_type), dma((1,))],
     )
     last = kernel(
         last_kernel,
         "last",
-        5,
-        [rows_type, ((row_count, width), F32)],
-        turn_scratch + [vmem((row_count, width), F32), dma((3,))],
-        inside=(1,),
+        "vavvh",
+        [("h", *rows_type), ("h", *pulled_type)],
+        [vmem(*rows_type), vmem(*pulled_type), dma((2,))],
     )
     dam_part = kernel(
         dam_part_kernel,
         "dam_part",
-        6,
-        [back_type, stiff_type, forces_type],
+        "hhhhhh",
+        [("h", *back_type), ("v", *stiff_type), ("v", (nodes, elements), I32), ("h", *forces_type)],
         [conn, conn, vmem(*dam_type), stiff, *coefs, vmem(*back_type), vmem(*forces_type)]
         + [*held, dma((6,)), dma((groups,))],
         flops=3 * product,
@@ -484,20 +470,19 @@
     free_part = kernel(
         free_part_kernel,
         "free_part",
-        6,
-        [forces_type, slots_type],
-        [conn, stiff, *coefs, vmem(*back_type), vmem(*back_type)]
+        "vavhhh",
+        [("h", *forces_type), ("h", *slots_type)],
+        [*coefs, vmem(*back_type), vmem(*back_type)]
         + [vmem(*free_type), vmem(*forces_type), vmem(*slots_type), *held]
-        + [dma((5,)), dma((groups,))],
-        inside=(1,),
+        + [dma((4,)), dma((groups,))],
         flops=3 * product,
         moved=4 * all_pairs * width,
     )
     dam_update = kernel(
         dam_update_kernel,
         "dam_update",
-        5,
-        [dam_type],
+        "hhhhh",
+        [("h", *dam_type)],
         [conn, vmem(*forces_type), vmem(*forces_type)]
         + [vmem((width, dam_count), F32), vmem(*dam_type), vmem((1, dam_count), F32)]
         + [vmem(*dam_type), dma((3,)), dma((groups,)), dma((groups,))],
@@ -507,21 +492,21 @@
 
     reg_row = reg_step.reshape(1, row_count)
     dam_row = dam_step.reshape(1, dam_count)
-    outgoing, place = pack(routes.T, history)
+    outgoing, place, history, reg_column = pack(routes.T, history, reg_row)
     for round_index in range(ROUNDS):
         received = exchange(outgoing, devices, capacity)
-        back_start, ordered, dam_force = dam_part(
+        back_start, ordered, columns, dam_force = dam_part(
             conn_free, conn_dam, dam_field, stiff_ref, stiff_coef, mass_coef
         )
         free_force, back = free_part(
-            conn_free, received, ordered, stiff_coef, mass_coef, back_start
+            columns, received, ordered, stiff_coef, mass_coef, back_start
         )
         returned = exchange(back, devices, capacity)
         (dam_field,) = dam_update(conn_dam, free_force, dam_force, dam_field, dam_row)
         if round_index < ROUNDS - 1:
-            history, outgoing = turn(place, returned, history, reg_row, dam_field)
+            history, outgoing = turn(place, returned, history, reg_column, dam_field)
         else:
-            history, pulled = last(place, returned, history, reg_row, dam_field)
+            history, pulled = last(place, returned, history, reg_column, dam_field)
     return (history, pulled, dam_field)
 
 

time: 91.8 us -> 88.3 us (0.962)
  Pallas kernels: 49.9 us -> 46.8 us
    pallas_call x9, Pallas kernels: 49.9 us -> 46.8 us  [run(): call(*[x if letter == 'a' else pltpu.with_memory_space_constraint(x, spac...]
  transfers between devices with their start and end apart: 4 -> 4, of which waited for: 4 -> 4; matrix products, arithmetic and copies ran while one was open for 0% -> 0% of each run, Pallas kernels for 32% -> 33%
where the time goes in v4:
time: 88.3 us; the launch traced here: 87.8 us
  Pallas kernels  46.8 us (53%)
  waiting for transfers between devices  24.6 us (28%)
  starting transfers between devices  15.5 us (18%)
  between operations  0.91 us (1%)
    pallas_call x9, Pallas kernels, run(): call(*[x if letter == 'a' else pltpu.with_memory_space_constraint(x, spac...  46.8 us
    all_to_all x4, waiting for transfers between devices, exchange(): lax.all_to_all(shaped, ('reg', 'dam'), split_axis=0, concat_axis=0, tiled...  24.6 us
    all_to_all x4, starting transfers between devices, exchange(): lax.all_to_all(shaped, ('reg', 'dam'), split_axis=0, concat_axis=0, tiled...  15.5 us
  transfers between devices with their start and end apart: 4, of which 4 were waited for; matrix products, arithmetic and copies ran while one was open for 0% of the time, Pallas kernels for 33%

profile of v4, /device:TPU:0, one launch (start us, length us, event | category | flops | bytes accessed | tf_op | source)
XLA Modules:
  0.0 87.8 jit_solution(4730839687825108840)
XLA Ops:
  0.6 2.0 %pack.1 = (bf16[512,384]{1,0:T(8,128)(2,1)}, bf16[512,128]{1,0:T(8,128)(2,1)S(1)}, bf16[128,384]{1,0:T(8,128)(2,1)S(1)}, f32[128,128]{1,0:T(8,128)S(1)}) custom-call(s32[2,128]{1,0:T(2,128)} %bitcast.21, bf16[128,384]{1,0:T(8,128)(2,1)} %history_hbm.1, f32[1,128]{1,0:T(1,128)} %bitcast.22), custom_call_target="tpu_custom_call" | custom-call | tf_op jit(solution)/shard_map/pack/pallas_call | solution.py:388
  2.6 7.3 %all-to-all-start = ((bf16[32,16,384]{2,1,0:T(8,128)(2,1)}), bf16[32,16,384]{2,1,0:T(8,128)(2,1)S(1)}, u32[]{:S(2)}, u32[]{:S(2)}) async-start(bf16[32,16,384]{2,1,0:T(8,128)(2,1)} %bitcast.16), calls=%async_computation | async-start | bytes 786432 | tf_op jit(solution)/shard_map/all_to_all | solution.py:368
  9.9 7.9 %dam_part.2 = (f32[384,512]{1,0:T(8,128)}, bf16[192,192]{1,0:T(8,128)(2,1)S(1)}, s32[64,64]{1,0:T(8,128)S(1)}, bf16[4096,384]{1,0:T(8,128)(2,1)}) custom-call(s32[64,64]{1,0:T(8,128)} %free_hbm.3, s32[64,64]{1,0:T(8,128)} %dam_conn_hbm.7, bf16[512,384]{1,0:T(8,128)(2,1)} %dam_hbm.3, bf16[192,192]{1,0:T(8,128)(2,1)} %stiff_hbm.3, f32[64]{0:T(128)} %stiff_coef_hbm.7, ...), custom_call_target="tpu_custom_call" | custom-call | flops 4831838208 | bytes 6291456 | tf_op jit(solution)/shard_map/dam_part/pallas_call | solution.py:388
  17.8 5.7 %all-to-all-done = bf16[32,16,384]{2,1,0:T(8,128)(2,1)S(1)} async-done(((bf16[32,16,384]{2,1,0:T(8,128)(2,1)}), bf16[32,16,384]{2,1,0:T(8,128)(2,1)S(1)}, u32[]{:S(2)}, u32[]{:S(2)}) %all-to-all-start) | async-done | bytes 393248 | tf_op jit(solution)/shard_map/all_to_all | solution.py:368
  23.4 6.7 %free_part.2 = (bf16[4096,384]{1,0:T(8,128)(2,1)}, bf16[512,384]{1,0:T(8,128)(2,1)}) custom-call(s32[64,64]{1,0:T(8,128)S(1)} %get-tuple-element.24.columns_ref, bf16[512,384]{1,0:T(8,128)(2,1)S(1)} %bitcast.13, bf16[192,192]{1,0:T(8,128)(2,1)S(1)} %get-tuple-element.26.order_ref, f32[64]{0:T(128)} %stiff_coef_hbm.7, f32[64]{0:T(128)} %mass_coef_hbm.7, ...), custom_call_target="tpu_custom_call" | custom-call | flops 4831838208 | bytes 6291456 | tf_op jit(solution)/shard_map/free_part/pallas_call | solution.py:388
  30.2 2.8 %all-to-all-start.1 = ((bf16[32,16,384]{2,1,0:T(8,128)(2,1)}), bf16[32,16,384]{2,1,0:T(8,128)(2,1)S(1)}, u32[]{:S(2)}, u32[]{:S(2)}) async-start(bf16[32,16,384]{2,1,0:T(8,128)(2,1)} %bitcast.17), calls=%async_computation.1 | async-start | bytes 786432 | tf_op jit(solution)/shard_map/all_to_all | solution.py:368
  33.0 6.7 %dam_update.2.dam_hbm.after_hbm = bf16[512,384]{1,0:T(8,128)(2,1)} custom-call(s32[64,64]{1,0:T(8,128)} %dam_conn_hbm.7, bf16[4096,384]{1,0:T(8,128)(2,1)} %get-tuple-element.28.free_force_hbm, bf16[4096,384]{1,0:T(8,128)(2,1)} %get-tuple-element.29.dam_force_hbm, bf16[512,384]{1,0:T(8,128)(2,1)} %dam_hbm.3, f32[1,512]{1,0:T(1,128)} %bitcast.19), custom_call_target="tpu_custom_call" | custom-call | flops 1610612736 | bytes 6291456 | tf_op jit(solution)/shard_map/dam_update/pallas_call | solution.py:388
  39.7 6.6 %all-to-all-done.1 = bf16[32,16,384]{2,1,0:T(8,128)(2,1)S(1)} async-done(((bf16[32,16,384]{2,1,0:T(8,128)(2,1)}), bf16[32,16,384]{2,1,0:T(8,128)(2,1)S(1)}, u32[]{:S(2)}, u32[]{:S(2)}) %all-to-all-start.1) | async-done | bytes 393248 | tf_op jit(solution)/shard_map/all_to_all | solution.py:368
  46.3 1.3 %turn.1 = (bf16[128,384]{1,0:T(8,128)(2,1)S(1)}, bf16[512,384]{1,0:T(8,128)(2,1)}) custom-call(bf16[512,128]{1,0:T(8,128)(2,1)S(1)} %get-tuple-element.23.place_ref, bf16[512,384]{1,0:T(8,128)(2,1)S(1)} %bitcast.12, bf16[128,384]{1,0:T(8,128)(2,1)S(1)} %get-tuple-element.32.history_ref, f32[128,128]{1,0:T(8,128)S(1)} %get-tuple-element.33.column_ref, ...), custom_call_target="tpu_custom_call" | custom-call | tf_op jit(solution)/shard_map/turn/pallas_call | solution.py:388
  47.6 2.6 %all-to-all-start.2 = ((bf16[32,16,384]{2,1,0:T(8,128)(2,1)}), bf16[32,16,384]{2,1,0:T(8,128)(2,1)S(1)}, u32[]{:S(2)}, u32[]{:S(2)}) async-start(bf16[32,16,384]{2,1,0:T(8,128)(2,1)} %bitcast.18), calls=%async_computation.2 | async-start | bytes 786432 | tf_op jit(solution)/shard_map/all_to_all | solution.py:368
  50.2 7.9 %dam_part.3 = (f32[384,512]{1,0:T(8,128)}, bf16[192,192]{1,0:T(8,128)(2,1)S(1)}, s32[64,64]{1,0:T(8,128)S(1)}, bf16[4096,384]{1,0:T(8,128)(2,1)}) custom-call(s32[64,64]{1,0:T(8,128)} %free_hbm.3, s32[64,64]{1,0:T(8,128)} %dam_conn_hbm.7, bf16[512,384]{1,0:T(8,128)(2,1)} %dam_update.2.dam_hbm.after_hbm, bf16[192,192]{1,0:T(8,128)(2,1)} %stiff_hbm.3, ...), custom_call_target="tpu_custom_call" | custom-call | flops 4831838208 | bytes 6291456 | tf_op jit(solution)/shard_map/dam_part/pallas_call | solution.py:388
  58.1 5.7 %all-to-all-done.2 = bf16[32,16,384]{2,1,0:T(8,128)(2,1)S(1)} async-done(((bf16[32,16,384]{2,1,0:T(8,128)(2,1)}), bf16[32,16,384]{2,1,0:T(8,128)(2,1)S(1)}, u32[]{:S(2)}, u32[]{:S(2)}) %all-to-all-start.2) | async-done | bytes 393248 | tf_op jit(solution)/shard_map/all_to_all | solution.py:368
  63.7 6.7 %free_part.3 = (bf16[4096,384]{1,0:T(8,128)(2,1)}, bf16[512,384]{1,0:T(8,128)(2,1)}) custom-call(s32[64,64]{1,0:T(8,128)S(1)} %get-tuple-element.30.columns_ref, bf16[512,384]{1,0:T(8,128)(2,1)S(1)} %bitcast.14, bf16[192,192]{1,0:T(8,128)(2,1)S(1)} %get-tuple-element.35.order_ref, f32[64]{0:T(128)} %stiff_coef_hbm.7, f32[64]{0:T(128)} %mass_coef_hbm.7, ...), custom_call_target="tpu_custom_call" | custom-call | flops 4831838208 | bytes 6291456 | tf_op jit(solution)/shard_map/free_part/pallas_call | solution.py:388
  70.5 2.8 %all-to-all-start.3 = ((bf16[32,16,384]{2,1,0:T(8,128)(2,1)}), bf16[32,16,384]{2,1,0:T(8,128)(2,1)S(1)}, u32[]{:S(2)}, u32[]{:S(2)}) async-start(bf16[32,16,384]{2,1,0:T(8,128)(2,1)} %bitcast.15), calls=%async_computation.3 | async-start | bytes 786432 | tf_op jit(solution)/shard_map/all_to_all | solution.py:368
  73.3 6.7 %dam_update.3.after_hbm = bf16[512,384]{1,0:T(8,128)(2,1)} custom-call(s32[64,64]{1,0:T(8,128)} %dam_conn_hbm.7, bf16[4096,384]{1,0:T(8,128)(2,1)} %get-tuple-element.39.free_force_hbm, bf16[4096,384]{1,0:T(8,128)(2,1)} %get-tuple-element.40.dam_force_hbm, bf16[512,384]{1,0:T(8,128)(2,1)} %dam_update.2.dam_hbm.after_hbm, f32[1,512]{1,0:T(1,128)} %bitcast.20), custom_call_target="tpu_custom_call" | custom-call | flops 1610612736 | bytes 6291456 | tf_op jit(solution)/shard_map/dam_update/pallas_call | solution.py:388
  80.0 6.6 %all-to-all-done.3 = bf16[32,16,384]{2,1,0:T(8,128)(2,1)S(1)} async-done(((bf16[32,16,384]{2,1,0:T(8,128)(2,1)}), bf16[32,16,384]{2,1,0:T(8,128)(2,1)S(1)}, u32[]{:S(2)}, u32[]{:S(2)}) %all-to-all-start.3) | async-done | bytes 393248 | tf_op jit(solution)/shard_map/all_to_all | solution.py:368
  86.6 1.0 %last.1 = (bf16[128,384]{1,0:T(8,128)(2,1)}, f32[128,384]{1,0:T(8,128)}) custom-call(bf16[512,128]{1,0:T(8,128)(2,1)S(1)} %get-tuple-element.23.place_ref, bf16[512,384]{1,0:T(8,128)(2,1)S(1)} %bitcast.11, bf16[128,384]{1,0:T(8,128)(2,1)S(1)} %get-tuple-element.38.history_ref, f32[128,128]{1,0:T(8,128)S(1)} %get-tuple-element.33.column_ref, ...), custom_call_target="tpu_custom_call" | custom-call | tf_op jit(solution)/shard_map/last/pallas_call | solution.py:388
Async XLA Ops:
  2.6 20.8 %all-to-all-start = ((bf16[32,16,384]{2,1,0:T(8,128)(2,1)}), bf16[32,16,384]{2,1,0:T(8,128)(2,1)S(1)}, u32[]{:S(2)}, u32[]{:S(2)}) async-start(bf16[32,16,384]{2,1,0:T(8,128)(2,1)} %bitcast.16), calls=%async_computation | async-start | bytes 786432 | tf_op jit(solution)/shard_map/all_to_all | solution.py:368
  30.2 16.2 %all-to-all-start.1 = ((bf16[32,16,384]{2,1,0:T(8,128)(2,1)}), bf16[32,16,384]{2,1,0:T(8,128)(2,1)S(1)}, u32[]{:S(2)}, u32[]{:S(2)}) async-start(bf16[32,16,384]{2,1,0:T(8,128)(2,1)} %bitcast.17), calls=%async_computation.1 | async-start | bytes 786432 | tf_op jit(solution)/shard_map/all_to_all | solution.py:368
  47.6 16.2 %all-to-all-start.2 = ((bf16[32,16,384]{2,1,0:T(8,128)(2,1)}), bf16[32,16,384]{2,1,0:T(8,128)(2,1)S(1)}, u32[]{:S(2)}, u32[]{:S(2)}) async-start(bf16[32,16,384]{2,1,0:T(8,128)(2,1)} %bitcast.18), calls=%async_computation.2 | async-start | bytes 786432 | tf_op jit(solution)/shard_map/all_to_all | solution.py:368
  70.5 16.2 %all-to-all-start.3 = ((bf16[32,16,384]{2,1,0:T(8,128)(2,1)}), bf16[32,16,384]{2,1,0:T(8,128)(2,1)S(1)}, u32[]{:S(2)}, u32[]{:S(2)}) async-start(bf16[32,16,384]{2,1,0:T(8,128)(2,1)} %bitcast.15), calls=%async_computation.3 | async-start | bytes 786432 | tf_op jit(solution)/shard_map/all_to_all | solution.py:368

commit v5 on v4

--- a/solution.py
+++ b/solution.py
@@ -5,9 +5,11 @@
 from jax import lax
 from jax.experimental import pallas as pl
 from jax.experimental.pallas import tpu as pltpu
+from jax.sharding import Mesh
 from jax.sharding import PartitionSpec as P
 
 ROUNDS = 2
+AXES = ("reg_high", "dam", "reg_low")
 GROUP = 8
 VMEM_BYTES = 28 * 1024 * 1024
 BF16 = jnp.bfloat16
@@ -45,8 +47,16 @@
     return jnp.sum(jnp.where(down == across, row, jnp.zeros_like(row)), axis=1, keepdims=True)
 
 
+def block_of(device, dam):
+    high = device // (2 * dam)
+    rest = device - high * (2 * dam)
+    low = rest // dam
+    return (high * dam + rest - low * dam) * 2 + low
+
+
 def pack_kernel(
     capacity,
+    dam,
     routes_hbm,
     history_hbm,
     step_hbm,
@@ -73,7 +83,7 @@
     for own in (row0, row1):
         same = jnp.where(col0 == own, 1, 0) + jnp.where(col1 == own, 1, 0)
         slot = jnp.sum(jnp.where(down < across, same, 0), axis=0, keepdims=True)
-        hits.append(own * capacity + slot == numbers)
+        hits.append(block_of(own, dam) * capacity + slot == numbers)
     place = mask_to_bf16(hits[0] | hits[1])
     place_ref[...] = place
     finish(inward[1:])
@@ -205,6 +215,8 @@
 
 
 def dam_part_kernel(
+    capacity,
+    dam,
     free_hbm,
     dam_conn_hbm,
     dam_hbm,
@@ -241,7 +253,10 @@
     )
     finish(inward)
     order_ref[...] = by_component(stiff_ref[...])
-    free_columns, dam_columns = free_ref[...].T, dam_conn_ref[...].T
+    dam_columns = dam_conn_ref[...].T
+    free_columns = free_ref[...].T
+    sender_of = free_columns // capacity
+    free_columns = free_columns + (block_of(sender_of, dam) - sender_of) * capacity
     columns_ref[...] = free_columns
     groups = force_sems.shape[0]
     held = (held0, held1)
@@ -365,7 +380,7 @@
 def exchange(rows, devices, capacity):
     width = rows.shape[1]
     shaped = rows.reshape(devices, capacity, width)
-    arrived = lax.all_to_all(shaped, ("reg", "dam"), split_axis=0, concat_axis=0, tiled=True)
+    arrived = lax.all_to_all(shaped, AXES, split_axis=0, concat_axis=0, tiled=True)
     return arrived.reshape(devices * capacity, width)
 
 
@@ -407,7 +422,7 @@
     reg_step,
     dam_step,
 ):
-    devices = lax.axis_size(("reg", "dam"))
+    devices = lax.axis_size(AXES)
     row_count, width = history.shape
     capacity = 4 * row_count // devices
     slots = devices * capacity
@@ -437,7 +452,7 @@
     product = 2 * all_pairs * slots * width
 
     pack = kernel(
-        functools.partial(pack_kernel, capacity),
+        functools.partial(pack_kernel, capacity, lax.axis_size("dam")),
         "pack",
         "hhh",
         [("h", *slots_type), ("v", *place_type), ("v", *rows_type), ("v", *column_type)],
@@ -458,7 +473,7 @@
         [vmem(*rows_type), vmem(*pulled_type), dma((2,))],
     )
     dam_part = kernel(
-        dam_part_kernel,
+        functools.partial(dam_part_kernel, capacity, lax.axis_size("dam")),
         "dam_part",
         "hhhhhh",
         [("h", *back_type), ("v", *stiff_type), ("v", (nodes, elements), I32), ("h", *forces_type)],
@@ -511,9 +526,12 @@
 
 
 def solution(mesh):
-    rows = P(("reg", "dam"), None)
-    flat = P(("reg", "dam"))
+    reg, dam = mesh.devices.shape
+    split = Mesh(mesh.devices.reshape(reg // 2, 2, dam), ("reg_high", "reg_low", "dam"))
+    axes = ("reg_high", "reg_low", "dam")
+    rows = P(axes, None)
+    flat = P(axes)
     in_specs = (rows, rows, rows, rows, rows, P(), flat, flat, flat, flat)
     return jax.shard_map(
-        shards, mesh=mesh, in_specs=in_specs, out_specs=(rows, rows, rows), check_vma=False
-    )
+        shards, mesh=split, in_specs=in_specs, out_specs=(rows, rows, rows), check_vma=False
+    )

time: 88.3 us -> 86.5 us (0.980)
  waiting for transfers between devices: 24.6 us -> 22.9 us
    all_to_all x4, waiting for transfers between devices: 24.6 us -> 22.9 us  [exchange(): lax.all_to_all(shaped, AXES, split_axis=0, concat_axis=0, tiled=True)]
  transfers between devices with their start and end apart: 4 -> 4, of which waited for: 4 -> 4; matrix products, arithmetic and copies ran while one was open for 0% -> 0% of each run, Pallas kernels for 33% -> 34%
where the time goes in v5:
time: 86.5 us; the launch traced here: 86 us
  Pallas kernels  46.7 us (54%)
  waiting for transfers between devices  22.9 us (26%)
  starting transfers between devices  15.5 us (18%)
  between operations  0.91 us (1%)
    pallas_call x9, Pallas kernels, run(): call(*[x if letter == 'a' else pltpu.with_memory_space_constraint(x, spac...  46.7 us
    all_to_all x4, waiting for transfers between devices, exchange(): lax.all_to_all(shaped, AXES, split_axis=0, concat_axis=0, tiled=True)  22.9 us
    all_to_all x4, starting transfers between devices, exchange(): lax.all_to_all(shaped, AXES, split_axis=0, concat_axis=0, tiled=True)  15.5 us
  transfers between devices with their start and end apart: 4, of which 4 were waited for; matrix products, arithmetic and copies ran while one was open for 0% of the time, Pallas kernels for 34%

profile of v5, /device:TPU:0, one launch (start us, length us, event | category | flops | bytes accessed | tf_op | source)
XLA Modules:
  0.0 86.0 jit_solution(77243096751920957)
XLA Ops:
  0.6 1.9 %pack.1 = (bf16[512,384]{1,0:T(8,128)(2,1)}, bf16[512,128]{1,0:T(8,128)(2,1)S(1)}, bf16[128,384]{1,0:T(8,128)(2,1)S(1)}, f32[128,128]{1,0:T(8,128)S(1)}) custom-call(s32[2,128]{1,0:T(2,128)} %bitcast.21, bf16[128,384]{1,0:T(8,128)(2,1)} %history_hbm.1, f32[1,128]{1,0:T(1,128)} %bitcast.22), custom_call_target="tpu_custom_call" | custom-call | tf_op jit(solution)/shard_map/pack/pallas_call | solution.py:403
  2.6 7.3 %all-to-all-start = ((bf16[32,16,384]{2,1,0:T(8,128)(2,1)}), bf16[32,16,384]{2,1,0:T(8,128)(2,1)S(1)}, u32[]{:S(2)}, u32[]{:S(2)}) async-start(bf16[32,16,384]{2,1,0:T(8,128)(2,1)} %bitcast.16), calls=%async_computation | async-start | bytes 786432 | tf_op jit(solution)/shard_map/all_to_all | solution.py:383
  9.9 7.8 %dam_part.2 = (f32[384,512]{1,0:T(8,128)}, bf16[192,192]{1,0:T(8,128)(2,1)S(1)}, s32[64,64]{1,0:T(8,128)S(1)}, bf16[4096,384]{1,0:T(8,128)(2,1)}) custom-call(s32[64,64]{1,0:T(8,128)} %free_hbm.3, s32[64,64]{1,0:T(8,128)} %dam_conn_hbm.7, bf16[512,384]{1,0:T(8,128)(2,1)} %dam_hbm.3, bf16[192,192]{1,0:T(8,128)(2,1)} %stiff_hbm.3, f32[64]{0:T(128)} %stiff_coef_hbm.7, ...), custom_call_target="tpu_custom_call" | custom-call | flops 4831838208 | bytes 6291456 | tf_op jit(solution)/shard_map/dam_part/pallas_call | solution.py:403
  17.7 5.3 %all-to-all-done = bf16[32,16,384]{2,1,0:T(8,128)(2,1)S(1)} async-done(((bf16[32,16,384]{2,1,0:T(8,128)(2,1)}), bf16[32,16,384]{2,1,0:T(8,128)(2,1)S(1)}, u32[]{:S(2)}, u32[]{:S(2)}) %all-to-all-start) | async-done | bytes 393248 | tf_op jit(solution)/shard_map/all_to_all | solution.py:383
  23.0 6.7 %free_part.2 = (bf16[4096,384]{1,0:T(8,128)(2,1)}, bf16[512,384]{1,0:T(8,128)(2,1)}) custom-call(s32[64,64]{1,0:T(8,128)S(1)} %get-tuple-element.24.columns_ref, bf16[512,384]{1,0:T(8,128)(2,1)S(1)} %bitcast.13, bf16[192,192]{1,0:T(8,128)(2,1)S(1)} %get-tuple-element.26.order_ref, f32[64]{0:T(128)} %stiff_coef_hbm.7, f32[64]{0:T(128)} %mass_coef_hbm.7, ...), custom_call_target="tpu_custom_call" | custom-call | flops 4831838208 | bytes 6291456 | tf_op jit(solution)/shard_map/free_part/pallas_call | solution.py:403
  29.7 2.8 %all-to-all-start.1 = ((bf16[32,16,384]{2,1,0:T(8,128)(2,1)}), bf16[32,16,384]{2,1,0:T(8,128)(2,1)S(1)}, u32[]{:S(2)}, u32[]{:S(2)}) async-start(bf16[32,16,384]{2,1,0:T(8,128)(2,1)} %bitcast.17), calls=%async_computation.1 | async-start | bytes 786432 | tf_op jit(solution)/shard_map/all_to_all | solution.py:383
  32.5 6.7 %dam_update.2.dam_hbm.after_hbm = bf16[512,384]{1,0:T(8,128)(2,1)} custom-call(s32[64,64]{1,0:T(8,128)} %dam_conn_hbm.7, bf16[4096,384]{1,0:T(8,128)(2,1)} %get-tuple-element.28.free_force_hbm, bf16[4096,384]{1,0:T(8,128)(2,1)} %get-tuple-element.29.dam_force_hbm, bf16[512,384]{1,0:T(8,128)(2,1)} %dam_hbm.3, f32[1,512]{1,0:T(1,128)} %bitcast.19), custom_call_target="tpu_custom_call" | custom-call | flops 1610612736 | bytes 6291456 | tf_op jit(solution)/shard_map/dam_update/pallas_call | solution.py:403
  39.2 6.2 %all-to-all-done.1 = bf16[32,16,384]{2,1,0:T(8,128)(2,1)S(1)} async-done(((bf16[32,16,384]{2,1,0:T(8,128)(2,1)}), bf16[32,16,384]{2,1,0:T(8,128)(2,1)S(1)}, u32[]{:S(2)}, u32[]{:S(2)}) %all-to-all-start.1) | async-done | bytes 393248 | tf_op jit(solution)/shard_map/all_to_all | solution.py:383
  45.4 1.3 %turn.1 = (bf16[128,384]{1,0:T(8,128)(2,1)S(1)}, bf16[512,384]{1,0:T(8,128)(2,1)}) custom-call(bf16[512,128]{1,0:T(8,128)(2,1)S(1)} %get-tuple-element.23.place_ref, bf16[512,384]{1,0:T(8,128)(2,1)S(1)} %bitcast.12, bf16[128,384]{1,0:T(8,128)(2,1)S(1)} %get-tuple-element.32.history_ref, f32[128,128]{1,0:T(8,128)S(1)} %get-tuple-element.33.column_ref, ...), custom_call_target="tpu_custom_call" | custom-call | tf_op jit(solution)/shard_map/turn/pallas_call | solution.py:403
  46.7 2.6 %all-to-all-start.2 = ((bf16[32,16,384]{2,1,0:T(8,128)(2,1)}), bf16[32,16,384]{2,1,0:T(8,128)(2,1)S(1)}, u32[]{:S(2)}, u32[]{:S(2)}) async-start(bf16[32,16,384]{2,1,0:T(8,128)(2,1)} %bitcast.18), calls=%async_computation.2 | async-start | bytes 786432 | tf_op jit(solution)/shard_map/all_to_all | solution.py:383
  49.3 7.8 %dam_part.3 = (f32[384,512]{1,0:T(8,128)}, bf16[192,192]{1,0:T(8,128)(2,1)S(1)}, s32[64,64]{1,0:T(8,128)S(1)}, bf16[4096,384]{1,0:T(8,128)(2,1)}) custom-call(s32[64,64]{1,0:T(8,128)} %free_hbm.3, s32[64,64]{1,0:T(8,128)} %dam_conn_hbm.7, bf16[512,384]{1,0:T(8,128)(2,1)} %dam_update.2.dam_hbm.after_hbm, bf16[192,192]{1,0:T(8,128)(2,1)} %stiff_hbm.3, ...), custom_call_target="tpu_custom_call" | custom-call | flops 4831838208 | bytes 6291456 | tf_op jit(solution)/shard_map/dam_part/pallas_call | solution.py:403
  57.1 5.3 %all-to-all-done.2 = bf16[32,16,384]{2,1,0:T(8,128)(2,1)S(1)} async-done(((bf16[32,16,384]{2,1,0:T(8,128)(2,1)}), bf16[32,16,384]{2,1,0:T(8,128)(2,1)S(1)}, u32[]{:S(2)}, u32[]{:S(2)}) %all-to-all-start.2) | async-done | bytes 393248 | tf_op jit(solution)/shard_map/all_to_all | solution.py:383
  62.4 6.7 %free_part.3 = (bf16[4096,384]{1,0:T(8,128)(2,1)}, bf16[512,384]{1,0:T(8,128)(2,1)}) custom-call(s32[64,64]{1,0:T(8,128)S(1)} %get-tuple-element.30.columns_ref, bf16[512,384]{1,0:T(8,128)(2,1)S(1)} %bitcast.14, bf16[192,192]{1,0:T(8,128)(2,1)S(1)} %get-tuple-element.35.order_ref, f32[64]{0:T(128)} %stiff_coef_hbm.7, f32[64]{0:T(128)} %mass_coef_hbm.7, ...), custom_call_target="tpu_custom_call" | custom-call | flops 4831838208 | bytes 6291456 | tf_op jit(solution)/shard_map/free_part/pallas_call | solution.py:403
  69.1 2.8 %all-to-all-start.3 = ((bf16[32,16,384]{2,1,0:T(8,128)(2,1)}), bf16[32,16,384]{2,1,0:T(8,128)(2,1)S(1)}, u32[]{:S(2)}, u32[]{:S(2)}) async-start(bf16[32,16,384]{2,1,0:T(8,128)(2,1)} %bitcast.15), calls=%async_computation.3 | async-start | bytes 786432 | tf_op jit(solution)/shard_map/all_to_all | solution.py:383
  72.0 6.7 %dam_update.3.after_hbm = bf16[512,384]{1,0:T(8,128)(2,1)} custom-call(s32[64,64]{1,0:T(8,128)} %dam_conn_hbm.7, bf16[4096,384]{1,0:T(8,128)(2,1)} %get-tuple-element.39.free_force_hbm, bf16[4096,384]{1,0:T(8,128)(2,1)} %get-tuple-element.40.dam_force_hbm, bf16[512,384]{1,0:T(8,128)(2,1)} %dam_update.2.dam_hbm.after_hbm, f32[1,512]{1,0:T(1,128)} %bitcast.20), custom_call_target="tpu_custom_call" | custom-call | flops 1610612736 | bytes 6291456 | tf_op jit(solution)/shard_map/dam_update/pallas_call | solution.py:403
  78.7 6.1 %all-to-all-done.3 = bf16[32,16,384]{2,1,0:T(8,128)(2,1)S(1)} async-done(((bf16[32,16,384]{2,1,0:T(8,128)(2,1)}), bf16[32,16,384]{2,1,0:T(8,128)(2,1)S(1)}, u32[]{:S(2)}, u32[]{:S(2)}) %all-to-all-start.3) | async-done | bytes 393248 | tf_op jit(solution)/shard_map/all_to_all | solution.py:383
  84.8 1.0 %last.1 = (bf16[128,384]{1,0:T(8,128)(2,1)}, f32[128,384]{1,0:T(8,128)}) custom-call(bf16[512,128]{1,0:T(8,128)(2,1)S(1)} %get-tuple-element.23.place_ref, bf16[512,384]{1,0:T(8,128)(2,1)S(1)} %bitcast.11, bf16[128,384]{1,0:T(8,128)(2,1)S(1)} %get-tuple-element.38.history_ref, f32[128,128]{1,0:T(8,128)S(1)} %get-tuple-element.33.column_ref, ...), custom_call_target="tpu_custom_call" | custom-call | tf_op jit(solution)/shard_map/last/pallas_call | solution.py:403
Async XLA Ops:
  2.6 20.4 %all-to-all-start = ((bf16[32,16,384]{2,1,0:T(8,128)(2,1)}), bf16[32,16,384]{2,1,0:T(8,128)(2,1)S(1)}, u32[]{:S(2)}, u32[]{:S(2)}) async-start(bf16[32,16,384]{2,1,0:T(8,128)(2,1)} %bitcast.16), calls=%async_computation | async-start | bytes 786432 | tf_op jit(solution)/shard_map/all_to_all | solution.py:383
  29.7 15.7 %all-to-all-start.1 = ((bf16[32,16,384]{2,1,0:T(8,128)(2,1)}), bf16[32,16,384]{2,1,0:T(8,128)(2,1)S(1)}, u32[]{:S(2)}, u32[]{:S(2)}) async-start(bf16[32,16,384]{2,1,0:T(8,128)(2,1)} %bitcast.17), calls=%async_computation.1 | async-start | bytes 786432 | tf_op jit(solution)/shard_map/all_to_all | solution.py:383
  46.7 15.7 %all-to-all-start.2 = ((bf16[32,16,384]{2,1,0:T(8,128)(2,1)}), bf16[32,16,384]{2,1,0:T(8,128)(2,1)S(1)}, u32[]{:S(2)}, u32[]{:S(2)}) async-start(bf16[32,16,384]{2,1,0:T(8,128)(2,1)} %bitcast.18), calls=%async_computation.2 | async-start | bytes 786432 | tf_op jit(solution)/shard_map/all_to_all | solution.py:383
  69.1 15.7 %all-to-all-start.3 = ((bf16[32,16,384]{2,1,0:T(8,128)(2,1)}), bf16[32,16,384]{2,1,0:T(8,128)(2,1)S(1)}, u32[]{:S(2)}, u32[]{:S(2)}) async-start(bf16[32,16,384]{2,1,0:T(8,128)(2,1)} %bitcast.15), calls=%async_computation.3 | async-start | bytes 786432 | tf_op jit(solution)/shard_map/all_to_all | solution.py:383

commit v6 on v5

--- a/solution.py
+++ b/solution.py
@@ -10,7 +10,8 @@
 
 ROUNDS = 2
 AXES = ("reg_high", "dam", "reg_low")
-GROUP = 8
+GROUP = 16
+LANES = 128
 VMEM_BYTES = 28 * 1024 * 1024
 BF16 = jnp.bfloat16
 F32 = jnp.float32
@@ -141,9 +142,16 @@
     lanes = lax.broadcasted_iota(jnp.int32, (nodes, width), 1).astype(jnp.int16)
     parts = []
     for e in range(first, first + GROUP):
-        own = jnp.broadcast_to(columns[:, e : e + 1], (nodes, width)).astype(jnp.int16)
+        own = jnp.broadcast_to(columns[:, e : e + 1], (nodes, LANES)).astype(jnp.int16)
+        own = jnp.concatenate([own] * (width // LANES), axis=1)
         parts.append(jnp.where(own == lanes, jnp.ones((), BF16), jnp.zeros((), BF16)))
     return jnp.concatenate(parts, axis=0)
+
+
+def select_spread(spread, width):
+    own = jnp.concatenate([spread] * (width // LANES), axis=1)
+    lanes = lax.broadcasted_iota(jnp.int32, own.shape, 1).astype(jnp.int16)
+    return jnp.where(own == lanes, jnp.ones((), BF16), jnp.zeros((), BF16))
 
 
 def element_forces(u, stiff, stiff_coef_ref, mass_coef_ref, first):
@@ -257,7 +265,10 @@
     free_columns = free_ref[...].T
     sender_of = free_columns // capacity
     free_columns = free_columns + (block_of(sender_of, dam) - sender_of) * capacity
-    columns_ref[...] = free_columns
+    nodes = free_columns.shape[0]
+    for e in range(free_columns.shape[1]):
+        own = jnp.broadcast_to(free_columns[:, e : e + 1], (nodes, LANES))
+        columns_ref[e * nodes : (e + 1) * nodes, :] = own.astype(jnp.int16)
     groups = force_sems.shape[0]
     held = (held0, held1)
     sender = Sender(force_ref, force_hbm, force_sems)
@@ -268,7 +279,7 @@
 
     def add(group):
         sender.start(group)
-        select = select_rows(free_columns, group * GROUP, back_ref.shape[1])
+        select = select_spread(chunks_of(columns_ref, groups)[group][...], back_ref.shape[1])
         part = dot_first(sender.chunks[group][...], select)
         back_ref[...] = part if group == 0 else back_ref[...] + part
 
@@ -307,14 +318,13 @@
         ],
         sems,
     )
-    columns = columns_ref[...]
     groups = force_sems.shape[0]
     made_chunks = chunks_of(made, groups)
     held = (held0, held1)
     sender = Sender(force_ref, force_hbm, force_sems)
 
     def gather(group):
-        select = select_rows(columns, group * GROUP, received_ref.shape[0])
+        select = select_spread(chunks_of(columns_ref, groups)[group][...], received_ref.shape[0])
         made_chunks[group][...] = select
         held[group % 2][...] = dot(select, received_ref[...]).astype(BF16)
         if group == 0:
@@ -476,7 +486,7 @@
         functools.partial(dam_part_kernel, capacity, lax.axis_size("dam")),
         "dam_part",
         "hhhhhh",
-        [("h", *back_type), ("v", *stiff_type), ("v", (nodes, elements), I32), ("h", *forces_type)],
+        [("h", *back_type), ("v", *stiff_type), ("v", (all_pairs, LANES), jnp.int16), ("h", *forces_type)],
         [conn, conn, vmem(*dam_type), stiff, *coefs, vmem(*back_type), vmem(*forces_type)]
         + [*held, dma((6,)), dma((groups,))],
         flops=3 * product,

time: 86.5 us -> 85.7 us (level)
  Pallas kernels: 46.7 us -> 44.1 us
  waiting for transfers between devices: 22.9 us -> 24.9 us
    pallas_call x9, Pallas kernels: 46.7 us -> 44.1 us  [run(): call(*[x if letter == 'a' else pltpu.with_memory_space_constraint(x, spac...]
    all_to_all x4, waiting for transfers between devices: 22.9 us -> 24.9 us  [exchange(): lax.all_to_all(shaped, AXES, split_axis=0, concat_axis=0, tiled=True)]
  transfers between devices with their start and end apart: 4 -> 4, of which waited for: 4 -> 4; matrix products, arithmetic and copies ran while one was open for 0% -> 0% of each run, Pallas kernels for 34% -> 32%
where the time goes in v6:
time: 85.7 us; the launch traced here: 85.2 us
  Pallas kernels  44.1 us (51%)
  waiting for transfers between devices  24.9 us (29%)
  starting transfers between devices  15.3 us (18%)
  between operations  0.89 us (1%)
    pallas_call x9, Pallas kernels, run(): call(*[x if letter == 'a' else pltpu.with_memory_space_constraint(x, spac...  44.1 us
    all_to_all x4, waiting for transfers between devices, exchange(): lax.all_to_all(shaped, AXES, split_axis=0, concat_axis=0, tiled=True)  24.9 us
    all_to_all x4, starting transfers between devices, exchange(): lax.all_to_all(shaped, AXES, split_axis=0, concat_axis=0, tiled=True)  15.3 us
  transfers between devices with their start and end apart: 4, of which 4 were waited for; matrix products, arithmetic and copies ran while one was open for 0% of the time, Pallas kernels for 32%

profile of v6, /device:TPU:0, one launch (start us, length us, event | category | flops | bytes accessed | tf_op | source)
XLA Modules:
  0.0 85.2 jit_solution(12941451663511971010)
XLA Ops:
  0.6 1.9 %pack.1 = (bf16[512,384]{1,0:T(8,128)(2,1)}, bf16[512,128]{1,0:T(8,128)(2,1)S(1)}, bf16[128,384]{1,0:T(8,128)(2,1)S(1)}, f32[128,128]{1,0:T(8,128)S(1)}) custom-call(s32[2,128]{1,0:T(2,128)} %bitcast.21, bf16[128,384]{1,0:T(8,128)(2,1)} %history_hbm.1, f32[1,128]{1,0:T(1,128)} %bitcast.22), custom_call_target="tpu_custom_call" | custom-call | tf_op jit(solution)/shard_map/pack/pallas_call | solution.py:413
  2.6 7.3 %all-to-all-start = ((bf16[32,16,384]{2,1,0:T(8,128)(2,1)}), bf16[32,16,384]{2,1,0:T(8,128)(2,1)S(1)}, u32[]{:S(2)}, u32[]{:S(2)}) async-start(bf16[32,16,384]{2,1,0:T(8,128)(2,1)} %bitcast.16), calls=%async_computation | async-start | bytes 786432 | tf_op jit(solution)/shard_map/all_to_all | solution.py:393
  9.9 7.8 %dam_part.2 = (f32[384,512]{1,0:T(8,128)}, bf16[192,192]{1,0:T(8,128)(2,1)S(1)}, s16[4096,128]{1,0:T(8,128)(2,1)S(1)}, bf16[4096,384]{1,0:T(8,128)(2,1)}) custom-call(s32[64,64]{1,0:T(8,128)} %free_hbm.3, s32[64,64]{1,0:T(8,128)} %dam_conn_hbm.7, bf16[512,384]{1,0:T(8,128)(2,1)} %dam_hbm.3, bf16[192,192]{1,0:T(8,128)(2,1)} %stiff_hbm.3, f32[64]{0:T(128)} %stiff_coef_hbm.7, ...), custom_call_target="tpu_custom_call" | custom-call | flops 4831838208 | bytes 6291456 | tf_op jit(solution)/shard_map/dam_part/pallas_call | solution.py:413
  17.7 5.3 %all-to-all-done = bf16[32,16,384]{2,1,0:T(8,128)(2,1)S(1)} async-done(((bf16[32,16,384]{2,1,0:T(8,128)(2,1)}), bf16[32,16,384]{2,1,0:T(8,128)(2,1)S(1)}, u32[]{:S(2)}, u32[]{:S(2)}) %all-to-all-start) | async-done | bytes 393248 | tf_op jit(solution)/shard_map/all_to_all | solution.py:393
  23.0 6.3 %free_part.2 = (bf16[4096,384]{1,0:T(8,128)(2,1)}, bf16[512,384]{1,0:T(8,128)(2,1)}) custom-call(s16[4096,128]{1,0:T(8,128)(2,1)S(1)} %get-tuple-element.24.columns_ref, bf16[512,384]{1,0:T(8,128)(2,1)S(1)} %bitcast.13, bf16[192,192]{1,0:T(8,128)(2,1)S(1)} %get-tuple-element.26.order_ref, f32[64]{0:T(128)} %stiff_coef_hbm.7, f32[64]{0:T(128)} %mass_coef_hbm.7, ...), custom_call_target="tpu_custom_call" | custom-call | flops 4831838208 | bytes 6291456 | tf_op jit(solution)/shard_map/free_part/pallas_call | solution.py:413
  29.3 2.8 %all-to-all-start.1 = ((bf16[32,16,384]{2,1,0:T(8,128)(2,1)}), bf16[32,16,384]{2,1,0:T(8,128)(2,1)S(1)}, u32[]{:S(2)}, u32[]{:S(2)}) async-start(bf16[32,16,384]{2,1,0:T(8,128)(2,1)} %bitcast.17), calls=%async_computation.1 | async-start | bytes 786432 | tf_op jit(solution)/shard_map/all_to_all | solution.py:393
  32.1 5.8 %dam_update.2.dam_hbm.after_hbm = bf16[512,384]{1,0:T(8,128)(2,1)} custom-call(s32[64,64]{1,0:T(8,128)} %dam_conn_hbm.7, bf16[4096,384]{1,0:T(8,128)(2,1)} %get-tuple-element.28.free_force_hbm, bf16[4096,384]{1,0:T(8,128)(2,1)} %get-tuple-element.29.dam_force_hbm, bf16[512,384]{1,0:T(8,128)(2,1)} %dam_hbm.3, f32[1,512]{1,0:T(1,128)} %bitcast.19), custom_call_target="tpu_custom_call" | custom-call | flops 1610612736 | bytes 6291456 | tf_op jit(solution)/shard_map/dam_update/pallas_call | solution.py:413
  38.0 7.1 %all-to-all-done.1 = bf16[32,16,384]{2,1,0:T(8,128)(2,1)S(1)} async-done(((bf16[32,16,384]{2,1,0:T(8,128)(2,1)}), bf16[32,16,384]{2,1,0:T(8,128)(2,1)S(1)}, u32[]{:S(2)}, u32[]{:S(2)}) %all-to-all-start.1) | async-done | bytes 393248 | tf_op jit(solution)/shard_map/all_to_all | solution.py:393
  45.0 1.3 %turn.1 = (bf16[128,384]{1,0:T(8,128)(2,1)S(1)}, bf16[512,384]{1,0:T(8,128)(2,1)}) custom-call(bf16[512,128]{1,0:T(8,128)(2,1)S(1)} %get-tuple-element.23.place_ref, bf16[512,384]{1,0:T(8,128)(2,1)S(1)} %bitcast.12, bf16[128,384]{1,0:T(8,128)(2,1)S(1)} %get-tuple-element.32.history_ref, f32[128,128]{1,0:T(8,128)S(1)} %get-tuple-element.33.column_ref, ...), custom_call_target="tpu_custom_call" | custom-call | tf_op jit(solution)/shard_map/turn/pallas_call | solution.py:413
  46.3 2.6 %all-to-all-start.2 = ((bf16[32,16,384]{2,1,0:T(8,128)(2,1)}), bf16[32,16,384]{2,1,0:T(8,128)(2,1)S(1)}, u32[]{:S(2)}, u32[]{:S(2)}) async-start(bf16[32,16,384]{2,1,0:T(8,128)(2,1)} %bitcast.18), calls=%async_computation.2 | async-start | bytes 786432 | tf_op jit(solution)/shard_map/all_to_all | solution.py:393
  48.9 7.8 %dam_part.3 = (f32[384,512]{1,0:T(8,128)}, bf16[192,192]{1,0:T(8,128)(2,1)S(1)}, s16[4096,128]{1,0:T(8,128)(2,1)S(1)}, bf16[4096,384]{1,0:T(8,128)(2,1)}) custom-call(s32[64,64]{1,0:T(8,128)} %free_hbm.3, s32[64,64]{1,0:T(8,128)} %dam_conn_hbm.7, bf16[512,384]{1,0:T(8,128)(2,1)} %dam_update.2.dam_hbm.after_hbm, bf16[192,192]{1,0:T(8,128)(2,1)} %stiff_hbm.3, ...), custom_call_target="tpu_custom_call" | custom-call | flops 4831838208 | bytes 6291456 | tf_op jit(solution)/shard_map/dam_part/pallas_call | solution.py:413
  56.7 5.3 %all-to-all-done.2 = bf16[32,16,384]{2,1,0:T(8,128)(2,1)S(1)} async-done(((bf16[32,16,384]{2,1,0:T(8,128)(2,1)}), bf16[32,16,384]{2,1,0:T(8,128)(2,1)S(1)}, u32[]{:S(2)}, u32[]{:S(2)}) %all-to-all-start.2) | async-done | bytes 393248 | tf_op jit(solution)/shard_map/all_to_all | solution.py:393
  62.0 6.3 %free_part.3 = (bf16[4096,384]{1,0:T(8,128)(2,1)}, bf16[512,384]{1,0:T(8,128)(2,1)}) custom-call(s16[4096,128]{1,0:T(8,128)(2,1)S(1)} %get-tuple-element.30.columns_ref, bf16[512,384]{1,0:T(8,128)(2,1)S(1)} %bitcast.14, bf16[192,192]{1,0:T(8,128)(2,1)S(1)} %get-tuple-element.35.order_ref, f32[64]{0:T(128)} %stiff_coef_hbm.7, f32[64]{0:T(128)} %mass_coef_hbm.7, ...), custom_call_target="tpu_custom_call" | custom-call | flops 4831838208 | bytes 6291456 | tf_op jit(solution)/shard_map/free_part/pallas_call | solution.py:413
  68.4 2.6 %all-to-all-start.3 = ((bf16[32,16,384]{2,1,0:T(8,128)(2,1)}), bf16[32,16,384]{2,1,0:T(8,128)(2,1)S(1)}, u32[]{:S(2)}, u32[]{:S(2)}) async-start(bf16[32,16,384]{2,1,0:T(8,128)(2,1)} %bitcast.15), calls=%async_computation.3 | async-start | bytes 786432 | tf_op jit(solution)/shard_map/all_to_all | solution.py:393
  71.0 5.8 %dam_update.3.after_hbm = bf16[512,384]{1,0:T(8,128)(2,1)} custom-call(s32[64,64]{1,0:T(8,128)} %dam_conn_hbm.7, bf16[4096,384]{1,0:T(8,128)(2,1)} %get-tuple-element.39.free_force_hbm, bf16[4096,384]{1,0:T(8,128)(2,1)} %get-tuple-element.40.dam_force_hbm, bf16[512,384]{1,0:T(8,128)(2,1)} %dam_update.2.dam_hbm.after_hbm, f32[1,512]{1,0:T(1,128)} %bitcast.20), custom_call_target="tpu_custom_call" | custom-call | flops 1610612736 | bytes 6291456 | tf_op jit(solution)/shard_map/dam_update/pallas_call | solution.py:413
  76.8 7.2 %all-to-all-done.3 = bf16[32,16,384]{2,1,0:T(8,128)(2,1)S(1)} async-done(((bf16[32,16,384]{2,1,0:T(8,128)(2,1)}), bf16[32,16,384]{2,1,0:T(8,128)(2,1)S(1)}, u32[]{:S(2)}, u32[]{:S(2)}) %all-to-all-start.3) | async-done | bytes 393248 | tf_op jit(solution)/shard_map/all_to_all | solution.py:393
  84.1 1.0 %last.1 = (bf16[128,384]{1,0:T(8,128)(2,1)}, f32[128,384]{1,0:T(8,128)}) custom-call(bf16[512,128]{1,0:T(8,128)(2,1)S(1)} %get-tuple-element.23.place_ref, bf16[512,384]{1,0:T(8,128)(2,1)S(1)} %bitcast.11, bf16[128,384]{1,0:T(8,128)(2,1)S(1)} %get-tuple-element.38.history_ref, f32[128,128]{1,0:T(8,128)S(1)} %get-tuple-element.33.column_ref, ...), custom_call_target="tpu_custom_call" | custom-call | tf_op jit(solution)/shard_map/last/pallas_call | solution.py:413
Async XLA Ops:
  2.6 20.4 %all-to-all-start = ((bf16[32,16,384]{2,1,0:T(8,128)(2,1)}), bf16[32,16,384]{2,1,0:T(8,128)(2,1)S(1)}, u32[]{:S(2)}, u32[]{:S(2)}) async-start(bf16[32,16,384]{2,1,0:T(8,128)(2,1)} %bitcast.16), calls=%async_computation | async-start | bytes 786432 | tf_op jit(solution)/shard_map/all_to_all | solution.py:393
  29.3 15.7 %all-to-all-start.1 = ((bf16[32,16,384]{2,1,0:T(8,128)(2,1)}), bf16[32,16,384]{2,1,0:T(8,128)(2,1)S(1)}, u32[]{:S(2)}, u32[]{:S(2)}) async-start(bf16[32,16,384]{2,1,0:T(8,128)(2,1)} %bitcast.17), calls=%async_computation.1 | async-start | bytes 786432 | tf_op jit(solution)/shard_map/all_to_all | solution.py:393
  46.3 15.7 %all-to-all-start.2 = ((bf16[32,16,384]{2,1,0:T(8,128)(2,1)}), bf16[32,16,384]{2,1,0:T(8,128)(2,1)S(1)}, u32[]{:S(2)}, u32[]{:S(2)}) async-start(bf16[32,16,384]{2,1,0:T(8,128)(2,1)} %bitcast.18), calls=%async_computation.2 | async-start | bytes 786432 | tf_op jit(solution)/shard_map/all_to_all | solution.py:393
  68.4 15.7 %all-to-all-start.3 = ((bf16[32,16,384]{2,1,0:T(8,128)(2,1)}), bf16[32,16,384]{2,1,0:T(8,128)(2,1)S(1)}, u32[]{:S(2)}, u32[]{:S(2)}) async-start(bf16[32,16,384]{2,1,0:T(8,128)(2,1)} %bitcast.15), calls=%async_computation.3 | async-start | bytes 786432 | tf_op jit(solution)/shard_map/all_to_all | solution.py:393

commit v7 on v6

--- a/solution.py
+++ b/solution.py
@@ -176,7 +176,7 @@
                 w = part(e, c)
                 before = jnp.where(lane == 0, nothing, pltpu.roll(w, 1, 1))
                 after = jnp.where(lane == samples - 1, nothing, pltpu.roll(w, samples - 1, 1))
-                accel = ((before + after) - (w + w)).astype(F32)
+                accel = ((after - w) + (before - w)).astype(F32)
                 row.append((k * own + m * accel).astype(BF16))
             blocks.append(jnp.concatenate(row, axis=1))
     return jnp.concatenate(blocks, axis=0)
@@ -325,14 +325,16 @@
 
     def gather(group):
         select = select_spread(chunks_of(columns_ref, groups)[group][...], received_ref.shape[0])
-        made_chunks[group][...] = select
         held[group % 2][...] = dot(select, received_ref[...]).astype(BF16)
         if group == 0:
             finish(inward[:2])
 
     def add(group):
         sender.start(group)
-        part = dot_first(sender.chunks[group][...], made_chunks[group][...])
+        part = dot_first(
+            sender.chunks[group][...],
+            select_spread(chunks_of(columns_ref, groups)[group][...], received_ref.shape[0]),
+        )
         total_ref[...] = part if group == 0 else total_ref[...] + part
 
     coefs = (stiff_coef_ref, mass_coef_ref)

time: 85.7 us -> 85.4 us (level)
  no operation moved by 1% of the time
where the time goes in v7:
time: 85.4 us; the launch traced here: 84.8 us
  Pallas kernels  43.4 us (51%)
  waiting for transfers between devices  25.1 us (29%)
  starting transfers between devices  15.3 us (18%)
  between operations  0.89 us (1%)
    pallas_call x9, Pallas kernels, run(): call(*[x if letter == 'a' else pltpu.with_memory_space_constraint(x, spac...  43.4 us
    all_to_all x4, waiting for transfers between devices, exchange(): lax.all_to_all(shaped, AXES, split_axis=0, concat_axis=0, tiled=True)  25.1 us
    all_to_all x4, starting transfers between devices, exchange(): lax.all_to_all(shaped, AXES, split_axis=0, concat_axis=0, tiled=True)  15.3 us
  transfers between devices with their start and end apart: 4, of which 4 were waited for; matrix products, arithmetic and copies ran while one was open for 0% of the time, Pallas kernels for 32%

profile of v7, /device:TPU:0, one launch (start us, length us, event | category | flops | bytes accessed | tf_op | source)
XLA Modules:
  0.0 84.8 jit_solution(12769314974497036859)
XLA Ops:
  0.6 1.9 %pack.1 = (bf16[512,384]{1,0:T(8,128)(2,1)}, bf16[512,128]{1,0:T(8,128)(2,1)S(1)}, bf16[128,384]{1,0:T(8,128)(2,1)S(1)}, f32[128,128]{1,0:T(8,128)S(1)}) custom-call(s32[2,128]{1,0:T(2,128)} %bitcast.21, bf16[128,384]{1,0:T(8,128)(2,1)} %history_hbm.1, f32[1,128]{1,0:T(1,128)} %bitcast.22), custom_call_target="tpu_custom_call" | custom-call | tf_op jit(solution)/shard_map/pack/pallas_call | solution.py:415
  2.6 7.3 %all-to-all-start = ((bf16[32,16,384]{2,1,0:T(8,128)(2,1)}), bf16[32,16,384]{2,1,0:T(8,128)(2,1)S(1)}, u32[]{:S(2)}, u32[]{:S(2)}) async-start(bf16[32,16,384]{2,1,0:T(8,128)(2,1)} %bitcast.16), calls=%async_computation | async-start | bytes 786432 | tf_op jit(solution)/shard_map/all_to_all | solution.py:395
  9.9 7.7 %dam_part.2 = (f32[384,512]{1,0:T(8,128)}, bf16[192,192]{1,0:T(8,128)(2,1)S(1)}, s16[4096,128]{1,0:T(8,128)(2,1)S(1)}, bf16[4096,384]{1,0:T(8,128)(2,1)}) custom-call(s32[64,64]{1,0:T(8,128)} %free_hbm.3, s32[64,64]{1,0:T(8,128)} %dam_conn_hbm.7, bf16[512,384]{1,0:T(8,128)(2,1)} %dam_hbm.3, bf16[192,192]{1,0:T(8,128)(2,1)} %stiff_hbm.3, f32[64]{0:T(128)} %stiff_coef_hbm.7, ...), custom_call_target="tpu_custom_call" | custom-call | flops 4831838208 | bytes 6291456 | tf_op jit(solution)/shard_map/dam_part/pallas_call | solution.py:415
  17.6 5.4 %all-to-all-done = bf16[32,16,384]{2,1,0:T(8,128)(2,1)S(1)} async-done(((bf16[32,16,384]{2,1,0:T(8,128)(2,1)}), bf16[32,16,384]{2,1,0:T(8,128)(2,1)S(1)}, u32[]{:S(2)}, u32[]{:S(2)}) %all-to-all-start) | async-done | bytes 393248 | tf_op jit(solution)/shard_map/all_to_all | solution.py:395
  23.0 6.1 %free_part.2 = (bf16[4096,384]{1,0:T(8,128)(2,1)}, bf16[512,384]{1,0:T(8,128)(2,1)}) custom-call(s16[4096,128]{1,0:T(8,128)(2,1)S(1)} %get-tuple-element.24.columns_ref, bf16[512,384]{1,0:T(8,128)(2,1)S(1)} %bitcast.13, bf16[192,192]{1,0:T(8,128)(2,1)S(1)} %get-tuple-element.26.order_ref, f32[64]{0:T(128)} %stiff_coef_hbm.7, f32[64]{0:T(128)} %mass_coef_hbm.7, ...), custom_call_target="tpu_custom_call" | custom-call | flops 4831838208 | bytes 6291456 | tf_op jit(solution)/shard_map/free_part/pallas_call | solution.py:415
  29.1 2.8 %all-to-all-start.1 = ((bf16[32,16,384]{2,1,0:T(8,128)(2,1)}), bf16[32,16,384]{2,1,0:T(8,128)(2,1)S(1)}, u32[]{:S(2)}, u32[]{:S(2)}) async-start(bf16[32,16,384]{2,1,0:T(8,128)(2,1)} %bitcast.17), calls=%async_computation.1 | async-start | bytes 786432 | tf_op jit(solution)/shard_map/all_to_all | solution.py:395
  31.9 5.8 %dam_update.2.dam_hbm.after_hbm = bf16[512,384]{1,0:T(8,128)(2,1)} custom-call(s32[64,64]{1,0:T(8,128)} %dam_conn_hbm.7, bf16[4096,384]{1,0:T(8,128)(2,1)} %get-tuple-element.28.free_force_hbm, bf16[4096,384]{1,0:T(8,128)(2,1)} %get-tuple-element.29.dam_force_hbm, bf16[512,384]{1,0:T(8,128)(2,1)} %dam_hbm.3, f32[1,512]{1,0:T(1,128)} %bitcast.19), custom_call_target="tpu_custom_call" | custom-call | flops 1610612736 | bytes 6291456 | tf_op jit(solution)/shard_map/dam_update/pallas_call | solution.py:415
  37.8 7.1 %all-to-all-done.1 = bf16[32,16,384]{2,1,0:T(8,128)(2,1)S(1)} async-done(((bf16[32,16,384]{2,1,0:T(8,128)(2,1)}), bf16[32,16,384]{2,1,0:T(8,128)(2,1)S(1)}, u32[]{:S(2)}, u32[]{:S(2)}) %all-to-all-start.1) | async-done | bytes 393248 | tf_op jit(solution)/shard_map/all_to_all | solution.py:395
  44.8 1.2 %turn.1 = (bf16[128,384]{1,0:T(8,128)(2,1)S(1)}, bf16[512,384]{1,0:T(8,128)(2,1)}) custom-call(bf16[512,128]{1,0:T(8,128)(2,1)S(1)} %get-tuple-element.23.place_ref, bf16[512,384]{1,0:T(8,128)(2,1)S(1)} %bitcast.12, bf16[128,384]{1,0:T(8,128)(2,1)S(1)} %get-tuple-element.32.history_ref, f32[128,128]{1,0:T(8,128)S(1)} %get-tuple-element.33.column_ref, ...), custom_call_target="tpu_custom_call" | custom-call | tf_op jit(solution)/shard_map/turn/pallas_call | solution.py:415
  46.1 2.6 %all-to-all-start.2 = ((bf16[32,16,384]{2,1,0:T(8,128)(2,1)}), bf16[32,16,384]{2,1,0:T(8,128)(2,1)S(1)}, u32[]{:S(2)}, u32[]{:S(2)}) async-start(bf16[32,16,384]{2,1,0:T(8,128)(2,1)} %bitcast.18), calls=%async_computation.2 | async-start | bytes 786432 | tf_op jit(solution)/shard_map/all_to_all | solution.py:395
  48.7 7.7 %dam_part.3 = (f32[384,512]{1,0:T(8,128)}, bf16[192,192]{1,0:T(8,128)(2,1)S(1)}, s16[4096,128]{1,0:T(8,128)(2,1)S(1)}, bf16[4096,384]{1,0:T(8,128)(2,1)}) custom-call(s32[64,64]{1,0:T(8,128)} %free_hbm.3, s32[64,64]{1,0:T(8,128)} %dam_conn_hbm.7, bf16[512,384]{1,0:T(8,128)(2,1)} %dam_update.2.dam_hbm.after_hbm, bf16[192,192]{1,0:T(8,128)(2,1)} %stiff_hbm.3, ...), custom_call_target="tpu_custom_call" | custom-call | flops 4831838208 | bytes 6291456 | tf_op jit(solution)/shard_map/dam_part/pallas_call | solution.py:415
  56.4 5.4 %all-to-all-done.2 = bf16[32,16,384]{2,1,0:T(8,128)(2,1)S(1)} async-done(((bf16[32,16,384]{2,1,0:T(8,128)(2,1)}), bf16[32,16,384]{2,1,0:T(8,128)(2,1)S(1)}, u32[]{:S(2)}, u32[]{:S(2)}) %all-to-all-start.2) | async-done | bytes 393248 | tf_op jit(solution)/shard_map/all_to_all | solution.py:395
  61.8 6.1 %free_part.3 = (bf16[4096,384]{1,0:T(8,128)(2,1)}, bf16[512,384]{1,0:T(8,128)(2,1)}) custom-call(s16[4096,128]{1,0:T(8,128)(2,1)S(1)} %get-tuple-element.30.columns_ref, bf16[512,384]{1,0:T(8,128)(2,1)S(1)} %bitcast.14, bf16[192,192]{1,0:T(8,128)(2,1)S(1)} %get-tuple-element.35.order_ref, f32[64]{0:T(128)} %stiff_coef_hbm.7, f32[64]{0:T(128)} %mass_coef_hbm.7, ...), custom_call_target="tpu_custom_call" | custom-call | flops 4831838208 | bytes 6291456 | tf_op jit(solution)/shard_map/free_part/pallas_call | solution.py:415
  67.9 2.6 %all-to-all-start.3 = ((bf16[32,16,384]{2,1,0:T(8,128)(2,1)}), bf16[32,16,384]{2,1,0:T(8,128)(2,1)S(1)}, u32[]{:S(2)}, u32[]{:S(2)}) async-start(bf16[32,16,384]{2,1,0:T(8,128)(2,1)} %bitcast.15), calls=%async_computation.3 | async-start | bytes 786432 | tf_op jit(solution)/shard_map/all_to_all | solution.py:395
  70.6 5.8 %dam_update.3.after_hbm = bf16[512,384]{1,0:T(8,128)(2,1)} custom-call(s32[64,64]{1,0:T(8,128)} %dam_conn_hbm.7, bf16[4096,384]{1,0:T(8,128)(2,1)} %get-tuple-element.39.free_force_hbm, bf16[4096,384]{1,0:T(8,128)(2,1)} %get-tuple-element.40.dam_force_hbm, bf16[512,384]{1,0:T(8,128)(2,1)} %dam_update.2.dam_hbm.after_hbm, f32[1,512]{1,0:T(1,128)} %bitcast.20), custom_call_target="tpu_custom_call" | custom-call | flops 1610612736 | bytes 6291456 | tf_op jit(solution)/shard_map/dam_update/pallas_call | solution.py:415
  76.4 7.2 %all-to-all-done.3 = bf16[32,16,384]{2,1,0:T(8,128)(2,1)S(1)} async-done(((bf16[32,16,384]{2,1,0:T(8,128)(2,1)}), bf16[32,16,384]{2,1,0:T(8,128)(2,1)S(1)}, u32[]{:S(2)}, u32[]{:S(2)}) %all-to-all-start.3) | async-done | bytes 393248 | tf_op jit(solution)/shard_map/all_to_all | solution.py:395
  83.7 1.0 %last.1 = (bf16[128,384]{1,0:T(8,128)(2,1)}, f32[128,384]{1,0:T(8,128)}) custom-call(bf16[512,128]{1,0:T(8,128)(2,1)S(1)} %get-tuple-element.23.place_ref, bf16[512,384]{1,0:T(8,128)(2,1)S(1)} %bitcast.11, bf16[128,384]{1,0:T(8,128)(2,1)S(1)} %get-tuple-element.38.history_ref, f32[128,128]{1,0:T(8,128)S(1)} %get-tuple-element.33.column_ref, ...), custom_call_target="tpu_custom_call" | custom-call | tf_op jit(solution)/shard_map/last/pallas_call | solution.py:415
Async XLA Ops:
  2.6 20.4 %all-to-all-start = ((bf16[32,16,384]{2,1,0:T(8,128)(2,1)}), bf16[32,16,384]{2,1,0:T(8,128)(2,1)S(1)}, u32[]{:S(2)}, u32[]{:S(2)}) async-start(bf16[32,16,384]{2,1,0:T(8,128)(2,1)} %bitcast.16), calls=%async_computation | async-start | bytes 786432 | tf_op jit(solution)/shard_map/all_to_all | solution.py:395
  29.1 15.7 %all-to-all-start.1 = ((bf16[32,16,384]{2,1,0:T(8,128)(2,1)}), bf16[32,16,384]{2,1,0:T(8,128)(2,1)S(1)}, u32[]{:S(2)}, u32[]{:S(2)}) async-start(bf16[32,16,384]{2,1,0:T(8,128)(2,1)} %bitcast.17), calls=%async_computation.1 | async-start | bytes 786432 | tf_op jit(solution)/shard_map/all_to_all | solution.py:395
  46.1 15.7 %all-to-all-start.2 = ((bf16[32,16,384]{2,1,0:T(8,128)(2,1)}), bf16[32,16,384]{2,1,0:T(8,128)(2,1)S(1)}, u32[]{:S(2)}, u32[]{:S(2)}) async-start(bf16[32,16,384]{2,1,0:T(8,128)(2,1)} %bitcast.18), calls=%async_computation.2 | async-start | bytes 786432 | tf_op jit(solution)/shard_map/all_to_all | solution.py:395
  67.9 15.7 %all-to-all-start.3 = ((bf16[32,16,384]{2,1,0:T(8,128)(2,1)}), bf16[32,16,384]{2,1,0:T(8,128)(2,1)S(1)}, u32[]{:S(2)}, u32[]{:S(2)}) async-start(bf16[32,16,384]{2,1,0:T(8,128)(2,1)} %bitcast.15), calls=%async_computation.3 | async-start | bytes 786432 | tf_op jit(solution)/shard_map/all_to_all | solution.py:395

commit v8 on v7

--- a/solution.py
+++ b/solution.py
@@ -46,6 +46,18 @@
     down = lax.broadcasted_iota(jnp.int32, (size, size), 0)
     across = lax.broadcasted_iota(jnp.int32, (size, size), 1)
     return jnp.sum(jnp.where(down == across, row, jnp.zeros_like(row)), axis=1, keepdims=True)
+
+
+def send_product(place_ref, rows, out_ref, out_hbm, sems):
+    parts = sems.shape[0]
+    size = out_ref.shape[0] // parts
+    copies = []
+    for i in range(parts):
+        part = slice(i * size, (i + 1) * size)
+        out_ref[part, :] = dot(place_ref[part, :], rows).astype(BF16)
+        copies.append(pltpu.make_async_copy(out_ref.at[part, :], out_hbm.at[part, :], sems.at[i]))
+        copies[-1].start()
+    return copies
 
 
 def block_of(device, dam):
@@ -69,27 +81,31 @@
     step_ref,
     out_ref,
     sems,
+    out_sems,
 ):
     inward = transfer(
         [(routes_hbm, routes_ref), (history_hbm, history_ref), (step_hbm, step_ref)], sems
     )
     slots, rows = place_ref.shape
-    finish(inward[:1])
-    row0, row1 = routes_ref[0:1, :], routes_ref[1:2, :]
-    col0, col1 = as_column(row0), as_column(row1)
     down = lax.broadcasted_iota(jnp.int32, (rows, rows), 0)
     across = lax.broadcasted_iota(jnp.int32, (rows, rows), 1)
+    earlier = mask_to_bf16(down < across)
+    devices = lax.broadcasted_iota(jnp.int32, (slots // capacity, rows), 0)
     numbers = lax.broadcasted_iota(jnp.int32, (slots, rows), 0)
+    finish(inward[:1])
+    own = [routes_ref[0:1, :], routes_ref[1:2, :]]
+    named = [row == devices for row in own]
+    before = dot(mask_to_bf16(named[0] | named[1]), earlier)
     hits = []
-    for own in (row0, row1):
-        same = jnp.where(col0 == own, 1, 0) + jnp.where(col1 == own, 1, 0)
-        slot = jnp.sum(jnp.where(down < across, same, 0), axis=0, keepdims=True)
-        hits.append(block_of(own, dam) * capacity + slot == numbers)
+    for row, mask in zip(own, named):
+        slot = jnp.sum(jnp.where(mask, before, 0.0), axis=0, keepdims=True).astype(jnp.int32)
+        hits.append(block_of(row, dam) * capacity + slot == numbers)
     place = mask_to_bf16(hits[0] | hits[1])
     place_ref[...] = place
-    finish(inward[1:])
-    out_ref[...] = dot(place, history_ref[...]).astype(BF16)
-    outward = transfer([(out_ref, out_hbm)], sems)
+    finish(inward[1:2])
+    history = history_ref[...]
+    outward = send_product(place_ref, history, out_ref, out_hbm, out_sems)
+    finish(inward[2:])
     column_ref[...] = jnp.broadcast_to(as_column(step_ref[...]), column_ref.shape)
     finish(outward)
 
@@ -97,12 +113,10 @@
 def turn_kernel(
     place_ref, returned_ref, history_ref, column_ref, after_hbm, next_ref, out_hbm, out_ref, sems
 ):
-    place = place_ref[...]
-    pulled = dot_first(place, returned_ref[...])
+    pulled = dot_first(place_ref[...], returned_ref[...])
     following = (history_ref[...].astype(F32) - column_ref[:, 0:1] * pulled).astype(BF16)
     next_ref[...] = following
-    out_ref[...] = dot(place, following).astype(BF16)
-    finish(transfer([(out_ref, out_hbm)], sems))
+    finish(send_product(place_ref, following, out_ref, out_hbm, sems))
 
 
 def last_kernel(
@@ -302,7 +316,6 @@
     mass_coef_ref,
     start_ref,
     total_ref,
-    made,
     force_ref,
     back_ref,
     held0,
@@ -319,7 +332,6 @@
         sems,
     )
     groups = force_sems.shape[0]
-    made_chunks = chunks_of(made, groups)
     held = (held0, held1)
     sender = Sender(force_ref, force_hbm, force_sems)
 
@@ -452,7 +464,6 @@
     coefs = [pltpu.SMEM((elements,), F32)] * 2
     held = [vmem((pairs, width), BF16)] * 2
     forces_type = ((all_pairs, width), BF16)
-    free_type = ((all_pairs, slots), BF16)
     back_type = ((width, slots), F32)
     stiff_type = (stiff_ref.shape, BF16)
     place_type = ((slots, row_count), BF16)
@@ -468,14 +479,14 @@
         "pack",
         "hhh",
         [("h", *slots_type), ("v", *place_type), ("v", *rows_type), ("v", *column_type)],
-        [vmem((2, row_count), I32), vmem((1, row_count), F32), vmem(*slots_type), dma((3,))],
+        [vmem((2, row_count), I32), vmem((1, row_count), F32), vmem(*slots_type), dma((3,)), dma((2,))],
     )
     turn = kernel(
         turn_kernel,
         "turn",
         "vavvh",
         [("v", *rows_type), ("h", *slots_type)],
-        [vmem(*slots_type), dma((1,))],
+        [vmem(*slots_type), dma((2,))],
     )
     last = kernel(
         last_kernel,
@@ -500,7 +511,7 @@
         "vavhhh",
         [("h", *forces_type), ("h", *slots_type)],
         [*coefs, vmem(*back_type), vmem(*back_type)]
-        + [vmem(*free_type), vmem(*forces_type), vmem(*slots_type), *held]
+        + [vmem(*forces_type), vmem(*slots_type), *held]
         + [dma((4,)), dma((groups,))],
         flops=3 * product,
         moved=4 * all_pairs * width,

time: 85.4 us -> 85.3 us (level)
  no operation moved by 1% of the time
where the time goes in v8:
time: 85.3 us; the launch traced here: 84.7 us
  Pallas kernels  43.4 us (51%)
  waiting for transfers between devices  25.1 us (29%)
  starting transfers between devices  15.3 us (18%)
  between operations  0.89 us (1%)
    pallas_call x9, Pallas kernels, run(): call(*[x if letter == 'a' else pltpu.with_memory_space_constraint(x, spac...  43.4 us
    all_to_all x4, waiting for transfers between devices, exchange(): lax.all_to_all(shaped, AXES, split_axis=0, concat_axis=0, tiled=True)  25.1 us
    all_to_all x4, starting transfers between devices, exchange(): lax.all_to_all(shaped, AXES, split_axis=0, concat_axis=0, tiled=True)  15.3 us
  transfers between devices with their start and end apart: 4, of which 4 were waited for; matrix products, arithmetic and copies ran while one was open for 0% of the time, Pallas kernels for 32%

profile of v8, /device:TPU:0, one launch (start us, length us, event | category | flops | bytes accessed | tf_op | source)
XLA Modules:
  0.0 84.7 jit_solution(9530267320359433579)
XLA Ops:
  0.6 1.9 %pack.1 = (bf16[512,384]{1,0:T(8,128)(2,1)}, bf16[512,128]{1,0:T(8,128)(2,1)S(1)}, bf16[128,384]{1,0:T(8,128)(2,1)S(1)}, f32[128,128]{1,0:T(8,128)S(1)}) custom-call(s32[2,128]{1,0:T(2,128)} %bitcast.21, bf16[128,384]{1,0:T(8,128)(2,1)} %history_hbm.1, f32[1,128]{1,0:T(1,128)} %bitcast.22), custom_call_target="tpu_custom_call" | custom-call | tf_op jit(solution)/shard_map/pack/pallas_call | solution.py:427
  2.5 7.3 %all-to-all-start = ((bf16[32,16,384]{2,1,0:T(8,128)(2,1)}), bf16[32,16,384]{2,1,0:T(8,128)(2,1)S(1)}, u32[]{:S(2)}, u32[]{:S(2)}) async-start(bf16[32,16,384]{2,1,0:T(8,128)(2,1)} %bitcast.16), calls=%async_computation | async-start | bytes 786432 | tf_op jit(solution)/shard_map/all_to_all | solution.py:407
  9.9 7.7 %dam_part.2 = (f32[384,512]{1,0:T(8,128)}, bf16[192,192]{1,0:T(8,128)(2,1)S(1)}, s16[4096,128]{1,0:T(8,128)(2,1)S(1)}, bf16[4096,384]{1,0:T(8,128)(2,1)}) custom-call(s32[64,64]{1,0:T(8,128)} %free_hbm.3, s32[64,64]{1,0:T(8,128)} %dam_conn_hbm.7, bf16[512,384]{1,0:T(8,128)(2,1)} %dam_hbm.3, bf16[192,192]{1,0:T(8,128)(2,1)} %stiff_hbm.3, f32[64]{0:T(128)} %stiff_coef_hbm.7, ...), custom_call_target="tpu_custom_call" | custom-call | flops 4831838208 | bytes 6291456 | tf_op jit(solution)/shard_map/dam_part/pallas_call | solution.py:427
  17.5 5.4 %all-to-all-done = bf16[32,16,384]{2,1,0:T(8,128)(2,1)S(1)} async-done(((bf16[32,16,384]{2,1,0:T(8,128)(2,1)}), bf16[32,16,384]{2,1,0:T(8,128)(2,1)S(1)}, u32[]{:S(2)}, u32[]{:S(2)}) %all-to-all-start) | async-done | bytes 393248 | tf_op jit(solution)/shard_map/all_to_all | solution.py:407
  23.0 6.1 %free_part.2 = (bf16[4096,384]{1,0:T(8,128)(2,1)}, bf16[512,384]{1,0:T(8,128)(2,1)}) custom-call(s16[4096,128]{1,0:T(8,128)(2,1)S(1)} %get-tuple-element.24.columns_ref, bf16[512,384]{1,0:T(8,128)(2,1)S(1)} %bitcast.13, bf16[192,192]{1,0:T(8,128)(2,1)S(1)} %get-tuple-element.26.order_ref, f32[64]{0:T(128)} %stiff_coef_hbm.7, f32[64]{0:T(128)} %mass_coef_hbm.7, ...), custom_call_target="tpu_custom_call" | custom-call | flops 4831838208 | bytes 6291456 | tf_op jit(solution)/shard_map/free_part/pallas_call | solution.py:427
  29.1 2.8 %all-to-all-start.1 = ((bf16[32,16,384]{2,1,0:T(8,128)(2,1)}), bf16[32,16,384]{2,1,0:T(8,128)(2,1)S(1)}, u32[]{:S(2)}, u32[]{:S(2)}) async-start(bf16[32,16,384]{2,1,0:T(8,128)(2,1)} %bitcast.17), calls=%async_computation.1 | async-start | bytes 786432 | tf_op jit(solution)/shard_map/all_to_all | solution.py:407
  31.9 5.8 %dam_update.2.dam_hbm.after_hbm = bf16[512,384]{1,0:T(8,128)(2,1)} custom-call(s32[64,64]{1,0:T(8,128)} %dam_conn_hbm.7, bf16[4096,384]{1,0:T(8,128)(2,1)} %get-tuple-element.28.free_force_hbm, bf16[4096,384]{1,0:T(8,128)(2,1)} %get-tuple-element.29.dam_force_hbm, bf16[512,384]{1,0:T(8,128)(2,1)} %dam_hbm.3, f32[1,512]{1,0:T(1,128)} %bitcast.19), custom_call_target="tpu_custom_call" | custom-call | flops 1610612736 | bytes 6291456 | tf_op jit(solution)/shard_map/dam_update/pallas_call | solution.py:427
  37.7 7.1 %all-to-all-done.1 = bf16[32,16,384]{2,1,0:T(8,128)(2,1)S(1)} async-done(((bf16[32,16,384]{2,1,0:T(8,128)(2,1)}), bf16[32,16,384]{2,1,0:T(8,128)(2,1)S(1)}, u32[]{:S(2)}, u32[]{:S(2)}) %all-to-all-start.1) | async-done | bytes 393248 | tf_op jit(solution)/shard_map/all_to_all | solution.py:407
  44.8 1.2 %turn.1 = (bf16[128,384]{1,0:T(8,128)(2,1)S(1)}, bf16[512,384]{1,0:T(8,128)(2,1)}) custom-call(bf16[512,128]{1,0:T(8,128)(2,1)S(1)} %get-tuple-element.23.place_ref, bf16[512,384]{1,0:T(8,128)(2,1)S(1)} %bitcast.12, bf16[128,384]{1,0:T(8,128)(2,1)S(1)} %get-tuple-element.32.history_ref, f32[128,128]{1,0:T(8,128)S(1)} %get-tuple-element.33.column_ref, ...), custom_call_target="tpu_custom_call" | custom-call | tf_op jit(solution)/shard_map/turn/pallas_call | solution.py:427
  46.0 2.6 %all-to-all-start.2 = ((bf16[32,16,384]{2,1,0:T(8,128)(2,1)}), bf16[32,16,384]{2,1,0:T(8,128)(2,1)S(1)}, u32[]{:S(2)}, u32[]{:S(2)}) async-start(bf16[32,16,384]{2,1,0:T(8,128)(2,1)} %bitcast.18), calls=%async_computation.2 | async-start | bytes 786432 | tf_op jit(solution)/shard_map/all_to_all | solution.py:407
  48.6 7.7 %dam_part.3 = (f32[384,512]{1,0:T(8,128)}, bf16[192,192]{1,0:T(8,128)(2,1)S(1)}, s16[4096,128]{1,0:T(8,128)(2,1)S(1)}, bf16[4096,384]{1,0:T(8,128)(2,1)}) custom-call(s32[64,64]{1,0:T(8,128)} %free_hbm.3, s32[64,64]{1,0:T(8,128)} %dam_conn_hbm.7, bf16[512,384]{1,0:T(8,128)(2,1)} %dam_update.2.dam_hbm.after_hbm, bf16[192,192]{1,0:T(8,128)(2,1)} %stiff_hbm.3, ...), custom_call_target="tpu_custom_call" | custom-call | flops 4831838208 | bytes 6291456 | tf_op jit(solution)/shard_map/dam_part/pallas_call | solution.py:427
  56.3 5.4 %all-to-all-done.2 = bf16[32,16,384]{2,1,0:T(8,128)(2,1)S(1)} async-done(((bf16[32,16,384]{2,1,0:T(8,128)(2,1)}), bf16[32,16,384]{2,1,0:T(8,128)(2,1)S(1)}, u32[]{:S(2)}, u32[]{:S(2)}) %all-to-all-start.2) | async-done | bytes 393248 | tf_op jit(solution)/shard_map/all_to_all | solution.py:407
  61.7 6.1 %free_part.3 = (bf16[4096,384]{1,0:T(8,128)(2,1)}, bf16[512,384]{1,0:T(8,128)(2,1)}) custom-call(s16[4096,128]{1,0:T(8,128)(2,1)S(1)} %get-tuple-element.30.columns_ref, bf16[512,384]{1,0:T(8,128)(2,1)S(1)} %bitcast.14, bf16[192,192]{1,0:T(8,128)(2,1)S(1)} %get-tuple-element.35.order_ref, f32[64]{0:T(128)} %stiff_coef_hbm.7, f32[64]{0:T(128)} %mass_coef_hbm.7, ...), custom_call_target="tpu_custom_call" | custom-call | flops 4831838208 | bytes 6291456 | tf_op jit(solution)/shard_map/free_part/pallas_call | solution.py:427
  67.9 2.6 %all-to-all-start.3 = ((bf16[32,16,384]{2,1,0:T(8,128)(2,1)}), bf16[32,16,384]{2,1,0:T(8,128)(2,1)S(1)}, u32[]{:S(2)}, u32[]{:S(2)}) async-start(bf16[32,16,384]{2,1,0:T(8,128)(2,1)} %bitcast.15), calls=%async_computation.3 | async-start | bytes 786432 | tf_op jit(solution)/shard_map/all_to_all | solution.py:407
  70.5 5.8 %dam_update.3.after_hbm = bf16[512,384]{1,0:T(8,128)(2,1)} custom-call(s32[64,64]{1,0:T(8,128)} %dam_conn_hbm.7, bf16[4096,384]{1,0:T(8,128)(2,1)} %get-tuple-element.39.free_force_hbm, bf16[4096,384]{1,0:T(8,128)(2,1)} %get-tuple-element.40.dam_force_hbm, bf16[512,384]{1,0:T(8,128)(2,1)} %dam_update.2.dam_hbm.after_hbm, f32[1,512]{1,0:T(1,128)} %bitcast.20), custom_call_target="tpu_custom_call" | custom-call | flops 1610612736 | bytes 6291456 | tf_op jit(solution)/shard_map/dam_update/pallas_call | solution.py:427
  76.3 7.2 %all-to-all-done.3 = bf16[32,16,384]{2,1,0:T(8,128)(2,1)S(1)} async-done(((bf16[32,16,384]{2,1,0:T(8,128)(2,1)}), bf16[32,16,384]{2,1,0:T(8,128)(2,1)S(1)}, u32[]{:S(2)}, u32[]{:S(2)}) %all-to-all-start.3) | async-done | bytes 393248 | tf_op jit(solution)/shard_map/all_to_all | solution.py:407
  83.6 1.0 %last.1 = (bf16[128,384]{1,0:T(8,128)(2,1)}, f32[128,384]{1,0:T(8,128)}) custom-call(bf16[512,128]{1,0:T(8,128)(2,1)S(1)} %get-tuple-element.23.place_ref, bf16[512,384]{1,0:T(8,128)(2,1)S(1)} %bitcast.11, bf16[128,384]{1,0:T(8,128)(2,1)S(1)} %get-tuple-element.38.history_ref, f32[128,128]{1,0:T(8,128)S(1)} %get-tuple-element.33.column_ref, ...), custom_call_target="tpu_custom_call" | custom-call | tf_op jit(solution)/shard_map/last/pallas_call | solution.py:427
Async XLA Ops:
  2.5 20.4 %all-to-all-start = ((bf16[32,16,384]{2,1,0:T(8,128)(2,1)}), bf16[32,16,384]{2,1,0:T(8,128)(2,1)S(1)}, u32[]{:S(2)}, u32[]{:S(2)}) async-start(bf16[32,16,384]{2,1,0:T(8,128)(2,1)} %bitcast.16), calls=%async_computation | async-start | bytes 786432 | tf_op jit(solution)/shard_map/all_to_all | solution.py:407
  29.1 15.7 %all-to-all-start.1 = ((bf16[32,16,384]{2,1,0:T(8,128)(2,1)}), bf16[32,16,384]{2,1,0:T(8,128)(2,1)S(1)}, u32[]{:S(2)}, u32[]{:S(2)}) async-start(bf16[32,16,384]{2,1,0:T(8,128)(2,1)} %bitcast.17), calls=%async_computation.1 | async-start | bytes 786432 | tf_op jit(solution)/shard_map/all_to_all | solution.py:407
  46.0 15.7 %all-to-all-start.2 = ((bf16[32,16,384]{2,1,0:T(8,128)(2,1)}), bf16[32,16,384]{2,1,0:T(8,128)(2,1)S(1)}, u32[]{:S(2)}, u32[]{:S(2)}) async-start(bf16[32,16,384]{2,1,0:T(8,128)(2,1)} %bitcast.18), calls=%async_computation.2 | async-start | bytes 786432 | tf_op jit(solution)/shard_map/all_to_all | solution.py:407
  67.9 15.7 %all-to-all-start.3 = ((bf16[32,16,384]{2,1,0:T(8,128)(2,1)}), bf16[32,16,384]{2,1,0:T(8,128)(2,1)S(1)}, u32[]{:S(2)}, u32[]{:S(2)}) async-start(bf16[32,16,384]{2,1,0:T(8,128)(2,1)} %bitcast.15), calls=%async_computation.3 | async-start | bytes 786432 | tf_op jit(solution)/shard_map/all_to_all | solution.py:407
